TPU v7x, 32 devices: a whole 2x2x4 slice. The times are simulated.
32 devices in a mesh: dp: 4 (over y, core), fsdp: 8 (over z, x).
Axes of the slice: x: 2, y: 2, z: 4, core: 2. Of those that a mesh axis runs over, the one named last changes fastest.
Arguments:
- tokens: bfloat16 [32, 1024, 768], P(('dp', 'fsdp')), may hold values from -6 to 6
- lengths: int32 [32], P(('dp', 'fsdp')), may hold values from 32 to 1024, as said below
- cotangent: bfloat16 [32, 1024, 768], P(('dp', 'fsdp')), may hold values from -6 to 6
- w_qkv: float32 [768, 2304], P(('dp', 'fsdp')), may hold values from -0.21875 to 0.21875
- m_qkv: float32 [768, 2304], P(('dp', 'fsdp')), may hold values from -0.00061035156 to 0.00061035156
- v_qkv: float32 [768, 2304], P(('dp', 'fsdp')), may hold values from 3.7117702e-09 to 5.927542e-08
- w_out: float32 [768, 768], P(('dp', 'fsdp')), may hold values from -1.25 to 1.25
- m_out: float32 [768, 768], P(('dp', 'fsdp')), may hold values from -0.00024414062 to 0.00024414062
- v_out: float32 [768, 768], P(('dp', 'fsdp')), may hold values from 5.6452776e-10 to 8.891313e-09
- w_up: float32 [768, 3072], P(('dp', 'fsdp')), may hold values from -0.21875 to 0.21875
- m_up: float32 [768, 3072], P(('dp', 'fsdp')), may hold values from -0.00061035156 to 0.00061035156
- v_up: float32 [768, 3072], P(('dp', 'fsdp')), may hold values from 3.7117702e-09 to 5.927542e-08
- w_down: float32 [3072, 768], P(('dp', 'fsdp')), may hold values from -0.109375 to 0.109375
- m_down: float32 [3072, 768], P(('dp', 'fsdp')), may hold values from -0.00061035156 to 0.00061035156
- v_down: float32 [3072, 768], P(('dp', 'fsdp')), may hold values from 3.7117702e-09 to 5.927542e-08
- packed: float32 [7680], P(('dp', 'fsdp')), may hold values from -0.8 to 3.2, as said below
- m_packed: float32 [7680], P(('dp', 'fsdp')), may hold values from -0.0024414062 to 0.0024414062
- v_packed: float32 [7680], P(('dp', 'fsdp')), may hold values from 5.927542e-08 to 9.45584e-07
Outputs:
- mixed: bfloat16 [32, 1024, 768], P(('dp', 'fsdp'))
- d_tokens: float32 [32, 1024, 768], P(('dp', 'fsdp'))
- grad_norm: float32 [], replicated
- new_w_qkv: float32 [768, 2304], P(('dp', 'fsdp'))
- new_m_qkv: float32 [768, 2304], P(('dp', 'fsdp'))
- new_v_qkv: float32 [768, 2304], P(('dp', 'fsdp'))
- new_w_out: float32 [768, 768], P(('dp', 'fsdp'))
- new_m_out: float32 [768, 768], P(('dp', 'fsdp'))
- new_v_out: float32 [768, 768], P(('dp', 'fsdp'))
- new_w_up: float32 [768, 3072], P(('dp', 'fsdp'))
- new_m_up: float32 [768, 3072], P(('dp', 'fsdp'))
- new_v_up: float32 [768, 3072], P(('dp', 'fsdp'))
- new_w_down: float32 [3072, 768], P(('dp', 'fsdp'))
- new_m_down: float32 [3072, 768], P(('dp', 'fsdp'))
- new_v_down: float32 [3072, 768], P(('dp', 'fsdp'))
- new_packed: float32 [7680], P(('dp', 'fsdp'))
- new_m_packed: float32 [7680], P(('dp', 'fsdp'))
- new_v_packed: float32 [7680], P(('dp', 'fsdp'))
Inputs may be any that keep to these rules, and one draw needn't show every extreme that they name: `lengths`: each padded sequence has at least 32 live tokens; in every draw one sequence has all 1024. `packed`: gains are positive, biases of both signs.
All inputs are finite; a program needn't handle non-finite values.
Results may differ from a plain program's by a relative error of at most 0.01.
The roundings to bfloat16 on the way count: a program that leaves them out, or rounds other values in their place, can miss the bound.
Values may be sent and summed in bfloat16 or wider, within the bound.
A program may use at most 192 MiB of HBM per device.

v0:
```python
import functools

import jax
import jax.numpy as jnp
from jax import lax
from jax.experimental import pallas as pl
from jax.experimental.pallas import tpu as pltpu
from jax.sharding import PartitionSpec as P

D = 768
FF = 3072
HEAD_DIM = 64
STEP = 10
HD = 64
F32 = jnp.float32
BF = jnp.bfloat16
MESH = pl.DeviceIdType.MESH

EPS_NORM = 1e-05
CLIP_NORM = 1.0
BETA_ONE = 0.9
BETA_TWO = 0.95
ADAM_EPSILON = 1e-08
DECAY_RATE = 0.1
VECTOR_RATE = 0.2


def nt(a,b): return lax.dot_general(a,b,(((1,),(1,)),((),())),preferred_element_type=F32)
def nn(a,b): return jnp.dot(a,b,preferred_element_type=F32)
def head_mask(rows):
    lane=lax.broadcasted_iota(jnp.int32,(rows,128),1)
    return (lane<HD)
def half(x,h,scale=1.0):
    m=head_mask(x.shape[0]); m = m if h==0 else jnp.logical_not(m)
    return jnp.where(m,x*jnp.asarray(scale,x.dtype),jnp.zeros_like(x))

def attn_fwd_pair(q_ref,k_ref,v_ref,length,o_ref,oT_ref,lse_ref,QB,tick=None):
    L=q_ref.shape[0]
    vT=v_ref[...].T
    for i in range(L//QB):
        nk=(i+1)*QB
        qs=q_ref[pl.ds(i*QB,QB),:]
        outs=[]
        jidx=lax.broadcasted_iota(jnp.int32,(nk,QB),0)
        lim=jnp.minimum(i*QB+1+lax.broadcasted_iota(jnp.int32,(1,QB),1),length)
        for h in range(2):
            s=nt(k_ref[pl.ds(0,nk),:],half(qs,h,0.125))
            s=jnp.where(jidx<lim,s,-1e9)
            m=jnp.max(s,0,keepdims=True)
            e=jnp.exp(s-m)
            l=jnp.sum(e,0,keepdims=True)
            oT=nn(vT[HD*h:HD*h+HD,:nk],e.astype(BF))
            outs.append(oT/l)
            lse_ref[pl.ds(h,1),pl.ds(i*QB,QB)]=m+jnp.log(l)
            if tick is not None: tick(2*i+h)
        oT=jnp.concatenate(outs,0)
        oT_ref[:,pl.ds(i*QB,QB)]=oT
        o_ref[pl.ds(i*QB,QB),:]=oT.T.astype(BF)

def attn_bwd_pair(q_ref,k_ref,v_ref,do_ref,oT_ref,lse_ref,length,dq_ref,dk_ref,dv_ref,dk_acc,dv_acc,QB,tick=None):
    L=q_ref.shape[0]
    kT=k_ref[...].T
    for i in reversed(range(L//QB)):
        nk=(i+1)*QB
        sl=pl.ds(i*QB,QB)
        qs=q_ref[sl,:]; do=do_ref[sl,:]
        doT=do.astype(F32).T
        prod=doT*oT_ref[:,sl]
        live=(i*QB+lax.broadcasted_iota(jnp.int32,(1,QB),1))<length
        tri=lax.broadcasted_iota(jnp.int32,(QB,QB),0)<=lax.broadcasted_iota(jnp.int32,(QB,QB),1)
        dqs=[]
        k=k_ref[pl.ds(0,nk),:]; v=v_ref[pl.ds(0,nk),:]
        dk=None; dv=None
        for h in range(2):
            delta=jnp.sum(prod[HD*h:HD*h+HD],0,keepdims=True)
            lse=jnp.where(live,lse_ref[pl.ds(h,1),sl],1e30)
            qm=half(qs,h,0.125); dom=half(do,h)
            s=nt(k,qm)
            p=jnp.exp(s-lse)
            pd=jnp.where(tri,p[nk-QB:],0.0)
            p=pd if i==0 else jnp.concatenate([p[:nk-QB],pd],0)
            dp=nt(v,dom)
            ds=(p*(dp-delta)).astype(BF)
            a=nn(p.astype(BF),dom); b=nn(ds,qm)
            dv=a if dv is None else dv+a
            dk=b if dk is None else dk+b
            dqs.append(nn(kT[HD*h:HD*h+HD,:nk],ds))
        dq_ref[sl,:]=(jnp.concatenate(dqs,0)*0.125).T.astype(BF)
        if i==L//QB-1:
            dk_acc[...]=dk; dv_acc[...]=dv
        else:
            dk_acc[pl.ds(0,nk),:]+=dk; dv_acc[pl.ds(0,nk),:]+=dv
        if tick is not None: tick(L//QB-1-i)
    dk_ref[...]=dk_acc[...].astype(BF); dv_ref[...]=dv_acc[...].astype(BF)

def fwd_call(qkv,length,QB=256):
    L=qkv.shape[0]; D=qkv.shape[1]//3; NP=D//128
    def k(len_ref,q,k_,v,o,oT,lse):
        attn_fwd_pair(q,k_,v,len_ref[0],o,oT,lse.at[0],QB)
    return pl.pallas_call(k,grid=(NP,),
      in_specs=[pl.BlockSpec(memory_space=pltpu.SMEM)]+[pl.BlockSpec((L,128),functools.partial(lambda off,p:(0,off+p),j*NP)) for j in range(3)],
      out_specs=[pl.BlockSpec((L,128),lambda p:(0,p)),pl.BlockSpec((128,L),lambda p:(p,0)),pl.BlockSpec((1,2,L),lambda p:(p,0,0))],
      out_shape=[jax.ShapeDtypeStruct((L,D),BF),jax.ShapeDtypeStruct((D,L),F32),jax.ShapeDtypeStruct((NP,2,L),F32)],
      compiler_params=pltpu.CompilerParams(vmem_limit_bytes=56*2**20),
      cost_estimate=pl.CostEstimate(flops=4*L*L*D//2,bytes_accessed=10*2**20,transcendentals=12*L*L//2))(length,qkv,qkv,qkv)
def bwd_call(qkv,do,oT,lse,length,QB=256):
    L=qkv.shape[0]; D=qkv.shape[1]//3; NP=D//128
    def k(len_ref,q,k_,v,do,oT,lse,dq,dk,dv,dka,dva):
        attn_bwd_pair(q,k_,v,do,oT,lse.at[0],len_ref[0],dq,dk,dv,dka,dva,QB)
    blk=pl.BlockSpec((L,128),lambda p:(0,p))
    return pl.pallas_call(k,grid=(NP,),
      in_specs=[pl.BlockSpec(memory_space=pltpu.SMEM)]+[pl.BlockSpec((L,128),functools.partial(lambda off,p:(0,off+p),j*NP)) for j in range(3)]+[blk,pl.BlockSpec((128,L),lambda p:(p,0)),pl.BlockSpec((1,2,L),lambda p:(p,0,0))],
      out_specs=[blk]*3,
      out_shape=[jax.ShapeDtypeStruct((L,D),BF)]*3,
      scratch_shapes=[pltpu.VMEM((L,128),F32)]*2,
      compiler_params=pltpu.CompilerParams(vmem_limit_bytes=56*2**20),
      cost_estimate=pl.CostEstimate(flops=10*L*L*D//2,bytes_accessed=14*2**20,transcendentals=12*L*L//2))(length,qkv,qkv,qkv,do,oT,lse)


class Place:
    def __init__(self, Z):
        dp=lax.axis_index("dp"); fs=lax.axis_index("fsdp")
        self.Z=Z; self.y=dp//2; self.c=dp%2; self.z=fs//2; self.x=fs%2
        self.nx=(dp,self.z*2+1-self.x)
        self.ny=((1-self.y)*2+self.c,fs)
        self.nc=(self.y*2+1-self.c,fs)
        self.me=self.piece(self.z)
        self.dp=dp; self.fs=fs
    def nz(self,z): return (self.dp,z*2+self.x)
    def piece(self,z,dx=0,dy=0,dc=0):
        y=self.y if dy==0 else 1-self.y
        x=self.x if dx==0 else 1-self.x
        c=self.c if dc==0 else 1-self.c
        return (y*2+c,z,x)
    def slab(self,y,dc=0):
        c=self.c if dc==0 else 1-self.c
        return y*2+c

def rcopy(src,dst,ss,rs,dev):
    return pltpu.make_async_remote_copy(src_ref=src,dst_ref=dst,send_sem=ss,recv_sem=rs,device_id=dev,device_id_type=MESH)

def when(cond,fn):
    if cond is True: fn()
    else: pl.when(cond)(fn)

def gather_sems(NG,Z):
    D=pltpu.SemaphoreType.DMA
    return [D((NG*2*(Z-1),)),D((NG*2*(Z-1),)),
            D((NG*2*Z,)),D((NG*2*Z,)),
            D((NG*2*Z,)),D((NG*2*Z,)),
            D((NG*2,)),D((NG*2,))]

class Gather:
    def __init__(self,P,G,groups,sems):
        self.P=P; self.G=G; self.groups=groups; self.zs,self.zr,self.xs,self.xr,self.ys,self.yr,self.cs,self.cr=sems
    def _cp(self,idx,lo,n,ss,rs,dev):
        r=self.G.at[(*idx,slice(None),pl.ds(lo,n))]
        return rcopy(r,r,ss,rs,dev)
    def zcp(self,g,d,t,zo,to):
        lo,n,_=self.groups[g]; i=(g*2+d)*(self.P.Z-1)+t
        return self._cp(self.P.piece(zo),lo,n,self.zs.at[i],self.zr.at[i],self.P.nz(to))
    def xfull(self,g,zo,arrive=0):
        lo,n,_=self.groups[g]; i=g*2*self.P.Z+zo
        return self._cp(self.P.piece(zo,dx=arrive),lo,n,self.xs.at[i],self.xr.at[i],self.P.nx)
    def yfull(self,g,zo,arrive=0):
        lo,n,_=self.groups[g]; i=g*2*self.P.Z+zo
        return self._cp(self.P.piece(zo,dy=arrive),lo,n,self.ys.at[i],self.yr.at[i],self.P.ny)
    def ydiag(self,g,zo,arrive=0):
        lo,n,a=self.groups[g]; i=g*2*self.P.Z+self.P.Z+zo
        return self._cp(self.P.piece(zo,dx=1,dy=arrive),lo,a,self.ys.at[i],self.yr.at[i],self.P.ny)
    def xdiag(self,g,zo,arrive=0):
        lo,n,a=self.groups[g]; i=g*2*self.P.Z+self.P.Z+zo
        return self._cp(self.P.piece(zo,dy=1,dx=arrive),lo+a,n-a,self.xs.at[i],self.xr.at[i],self.P.nx)
    def ccp(self,g,k,arrive=0):
        lo,n,_=self.groups[g]
        y=self.P.y if k==0 else 1-self.P.y
        r=self.G.at[self.P.slab(y,dc=arrive),:,:,:,pl.ds(lo,n)]
        return rcopy(r,r,self.cs.at[g*2+k],self.cr.at[g*2+k],self.P.nc)
    def own(self,g):
        z=self.P.z; Z=self.P.Z
        when(z<Z-1,lambda: self.zcp(g,0,0,z,z+1).start())
        when(z>0,lambda: self.zcp(g,1,0,z,z-1).start())
        self.xfull(g,z).start(); self.yfull(g,z).start()
    def zarrive(self,g,t):
        z=self.P.z; Z=self.P.Z
        def below():
            zo=z-1-t
            self.zcp(g,0,t,zo,z).wait_recv()
            if t+1<Z-1:
                when(z<Z-1,lambda: self.zcp(g,0,t+1,zo,z+1).start())
            self.xfull(g,zo).start(); self.yfull(g,zo).start()
        def above():
            zo=z+1+t
            self.zcp(g,1,t,zo,z).wait_recv()
            if t+1<Z-1:
                when(z>0,lambda: self.zcp(g,1,t+1,zo,z-1).start())
            self.xfull(g,zo).start(); self.yfull(g,zo).start()
        when(z-1-t>=0,below); when(z+1+t<Z,above)
    def _diag(self,g,zo):
        self.xfull(g,zo,1).wait_recv(); self.ydiag(g,zo).start()
        self.yfull(g,zo,1).wait_recv(); self.xdiag(g,zo).start()
    def diag(self,g,t):
        z=self.P.z; Z=self.P.Z
        if t==0: self._diag(g,z)
        else:
            when(z-t>=0,lambda: self._diag(g,z-t))
            when(z+t<Z,lambda: self._diag(g,z+t))
    def corner(self,g):
        self.ccp(g,0).start()
        for zo in range(self.P.Z):
            self.ydiag(g,zo,1).wait_recv(); self.xdiag(g,zo,1).wait_recv()
        self.ccp(g,1).start()
    def sibling(self,g):
        self.ccp(g,0,1).wait_recv(); self.ccp(g,1,1).wait_recv()
    def drain(self,g):
        z=self.P.z; Z=self.P.Z
        for zo in range(Z):
            self.xfull(g,zo).wait_send(); self.yfull(g,zo).wait_send()
            self.xdiag(g,zo).wait_send(); self.ydiag(g,zo).wait_send()
        for k in range(2): self.ccp(g,k).wait_send()
        for t in range(Z-1):
            when(jnp.logical_and(z<Z-1,z-t>=0),lambda: self.zcp(g,0,t,z-t,z+1).wait_send())
            when(jnp.logical_and(z>0,z+t<=Z-1),lambda: self.zcp(g,1,t,z+t,z-1).wait_send())
    def events(self,g):
        Z=self.P.Z
        ev=[lambda: self.own(g)]
        for t in range(Z-1):
            ev.append(lambda t=t: self.zarrive(g,t))
            ev.append(lambda t=t: self.diag(g,t))
        ev.append(lambda: self.diag(g,Z-1))
        ev.append(lambda: self.corner(g))
        ev.append(lambda: self.sibling(g))
        return ev


SLOT = 1280
NB=7
def rs_sems(NG,Z):
    D=pltpu.SemaphoreType.DMA
    return [D((NG*2,)),D((NG*2,)),
            D((NG*3,)),D((NG*3,)),
            D((NG*2,)),D((NG*2,)),
            D((NG*2*Z,)),D((NG*2*Z,))]
def rs_bufs(Z):
    V=lambda *s: pltpu.VMEM(s,BF)
    h=640
    return [V(2,2,Z,2,16,SLOT),V(2,Z,2,16,h),V(2,Z,16,h),V(2,2,Z,16,h),V(2,Z,16,h),V(4,Z,16,SLOT),V(4,Z,16,SLOT)]
class Scatter:
    def __init__(self,P,R,groups,bufs,sems):
        self.P=P; self.R=R; self.groups=groups; self.bufs=bufs
        self.cs,self.cr,self.xs,self.xr,self.ys,self.yr,self.zs,self.zr=sems
    def buf(self,g,i,w):
        b=self.bufs[i]
        b=b.at[g%b.shape[0]]
        nd=len(b.shape)
        return b.at[(slice(None),)*(nd-1)+(pl.ds(0,w),)]
    def row(self,dy=0,dc=0):
        y=self.P.y if dy==0 else 1-self.P.y
        c=self.P.c if dc==0 else 1-self.P.c
        return y*2+c
    def add(self,dst,src):
        def body(z,_):
            d=dst(z); s=src(z)
            d[...]=(d[...].astype(F32)+s[...].astype(F32)).astype(BF)
            return 0
        lax.fori_loop(0,self.P.Z,body,0)
    def ccp(self,g,k):
        lo,n,_=self.groups[g]
        return rcopy(self.R.at[self.row(k,1),:,:,:,pl.ds(lo,n)],self.buf(g,0,n).at[k],self.cs.at[g*2+k],self.cr.at[g*2+k],self.P.nc)
    def x1(self,g,k):
        lo,n,a=self.groups[g]
        return rcopy(self.R.at[self.row(k),:,1-self.P.x,:,pl.ds(lo+a,n-a)],self.buf(g,3,n-a).at[k],self.xs.at[g*3+k],self.xr.at[g*3+k],self.P.nx)
    def y1(self,g):
        lo,n,a=self.groups[g]
        return rcopy(self.R.at[self.row(1),:,:,:,pl.ds(lo,a)],self.buf(g,1,a),self.ys.at[g*2],self.yr.at[g*2],self.P.ny)
    def x2(self,g):
        lo,n,a=self.groups[g]
        return rcopy(self.R.at[self.row(0),:,1-self.P.x,:,pl.ds(lo,a)],self.buf(g,2,a),self.xs.at[g*3+2],self.xr.at[g*3+2],self.P.nx)
    def y2(self,g):
        lo,n,a=self.groups[g]
        return rcopy(self.R.at[self.row(1),:,self.P.x,:,pl.ds(lo+a,n-a)],self.buf(g,4,n-a),self.ys.at[g*2+1],self.yr.at[g*2+1],self.P.ny)
    def zc(self,g,d,zo,to):
        lo,n,_=self.groups[g]; i=(g*2+d)*self.P.Z+zo
        return rcopy(self.R.at[self.row(0),zo,self.P.x,:,pl.ds(lo,n)],self.buf(g,5+d,n).at[zo],self.zs.at[i],self.zr.at[i],self.P.nz(to))
    def s_c(self,g):
        self.ccp(g,1).start(); self.ccp(g,0).start()
    def a_c(self,g):
        lo,n,a=self.groups[g]; R=self.R; b=self.buf(g,0,n)
        for k in (1,0):
            self.ccp(g,k).wait_recv()
            r=self.row(k)
            self.add(lambda z: R.at[r,z,:,:,pl.ds(lo,n)],lambda z: b.at[k,z])
            self.x1(g,k).start()
            if k==1: self.y1(g).start()
    def a_1(self,g):
        lo,n,a=self.groups[g]; R=self.R; P=self.P; B1=self.buf(g,1,a); B3=self.buf(g,3,n-a)
        self.y1(g).wait_recv()
        r=self.row(0)
        self.add(lambda z: R.at[r,z,:,:,pl.ds(lo,a)],lambda z: B1.at[z])
        for k in (1,0):
            self.x1(g,k).wait_recv()
            q=self.row(k)
            self.add(lambda z: R.at[q,z,P.x,:,pl.ds(lo+a,n-a)],lambda z: B3.at[k,z])
        self.x2(g).start()
        self.y2(g).start()
    def a_2(self,g):
        lo,n,a=self.groups[g]; R=self.R; P=self.P; B2=self.buf(g,2,a); B4=self.buf(g,4,n-a)
        r=self.row(0)
        self.x2(g).wait_recv()
        self.add(lambda z: R.at[r,z,P.x,:,pl.ds(lo,a)],lambda z: B2.at[z])
        self.y2(g).wait_recv()
        self.add(lambda z: R.at[r,z,P.x,:,pl.ds(lo+a,n-a)],lambda z: B4.at[z])
    def zstep(self,g,t):
        lo,n,_=self.groups[g]; R=self.R; P=self.P; Z=P.Z; z=P.z
        r=self.row(0)
        def acc(zo,b):
            d=R.at[r,zo,P.x,:,pl.ds(lo,n)]
            d[...]=(d[...].astype(F32)+b[zo].astype(F32)).astype(BF)
        def up():
            zo=Z-1-t
            @pl.when(z>0)
            def _():
                self.zc(g,0,zo,z).wait_recv()
                acc(zo,self.buf(g,5,n))
            self.zc(g,0,zo,z+1).start()
        def down():
            zo=t
            @pl.when(z<Z-1)
            def _():
                self.zc(g,1,zo,z).wait_recv()
                acc(zo,self.buf(g,6,n))
            self.zc(g,1,zo,z-1).start()
        when(z<Z-1-t,up); when(z>t,down)
    def final(self,g,out):
        lo,n,_=self.groups[g]; P=self.P; Z=P.Z; z=P.z
        out[...]=self.R[self.row(0),z,P.x,:,pl.ds(lo,n)].astype(F32)
        @pl.when(z>0)
        def _():
            self.zc(g,0,z,z).wait_recv()
            out[...]+=self.buf(g,5,n)[z].astype(F32)
        @pl.when(z<Z-1)
        def _():
            self.zc(g,1,z,z).wait_recv()
            out[...]+=self.buf(g,6,n)[z].astype(F32)
    def drain(self,g):
        Z=self.P.Z; z=self.P.z
        for k in range(2):
            self.ccp(g,k).wait_send(); self.x1(g,k).wait_send()
        self.x2(g).wait_send(); self.y1(g).wait_send(); self.y2(g).wait_send()
        for t in range(Z-1):
            when(z<Z-1-t,lambda: self.zc(g,0,Z-1-t,z+1).wait_send())
            when(z>t,lambda: self.zc(g,1,t,z-1).wait_send())
    def events(self,g,out):
        ev=[lambda: self.s_c(g),lambda: self.a_c(g),lambda: self.a_1(g),lambda: self.a_2(g)]
        for t in range(self.P.Z-1): ev.append(lambda t=t: self.zstep(g,t))
        ev.append(lambda: self.final(g,out))
        return ev

def norm_sems(Z):
    D=pltpu.SemaphoreType.DMA
    return [D((3+Z,)),D((3+Z,))]
def norm_bufs(Z): return [pltpu.VMEM((4+Z,8,128),F32),pltpu.VMEM((3,8,128),F32)]
def all_sum(P,buf,got,ss,rs):
    Z=P.Z
    for i,dev in enumerate((P.nc,P.nx,P.ny)):
        cp=rcopy(buf.at[i],got.at[i],ss.at[i],rs.at[i],dev)
        cp.start(); cp.wait()
        buf[i+1]=buf[i]+got[i]
    buf[4+P.z]=buf[3]
    for t in range(Z):
        def send(): rcopy(buf.at[3],buf.at[4+P.z],ss.at[3+t],rs.at[3+P.z],P.nz(t)).start()
        when(P.z!=t,send)
    for t in range(Z):
        def wait():
            cp=rcopy(buf.at[3],buf.at[4+t],ss.at[3+t],rs.at[3+t],P.nz(t))
            cp.wait_send(); cp.wait_recv()
        when(P.z!=t,wait)
    tot=buf[4]
    for t in range(1,Z): tot=tot+buf[4+t]
    return tot
def enter_all(P,Z):
    bar=pltpu.get_barrier_semaphore()
    def sig(d): pl.semaphore_signal(bar,inc=1,device_id=d,device_id_type=MESH)
    sig(P.nx); sig(P.ny); sig(P.nc)
    for t in range(Z):
        when(P.z!=t,lambda: sig(P.nz(t)))
    pl.semaphore_wait(bar,3+Z-1)


W3 = 768
CW = 1152
QKV_AT = 0
VEC_AT = 3456
VEC_COLS = 128
OUT_AT = 3584
DOWN_AT = 4736
UP_AT = 9344
COLS = 13952
GATHER = [(2304, 1280, 640), (0, 2304, 1152), (3584, 5760, 2944), (9344, 1152, 640), (10496, 1152, 512), (11648, 2304, 1152)]
SCATTER = ([(UP_AT + CW * c, CW, 640 if c % 2 else 512) for c in range(4)]
           + [(DOWN_AT + CW * c, CW, 640 if c % 2 else 512) for c in range(4)]
           + [(OUT_AT, CW, 512), (0, CW, 640), (CW, CW, 512), (2 * CW, 1280, 640)])

def al(v, m): return pl.multiple_of(v, m)

def third_cols(s): return [(D * j + 256 * s, 256) for j in range(3)]

def pack_rows(G, me, at, main, rest):
    G[(*me,slice(None),pl.ds(at,W3))]=main.astype(BF)
    parts=[jnp.concatenate([rest[:,256*s:256*s+128],rest[:,256*s+128:256*s+256]],0) for s in range(3)]
    G[(*me,slice(None),pl.ds(al(at+W3,128),W3//2))]=jnp.concatenate(parts,1).astype(BF)

def pack_own(place, G, wqkv, wout, wup, wdown, vec):
    me=place.me
    lo=al(8*place.x,8); ro=al(16*(1-place.x),8)
    def cols(w,cs):
        return [jnp.concatenate([w[pl.ds(a,n),pl.ds(c,k)] for c,k in cs],1) for a,n in ((lo,16),(ro,8))]
    for s in range(3): pack_rows(G,me,QKV_AT+CW*s,*cols(wqkv,third_cols(s)))
    pack_rows(G,me,OUT_AT,*cols(wout,[(0,W3)]))
    for c in range(4): pack_rows(G,me,UP_AT+CW*c,*cols(wup,[(W3*c,W3)]))
    for r in range(6):
        G[(*me,slice(None),pl.ds(DOWN_AT+r*D,D))]=wdown[pl.ds(16*r,16),:].astype(BF)
    G[(*me,slice(None),pl.ds(VEC_AT,VEC_COLS))]=vec[...]

def unpack24(G, at, dst):
    Z=G.shape[1]
    def body(j,_):
        r=al(j*48,16); d=j//Z; z=lax.rem(j,Z)
        dst[pl.ds(r,16),:]=G[d,z,0,:,pl.ds(al(at,128),W3)]
        dst[pl.ds(r+32,16),:]=G[d,z,1,:,pl.ds(al(at,128),W3)]
        a=G[d,z,0,:,pl.ds(al(at+W3,128),W3//2)].astype(F32)
        b=G[d,z,1,:,pl.ds(al(at+W3,128),W3//2)].astype(F32)
        parts=[]
        for s in range(3):
            q=slice(128*s,128*s+128)
            parts+=[jnp.concatenate([a[:8,q],b[:8,q]],0),jnp.concatenate([a[8:,q],b[8:,q]],0)]
        dst[pl.ds(r+16,16),:]=jnp.concatenate(parts,1).astype(BF)
        return 0
    lax.fori_loop(0,G.shape[0]*Z,body,0)

def pack24(G, at, src):
    Z=G.shape[1]
    def body(j,_):
        r=al(j*48,16); d=j//Z; z=lax.rem(j,Z)
        pack_rows(G,(d,z,0),al(at,128),src[pl.ds(r,16),:],src[pl.ds(al(r+16,8),8),:])
        pack_rows(G,(d,z,1),al(at,128),src[pl.ds(r+32,16),:],src[pl.ds(al(r+24,8),8),:])
        return 0
    lax.fori_loop(0,G.shape[0]*Z,body,0)

def unpack_down(G, c, dst):
    def body(k,_):
        for r in range(6):
            dst[pl.ds(al(k*96+16*r,16),16),:]=G[c,k//2,lax.rem(k,2),:,pl.ds(DOWN_AT+r*D,D)]
        return 0
    lax.fori_loop(0,2*G.shape[1],body,0)

def pack_down(G, c, src):
    def body(k,_):
        for r in range(6):
            G[c,k//2,lax.rem(k,2),:,pl.ds(DOWN_AT+r*D,D)]=src[pl.ds(al(k*96+16*r,16),16),:].astype(BF)
        return 0
    lax.fori_loop(0,2*G.shape[1],body,0)

def vec_shift(k): return (240*k)//128

def unpack_vec(G, V, V1):
    V[...]=jnp.zeros_like(V)
    Z=G.shape[1]
    for k in range(8*Z):
        V[pl.ds(vec_shift(k),3),:]+=G[k//(2*Z),k//2%Z,k%2,:,pl.ds(VEC_AT,VEC_COLS)].astype(F32)[0:3]
    for t in range(60):
        V1[:,pl.ds(128*t,128)]=V[pl.ds(t,1),:]

def pack_vec(G, V, V1):
    V[...]=jnp.zeros_like(V)
    for t in range(60):
        V[pl.ds(t,1),:]=V1[:,pl.ds(128*t,128)]
    Z=G.shape[1]
    for k in range(8*Z):
        G[k//(2*Z),k//2%Z,k%2,:,pl.ds(VEC_AT,VEC_COLS)]=V[pl.ds(vec_shift(k),16),:].astype(BF)

def norm_parts(x):
    c=x-jnp.mean(x,-1,keepdims=True)
    s=lax.rsqrt(jnp.mean(c*c,-1,keepdims=True)+EPS_NORM)
    return c*s,s

def norm_back(dx, xh, s):
    return s*(dx-jnp.mean(dx,-1,keepdims=True)-xh*jnp.mean(dx*xh,-1,keepdims=True))

def gelu_both(u):
    k0=0.7978845608028654; k1=0.044715
    u2=u*u
    t=jnp.tanh(k0*(u*(1.0+k1*u2)))
    h=0.5*(1.0+t)
    return u*h, h+(0.5*k0)*u*(1.0-t*t)*(1.0+(3.0*k1)*u2)

RB=256

RULES=((1,1,0),(2,3,1),(2,7,4))

class Clock:
    def __init__(self, places):
        self.times=places
        self.slots={}
        self.tail=[]
    def fill(self, events, deadlines):
        index={(n,s):i for i,(n,s,_) in enumerate(self.times)}
        times=[t for _,_,t in self.times]
        where={}
        last=0
        for time,key,fn in sorted(events,key=lambda e: e[0]):
            i=next((i for i,t in enumerate(times) if t>=time),len(times))
            where[key]=i
        for key,place in deadlines.items():
            where[key]=min(where[key],index[place])
        keys=sorted(where,key=lambda k:(k[0],k[1],-k[2]))
        prev=None
        for k in keys:
            if prev is not None and prev[:2]==k[:2]: where[k]=min(where[k],where[prev])
            prev=k
        fns={key:(time,fn) for time,key,fn in events}
        self.where=where
        self.order=[]
        for key in sorted(where,key=lambda k:(where[k],fns[k][0],k)):
            i=where[key]
            self.order.append(key)
            if i<len(times): self.slots.setdefault(self.times[i][:2],[]).append(fns[key][1])
            else: self.tail.append(fns[key][1])
    def at(self, name, step, count):
        for k in range(count):
            todo=self.slots.get((name,k))
            if todo:
                def run(todo=todo):
                    for f in todo: f()
                if isinstance(step,int):
                    if step==k: run()
                else: pl.when(step==k)(run)

def schedule(sched):
    p=[]
    t=[0.0]
    def add(name,step,dt):
        p.append((name,step,t[0])); t[0]+=dt
    for i in range(4): add("stat",i,0.5)
    t[0]=max(t[0],sched["first"])
    for i in range(3):
        add("third",i,0.6)
        for k in range(4): add("qkv",4*i+k,0.4)
        for pp in range(2):
            for k in range(4): add("af",8*i+4*pp+k,(0.8,0.8,1.4,1.4)[k])
    add("out",0,0.6)
    for k in range(4): add("ob",k,1.0)
    for c in range(4):
        add("chunk",c,1.0)
        for k in range(4): add("mr",4*c+k,1.35)
        for k in range(3): add("mw",3*c+k,0.6)
        for k in range(3): add("mu",3*c+k,0.6)
        add("mp",c,0.3)
    for k in range(4): add("bb",k,1.2)
    for k in range(3): add("bw",k,0.6)
    add("bp",0,0.3)
    for i in range(3):
        for pp in range(2):
            for k in range(4): add("ab",8*i+4*pp+k,0.9)
        for k in range(4): add("dh",4*i+k,0.5)
        if i==2:
            for k in range(4): add("ln",k,0.8)
        for k in range(3): add("dq",3*i+k,0.6)
        add("dp",i,0.3)
    return p

def mega_kernel(Z,sched,tok_h,cot_h,len_ref,wqkv_s,wout_s,wup_s,wdown_s,vec_s,
               mixed_o,dtok_o,own_o,nrm_o,
               G,tok,cot,F1,F2,F3,qkv,B1,B2,B3,hT,aT,oT,W0,W1,dW,lse,V,V1,dV1,dka,dva,own,nrm,dsem,*rest):
    gsems=rest[:8]; rbufs=rest[8:8+NB]; rsems=rest[8+NB:16+NB]; nb,got,ns,nr=rest[16+NB:]
    L=tok.shape[0]
    NBK=L//RB
    place=Place(Z)
    def dma(a,b,i):
        cp=pltpu.make_async_copy(a,b,dsem.at[i]); cp.start(); return cp
    ldt=dma(tok_h,tok,0); ldc=dma(cot_h,cot,1)
    pack_own(place,G,wqkv_s,wout_s,wup_s,wdown_s,vec_s)
    enter_all(place,Z)
    ga=Gather(place,G,GATHER,gsems)
    sc=Scatter(place,G,SCATTER,rbufs,rsems)
    clock=Clock(schedule(sched))
    events=[]; deadlines={}
    w=0.0
    for g,(lo,n,_) in enumerate(GATHER):
        d=sched["link"]*n/COLS
        ev=ga.events(g)
        for k,f in enumerate(ev):
            if k==0: time=max(0.0,w-sched["ahead"])
            else: time=w+sched["lat"]+d*min(k,len(ev)-2)/(len(ev)-2)+(sched["sib"] if k==len(ev)-1 else 0.0)
            events.append((time,("g",g,k),f))
        w+=d
    for g,place_ in enumerate((("third",0),("third",1),("out",0),("chunk",0),("chunk",1),("chunk",2))):
        deadlines[("g",g,9)]=place_
    tm={(n,s):t for n,s,t in clock.times}
    ready=[tm[("mp",c)] for c in range(4)]+[tm[("mp",3)]+sched["dgap"]*(k+1) for k in range(4)]+[tm[("bp",0)]]+[tm[("dp",i)] for i in range(3)]
    rt=sched["rs"]
    at_=[]
    for g,(lo,n,_) in enumerate(SCATTER):
        ev=sc.events(g,own.at[:,pl.ds(lo,n)])
        at_.append([])
        t=ready[g]
        for k,f in enumerate(ev):
            t=t+rt[k]
            if g: t=max(t,at_[g-1][k]+0.01)
            for back_,slot,first in RULES:
                if k==first and g>=back_: t=max(t,at_[g-back_][slot]+0.01)
            at_[g].append(t)
            events.append((t,("s",g,k),f))
    clock.fill(events,deadlines)
    index={(n,s):i for i,(n,s,_) in enumerate(clock.times)}
    after=[("mp",c) for c in range(4)]+[("mp",3)]*4+[("bp",0)]+[("dp",i) for i in range(3)]
    for g in range(len(SCATTER)): assert clock.where[("s",g,0)]>=index[after[g]]
    pos={k:i for i,k in enumerate(clock.order)}
    for g in range(len(SCATTER)):
        for back_,slot,first in RULES:
            if g>=back_: assert pos[("s",g-back_,slot)]<pos[("s",g,first)]
        for k in range(1,8): assert pos[("s",g,k-1)]<pos[("s",g,k)]
    def at(name,step,count): clock.at(name,step,count)
    def rows(i): return pl.ds(al(i*RB,RB),RB)
    length=len_ref[0]
    ldt.wait()
    xhat=F1; h1=B1; o=B3
    for i in range(4):
        at("stat",i,4)
        if i<NBK:
            xhat[rows(i),:]=norm_parts(tok[rows(i),:].astype(F32))[0]
    def third(i,_):
        s=lax.rem(i+2,3)
        at("third",i,3)
        @pl.when(i==0)
        def _():
            unpack_vec(G,V,V1)
            def first(j,_):
                h1[rows(j),:]=(xhat[rows(j),:]*V1[:,0:D]+V1[:,D:2*D]).astype(BF)
                return 0
            lax.fori_loop(0,NBK,first,0)
        unpack24(G,QKV_AT+CW*s,W0)
        def block(j,_):
            at("qkv",4*i+j,12)
            qkv[s,rows(j),:]=nn(h1[rows(j),:],W0[...]).astype(BF)
            return 0
        lax.fori_loop(0,NBK,block,0)
        def pair(pp,_):
            p=2*s+pp
            def col(j): return qkv.at[s,:,pl.ds(al(256*j+128*pp,128),128)]
            c=pl.ds(al(128*p,128),128)
            attn_fwd_pair(col(0),col(1),col(2),length,o.at[:,c],oT.at[c,:],lse.at[p],512,
                          tick=lambda k: at("af",8*i+4*pp+k,24))
            return 0
        lax.fori_loop(0,2,pair,0)
        return 0
    lax.fori_loop(0,3,third,0)
    at("out",0,1)
    unpack24(G,OUT_AT,W0)
    ldc.wait()
    r1=F1; mixed=F2; dh2=F3; h2=B1; h2T=hT
    def out_block(i,_):
        at("ob",i,4)
        sl=rows(i)
        r=tok[sl,:].astype(F32)+nn(o[sl,:],W0[...])+V1[:,4*D:5*D]
        r1[sl,:]=r
        mixed[sl,:]=r+V1[:,5*D:6*D]
        hb=(norm_parts(r)[0]*V1[:,2*D:3*D]+V1[:,3*D:4*D]).astype(BF)
        h2[sl,:]=hb
        h2T[:,sl]=hb.T
        pos_=i*RB+lax.broadcasted_iota(jnp.int32,(RB,D),0)
        cot[sl,:]=jnp.where(pos_<length,cot[sl,:],jnp.zeros((),BF))
        dh2[sl,:]=jnp.zeros((RB,D),F32)
        return 0
    lax.fori_loop(0,NBK,out_block,0)
    du_s=B2
    def chunk(c,_):
        at("chunk",c,4)
        for g,when_ in enumerate((0,0,0,0,1,2)):
            pl.when(c==when_)(lambda g=g: ga.drain(g))
        unpack24(G,UP_AT+CW*c,W0)
        unpack_down(G,c,W1)
        bu=V1[:,pl.ds(al(6*D+c*W3,128),W3)]
        def mrows(i,acc):
            at("mr",4*c+i,16)
            sl=rows(i)
            u=nn(h2[sl,:],W0[...])+bu
            a,slope=gelu_both(u)
            ab=a.astype(BF)
            mixed[sl,:]+=nn(ab,W1[...])
            aT[:,sl]=ab.T
            du=(nt(cot[sl,:],W1[...])*slope).astype(BF)
            du_s[sl,:]=du
            dh2[sl,:]+=nt(du,W0[...])
            return acc+jnp.sum(du.astype(F32),0,keepdims=True)
        s=lax.fori_loop(0,NBK,mrows,jnp.zeros((1,W3),F32))
        dV1[:,pl.ds(al(6*D+c*W3,128),W3)]=s
        def wrows(i,_):
            at("mw",3*c+i,12)
            dW[rows(i),:]=nn(aT[rows(i),:],cot[...])
            return 0
        lax.fori_loop(0,W3//RB,wrows,0)
        pack_down(G,c,dW)
        def urows(i,_):
            at("mu",3*c+i,12)
            dW[rows(i),:]=nn(h2T[rows(i),:],du_s[...])
            return 0
        lax.fori_loop(0,D//RB,urows,0)
        pack24(G,UP_AT+CW*c,dW)
        at("mp",c,4)
        return 0
    lax.fori_loop(0,FF//W3,chunk,0)
    mixed_b=B2
    def fin(i,_):
        mixed_b[rows(i),:]=mixed[rows(i),:].astype(BF)
        return 0
    lax.fori_loop(0,NBK,fin,0)
    outs=[dma(mixed_b,mixed_o,2)]
    unpack24(G,OUT_AT,W0)
    dr1=F3; dy=B3; do=B1
    def back(i,acc):
        at("bb",i,4)
        sl=rows(i)
        dh=dh2[sl,:]
        xh,s=norm_parts(r1[sl,:])
        g=cot[sl,:].astype(F32)
        dr=g+norm_back(dh*V1[:,2*D:3*D],xh,s)
        dr1[sl,:]=dr
        dyb=dr.astype(BF)
        dy[sl,:]=dyb
        do[sl,:]=nt(dyb,W0[...]).astype(BF)
        new=(dh*xh,dh,dyb.astype(F32),g)
        return tuple(a+jnp.sum(b,0,keepdims=True) for a,b in zip(acc,new))
    z1=jnp.zeros((1,D),F32)
    sums=lax.fori_loop(0,NBK,back,(z1,z1,z1,z1))
    for j,v in enumerate(sums): dV1[:,pl.ds((2+j)*D,D)]=v
    def orow(i,_):
        at("bw",i,3)
        dW[rows(i),:]=nn(oT[rows(i),:].astype(BF),dy[...])
        return 0
    lax.fori_loop(0,D//RB,orow,0)
    pack24(G,OUT_AT,dW)
    at("bp",0,1)
    h1T=hT; dqkv=B3; dh1=F2
    outs[0].wait()
    def again(i,_):
        sl=rows(i)
        hb=(norm_parts(tok[sl,:].astype(F32))[0]*V1[:,0:D]+V1[:,D:2*D]).astype(BF)
        h1T[:,sl]=hb.T
        dh1[sl,:]=jnp.zeros((RB,D),F32)
        return 0
    lax.fori_loop(0,NBK,again,0)
    def third_back(s,_):
        unpack24(G,QKV_AT+CW*s,W0)
        def pair(pp,_):
            p=2*s+pp
            def col(j): return qkv.at[s,:,pl.ds(al(256*j+128*pp,128),128)]
            def dcol(j): return dqkv.at[:,pl.ds(al(256*j+128*pp,128),128)]
            c=pl.ds(al(128*p,128),128)
            attn_bwd_pair(col(0),col(1),col(2),do.at[:,c],oT.at[c,:],lse.at[p],length,
                          dcol(0),dcol(1),dcol(2),dka,dva,256,tick=lambda k: at("ab",8*s+4*pp+k,24))
            return 0
        lax.fori_loop(0,2,pair,0)
        def drow(i,_):
            at("dh",4*s+i,12)
            dh1[rows(i),:]+=nt(dqkv[rows(i),:],W0[...])
            return 0
        lax.fori_loop(0,NBK,drow,0)
        @pl.when(s==2)
        def _():
            def lrow(i,acc):
                at("ln",i,4)
                sl=rows(i)
                dh=dh1[sl,:]
                xh,r=norm_parts(tok[sl,:].astype(F32))
                F1[sl,:]=dr1[sl,:]+norm_back(dh*V1[:,0:D],xh,r)
                return tuple(a+jnp.sum(b,0,keepdims=True) for a,b in zip(acc,(dh*xh,dh)))
            a,b=lax.fori_loop(0,NBK,lrow,(z1,z1))
            dV1[:,0:D]=a
            dV1[:,D:2*D]=b
            pack_vec(G,V,dV1)
        def qrow(i,_):
            at("dq",3*s+i,9)
            dW[rows(i),:]=nn(h1T[rows(i),:],dqkv[...])
            return 0
        lax.fori_loop(0,D//RB,qrow,0)
        pack24(G,QKV_AT+CW*s,dW)
        at("dp",s,3)
        return 0
    lax.fori_loop(0,3,third_back,0)
    outs=[dma(F1,dtok_o,3)]
    for f in clock.tail: f()
    flat=lax.broadcasted_iota(jnp.int32,(16,VEC_COLS),0)*VEC_COLS+lax.broadcasted_iota(jnp.int32,(16,VEC_COLS),1)
    start=lax.rem(240*((place.dp*Z+place.z)*2+place.x),128)
    vec=own[:,pl.ds(VEC_AT,VEC_COLS)]
    vec=jnp.where(jnp.logical_and(flat>=start,flat<start+240),vec,0.0)
    left=own[:,pl.ds(0,VEC_AT)]; right=own[:,pl.ds(OUT_AT,COLS-OUT_AT)]
    nb[0]=jnp.full((8,128),1.0,F32)*(jnp.sum(left*left)+jnp.sum(right*right)+jnp.sum(vec*vec))
    outs.append(dma(own,own_o,4))
    nrm[...]=all_sum(place,nb,got,ns,nr)
    outs.append(dma(nrm,nrm_o,5))
    for g in range(len(SCATTER)): sc.drain(g)
    for cp in outs: cp.wait()

SCHED=dict(first=14.0,link=57.0,ahead=4.0,lat=4.0,sib=2.0,dgap=1.5,rs=[0,1.8,4.5,3.0,1.5,2.0,2.0,2.0])
def mega_call(Z,tok,cot,length,wqkv,wout,wup,wdown,vec,sched=SCHED):
    L=tok.shape[0]; pieces=8*Z
    S=jax.ShapeDtypeStruct; V=pltpu.VMEM
    vm=pl.BlockSpec(memory_space=pltpu.VMEM); an=pl.BlockSpec(memory_space=pl.ANY); sm=pl.BlockSpec(memory_space=pltpu.SMEM)
    outs=[S((L,D),BF),S((L,D),F32),S((16,COLS),F32),S((8,128),F32)]
    f=lambda: V((L,D),F32)
    b=lambda: V((L,D),BF)
    scratch=[V((4,Z,2,16,COLS),BF),b(),b(),f(),f(),f(),V((3,L,D),BF),b(),b(),b(),V((D,L),BF),V((D,L),BF),V((D,L),F32),
             V((D,W3),BF),V((W3,D),BF),V((D,W3),F32),V((6,2,L),F32),V((80,128),F32),V((1,10*D),F32),V((1,10*D),F32),
             V((L,128),F32),V((L,128),F32),V((16,COLS),F32),V((8,128),F32),pltpu.SemaphoreType.DMA((6,))]
    return pl.pallas_call(functools.partial(mega_kernel,Z,sched),out_shape=outs,
        in_specs=[an,an,sm]+[vm]*5,out_specs=[an]*len(outs),
        scratch_shapes=scratch+gather_sems(len(GATHER),Z)+rs_bufs(Z)+rs_sems(len(SCATTER),Z)+norm_bufs(Z)+norm_sems(Z),
        compiler_params=pltpu.CompilerParams(collective_id=1,has_side_effects=True,vmem_limit_bytes=63*2**20),
        cost_estimate=pl.CostEstimate(flops=60*10**9,bytes_accessed=60*2**20,transcendentals=10**7))(tok,cot,length,wqkv,wout,wup,wdown,vec)


def adam_step(weight, first_mom, second_mom, gradient, step_rate):
    first_new = BETA_ONE * first_mom + (1.0 - BETA_ONE) * gradient
    second_new = BETA_TWO * second_mom + (1.0 - BETA_TWO) * gradient * gradient
    fix_one = 1.0 - BETA_ONE**STEP
    fix_two = 1.0 - BETA_TWO**STEP
    update = (
        first_new / fix_one / (jnp.sqrt(second_new / fix_two) + ADAM_EPSILON) + DECAY_RATE * weight
    )
    return (weight - step_rate * update, first_new, second_new)


def adam_kernel(par_ref, own, nrm, *refs):
    ins, outs = refs[:12], refs[12:]
    factor = jnp.minimum(1.0, CLIP_NORM / (jnp.sqrt(nrm[0:1, 0:1]) + 1e-06))
    main_at = al(8 * par_ref[0], 8)
    rest_at = al(16 * (1 - par_ref[0]), 8)

    def step(i, rows, cols, grad, rate):
        w, m, v = [r[rows, cols] for r in ins[3 * i : 3 * i + 3]]
        new = adam_step(w, m, v, grad * factor, rate)
        for r, a in zip(outs[3 * i : 3 * i + 3], new):
            r[rows, cols] = a

    def chunk(i, at, cols, rate):
        main = own[:, pl.ds(at, W3)]
        packed = own[:, pl.ds(at + W3, W3 // 2)]
        parts = []
        for s in range(3):
            parts += [packed[:8, 128 * s : 128 * s + 128], packed[8:, 128 * s : 128 * s + 128]]
        rest = jnp.concatenate(parts, 1)
        done = 0
        for c, n in cols:
            step(i, pl.ds(main_at, 16), pl.ds(c, n), main[:, done : done + n], rate)
            step(i, pl.ds(rest_at, 8), pl.ds(c, n), rest[:, done : done + n], rate)
            done += n

    for s in range(3):
        chunk(0, QKV_AT + CW * s, third_cols(s), D ** (-0.5))
    chunk(1, OUT_AT, [(0, W3)], D ** (-0.5))
    for c in range(4):
        chunk(2, UP_AT + CW * c, [(W3 * c, W3)], D ** (-0.5))
    for r in range(6):
        grad = own[:, pl.ds(DOWN_AT + r * D, D)]
        step(3, pl.ds(16 * r, 16), slice(None), grad, FF ** (-0.5))


def adam_call(parity, own, nrm, states):
    vm = pl.BlockSpec(memory_space=pltpu.VMEM)
    sm = pl.BlockSpec(memory_space=pltpu.SMEM)
    return pl.pallas_call(
        adam_kernel,
        out_shape=[jax.ShapeDtypeStruct(a.shape, F32) for a in states],
        in_specs=[sm, vm, vm] + [vm] * 12,
        out_specs=[vm] * 12,
        compiler_params=pltpu.CompilerParams(vmem_limit_bytes=40 * 2**20),
        cost_estimate=pl.CostEstimate(
            flops=10**7, bytes_accessed=8 * 2**20, transcendentals=10**6
        ),
    )(parity, own, nrm, *states)


def layer_norm(values, gain, shift):
    center = jnp.mean(values, -1, keepdims=True)
    centered = values - center
    spread = jnp.mean(centered * centered, -1, keepdims=True)
    return centered * lax.rsqrt(spread + EPS_NORM) * gain + shift


def smooth_gate(value):
    return jax.nn.gelu(value, approximate=True)


def plain_shards(tokens, lengths, cotangent, *state):
    w_qkv, m_qkv, v_qkv, w_out, m_out, v_out, w_up, m_up, v_up = state[:9]
    w_down, m_down, v_down, packed, m_packed, v_packed = state[9:]
    seq_count, seq_len, model_width = tokens.shape
    row_count = seq_count * seq_len
    axes = ("dp", "fsdp")
    wqkv_b, wout_b, wup_b, wdown_b, vector_b = [
        lax.all_gather(w.astype(BF), axes, axis=0, tiled=True)
        for w in (w_qkv, w_out, w_up, w_down, packed)
    ]
    vector = vector_b.astype(F32)
    gain_one, bias_one, gain_two, bias_two, bias_attn, bias_down = [
        vector[i * model_width : (i + 1) * model_width] for i in range(6)
    ]
    bias_up = vector[6 * model_width :]
    positions = jnp.arange(seq_len, dtype=jnp.int32)
    live_rows = positions[None, :] < lengths[:, None]
    inputs = tokens.astype(F32).reshape(row_count, model_width)
    normed_one, norm_one_back = jax.vjp(layer_norm, inputs, gain_one, bias_one)
    normed_one_b = normed_one.astype(BF)
    qkv_all = jnp.dot(normed_one_b, wqkv_b, preferred_element_type=F32).astype(BF)
    seqs = [slice(i * seq_len, (i + 1) * seq_len) for i in range(seq_count)]
    ahead = [fwd_call(qkv_all[s], lengths[i : i + 1], 512) for i, s in enumerate(seqs)]
    attended_b = jnp.concatenate([a[0] for a in ahead], 0)
    resid_one = inputs + jnp.dot(attended_b, wout_b, preferred_element_type=F32) + bias_attn
    normed_two, norm_two_back = jax.vjp(layer_norm, resid_one, gain_two, bias_two)
    normed_two_b = normed_two.astype(BF)
    upper = jnp.dot(normed_two_b, wup_b, preferred_element_type=F32) + bias_up
    activ, gate_back = jax.vjp(smooth_gate, upper)
    activ_b = activ.astype(BF)
    mixed = resid_one + jnp.dot(activ_b, wdown_b, preferred_element_type=F32) + bias_down
    mixed = mixed.reshape(seq_count, seq_len, model_width).astype(BF)
    grad_b = jnp.where(live_rows[:, :, None], cotangent, jnp.zeros((), BF))
    grad_b = grad_b.reshape(row_count, model_width)
    grad_full = grad_b.astype(F32)
    d_wdown = jnp.dot(activ_b.T, grad_b, preferred_element_type=F32)
    d_bias_down = jnp.sum(grad_full, 0)
    d_activ = jnp.dot(grad_b, wdown_b.T, preferred_element_type=F32)
    (d_upper,) = gate_back(d_activ)
    d_upper_b = d_upper.astype(BF)
    d_bias_up = jnp.sum(d_upper_b.astype(F32), 0)
    d_wup = jnp.dot(normed_two_b.T, d_upper_b, preferred_element_type=F32)
    d_normed_two = jnp.dot(d_upper_b, wup_b.T, preferred_element_type=F32)
    d_resid_norm, d_gain_two, d_bias_two = norm_two_back(d_normed_two)
    d_resid = grad_full + d_resid_norm
    d_branch_b = d_resid.astype(BF)
    d_bias_attn = jnp.sum(d_branch_b.astype(F32), 0)
    d_wout = jnp.dot(attended_b.T, d_branch_b, preferred_element_type=F32)
    d_attended_b = jnp.dot(d_branch_b, wout_b.T, preferred_element_type=F32).astype(BF)
    back = [
        bwd_call(qkv_all[s], d_attended_b[s], a[1], a[2], lengths[i : i + 1])
        for i, (s, a) in enumerate(zip(seqs, ahead))
    ]
    d_qkv_b = jnp.concatenate([jnp.concatenate(b, 1) for b in back], 0)
    d_wqkv = jnp.dot(normed_one_b.T, d_qkv_b, preferred_element_type=F32)
    d_normed_one = jnp.dot(d_qkv_b, wqkv_b.T, preferred_element_type=F32)
    d_input_norm, d_gain_one, d_bias_one = norm_one_back(d_normed_one)
    d_tokens = (d_resid + d_input_norm).reshape(seq_count, seq_len, model_width)
    d_vector = jnp.concatenate(
        [d_gain_one, d_bias_one, d_gain_two, d_bias_two, d_bias_attn, d_bias_down, d_bias_up]
    )
    owned = [
        lax.psum_scatter(g, axes, scatter_dimension=0, tiled=True)
        for g in (d_wqkv, d_wout, d_wup, d_wdown, d_vector)
    ]
    grad_norm = jnp.sqrt(lax.psum(sum(jnp.sum(g * g) for g in owned), axes))
    factor = jnp.minimum(1.0, CLIP_NORM / (grad_norm + 1e-06))
    rates = (D ** (-0.5), D ** (-0.5), D ** (-0.5), FF ** (-0.5), VECTOR_RATE)
    new = ()
    for i, (g, rate) in enumerate(zip(owned, rates)):
        new += adam_step(*state[3 * i : 3 * i + 3], g * factor, rate)
    return (mixed, d_tokens, grad_norm) + new


def direct_shards(Z, tokens, lengths, cotangent, *state):
    packed, m_packed, v_packed = state[12:]
    dp = lax.axis_index("dp")
    fsdp = lax.axis_index("fsdp")
    n = packed.shape[0]
    start = ((dp * 2 * Z + fsdp) * n) % VEC_COLS
    vec = lax.dynamic_update_slice(
        jnp.zeros((16 * VEC_COLS,), BF), packed.astype(BF), (start,)
    ).reshape(16, VEC_COLS)
    mixed, d_tokens, own, norm_tile = mega_call(
        Z, tokens[0], cotangent[0], lengths, state[0], state[3], state[6], state[9], vec
    )
    grad_norm = jnp.sqrt(norm_tile[0, 0])
    factor = jnp.minimum(1.0, CLIP_NORM / (grad_norm + 1e-06))
    parity = (fsdp % 2).astype(jnp.int32).reshape(1)
    new = adam_call(parity, own, norm_tile, state[:12])
    g_vec = lax.dynamic_slice(own[:, VEC_AT:OUT_AT].reshape(-1), (start,), (n,))
    new_vec = adam_step(packed, m_packed, v_packed, g_vec * factor, VECTOR_RATE)
    return (mixed[None], d_tokens[None], grad_norm) + tuple(new) + new_vec


def solution(mesh):
    rows = P(("dp", "fsdp"), None)
    seqs = P(("dp", "fsdp"), None, None)
    flat = P(("dp", "fsdp"))
    in_specs = (seqs, flat, seqs) + (rows,) * 12 + (flat,) * 3
    out_specs = (seqs, seqs, P()) + (rows,) * 12 + (flat,) * 3
    dp, fsdp = mesh.shape["dp"], mesh.shape["fsdp"]

    def shards(*args):
        tokens, w_qkv = args[0], args[3]
        fits = (
            dp == 4
            and fsdp == 8
            and tokens.shape[0] == 1
            and tokens.shape[1] == 1024
            and w_qkv.shape[0] * dp * fsdp == D
        )
        step = functools.partial(direct_shards, fsdp // 2) if fits else plain_shards
        return step(*args)

    return jax.shard_map(
        shards, mesh=mesh, in_specs=in_specs, out_specs=out_specs, check_vma=False
    )
```

profile of v0, /device:TPU:0, one launch (start us, length us, event | category | flops | bytes accessed | tf_op | source)
XLA Modules:
  0.0 322.7 jit_solution(7987579120166020638)
XLA Ops:
  1.3 0.7 convert_element_type.3
  2.0 0.2 dynamic_update_slice.3
  2.2 0.0 copy-start.16
  2.2 0.6 copy-done.16
  2.8 0.0 copy-start.1
  2.8 300.1 %shard_map.313 = (bf16[1024,768]{1,0:T(8,128)(2,1)}, f32[1024,768]{1,0:T(8,128)}, f32[16,13952]{1,0:T(8,128)}, f32[8,128]{1,0:T(8,128)}) custom-call(bf16[1024,768]{1,0:T(8,128)(2,1)} %bitcast.12, bf16[1024,768]{1,0:T(8,128)(2,1)} %bitcast.13, s32[1]{0:T(128)S(6)} %copy.39.len_ref, f32[24,2304]{1,0:T(8,128)} %refs_0_.1, f32[24,768]{1,0:T(8,128)} %refs_3_.1, ...), custom_call_target="tpu_custom_call" | custom-call | flops 60000002048 | bytes 62914560 | tf_op jit(solution)/shard_map/pallas_call | solution.py:816
  302.9 1.2 slice.6
  304.8 0.0 copy-done.1
  304.8 0.0 copy-done.2
  304.8 0.0 copy-done.3
  304.8 0.0 copy-done.10
  304.8 0.0 copy-start
  304.8 1.2 copy-done
  306.0 1.0 copy-done.4
  307.0 1.0 copy-done.5
  307.9 1.0 copy-done.6
  308.9 0.9 copy-done.7
  309.8 0.9 copy-done.8
  310.8 0.9 copy-done.9
  311.7 0.9 copy-done.11
  312.6 0.9 copy-done.12
  313.5 0.7 copy-done.13
  314.1 1.8 shard_map.314
  316.0 0.7 slice_bitcast_fusion
  316.7 0.0 copy-done.17
  316.7 0.0 copy-done.18
  316.7 0.0 copy-done.19
  316.8 0.7 multiply_subtract_fusion
  317.4 0.0 copy-done.15
  317.4 1.1 copy.40
  318.6 1.3 copy-done.14
  319.9 1.7 copy.41
  (18 shorter events, 0.0 us)
Async XLA Ops:
  2.2 0.6 copy-start.16
  2.8 302.0 %copy-start.1 = (f32[24,3072]{1,0:T(8,128)S(1)}, f32[24,3072]{1,0:T(8,128)}, u32[]{:S(2)}) copy-start(f32[24,3072]{1,0:T(8,128)} %refs_6_.1) | copy-start | bytes 884740
  2.8 302.0 %copy-start.2 = (f32[96,768]{1,0:T(8,128)S(1)}, f32[96,768]{1,0:T(8,128)}, u32[]{:S(2)}) copy-start(f32[96,768]{1,0:T(8,128)} %refs_9_.1) | copy-start | bytes 884740
  2.8 302.0 %copy-start.3 = (f32[24,3072]{1,0:T(8,128)S(1)}, f32[24,3072]{1,0:T(8,128)}, u32[]{:S(2)}) copy-start(f32[24,3072]{1,0:T(8,128)} %refs_7_.1) | copy-start | bytes 884740
  2.8 302.0 %copy-start.10 = (f32[24,768]{1,0:T(8,128)S(1)}, f32[24,768]{1,0:T(8,128)}, u32[]{:S(2)}) copy-start(f32[24,768]{1,0:T(8,128)} %refs_3_.1) | copy-start | bytes 221188
  304.8 1.2 copy-start
  306.0 1.0 copy-start.4
  307.0 1.0 copy-start.5
  307.9 1.0 copy-start.6
  308.9 0.9 copy-start.7
  309.8 0.9 copy-start.8
  310.7 0.9 copy-start.9
  311.7 0.9 copy-start.11
  312.6 0.9 copy-start.12
  313.5 0.7 copy-start.13
  314.1 2.6 copy-start.17
  314.1 2.6 copy-start.18
  314.1 2.6 copy-start.19
  314.1 3.3 %copy-start.15 = (bf16[1024,768]{1,0:T(8,128)(2,1)S(1)}, bf16[1024,768]{1,0:T(8,128)(2,1)}, u32[]{:S(2)}) copy-start(bf16[1024,768]{1,0:T(8,128)(2,1)} %get-tuple-element.34) | copy-start | bytes 4718596
  317.4 2.5 copy-start.14
where the time goes:
time: 323 us
  Pallas kernels  302 us (93%)
  local copies, waits for them, and re-layouts  16.1 us (5%)
  between operations  3.26 us (1%)
    pallas_call x1, Pallas kernels, mega_call(): pl.pallas_call(functools.partial(mega_kernel, Z, sched), out_shape=outs,...  300 us
    unnamed x42, local copies, waits for them, and re-layouts  14 us

commit v1 on v0

--- a/solution.py
+++ b/solution.py
@@ -40,6 +40,7 @@
     for i in range(L//QB):
         nk=(i+1)*QB
         qs=q_ref[pl.ds(i*QB,QB),:]
+        if tick is not None: tick(i)
         outs=[]
         jidx=lax.broadcasted_iota(jnp.int32,(nk,QB),0)
         lim=jnp.minimum(i*QB+1+lax.broadcasted_iota(jnp.int32,(1,QB),1),length)
@@ -52,7 +53,6 @@
             oT=nn(vT[HD*h:HD*h+HD,:nk],e.astype(BF))
             outs.append(oT/l)
             lse_ref[pl.ds(h,1),pl.ds(i*QB,QB)]=m+jnp.log(l)
-            if tick is not None: tick(2*i+h)
         oT=jnp.concatenate(outs,0)
         oT_ref[:,pl.ds(i*QB,QB)]=oT
         o_ref[pl.ds(i*QB,QB),:]=oT.T.astype(BF)
@@ -61,6 +61,7 @@
     L=q_ref.shape[0]
     kT=k_ref[...].T
     for i in reversed(range(L//QB)):
+        if tick is not None: tick(L//QB-1-i)
         nk=(i+1)*QB
         sl=pl.ds(i*QB,QB)
         qs=q_ref[sl,:]; do=do_ref[sl,:]
@@ -90,7 +91,6 @@
             dk_acc[...]=dk; dv_acc[...]=dv
         else:
             dk_acc[pl.ds(0,nk),:]+=dk; dv_acc[pl.ds(0,nk),:]+=dv
-        if tick is not None: tick(L//QB-1-i)
     dk_ref[...]=dk_acc[...].astype(BF); dv_ref[...]=dv_acc[...].astype(BF)
 
 def fwd_call(qkv,length,QB=256):
@@ -261,7 +261,7 @@
     def add(self,dst,src):
         def body(z,_):
             d=dst(z); s=src(z)
-            d[...]=(d[...].astype(F32)+s[...].astype(F32)).astype(BF)
+            d[...]=d[...]+s[...]
             return 0
         lax.fori_loop(0,self.P.Z,body,0)
     def ccp(self,g,k):
@@ -310,27 +310,31 @@
         self.add(lambda z: R.at[r,z,P.x,:,pl.ds(lo,a)],lambda z: B2.at[z])
         self.y2(g).wait_recv()
         self.add(lambda z: R.at[r,z,P.x,:,pl.ds(lo+a,n-a)],lambda z: B4.at[z])
-    def zstep(self,g,t):
-        lo,n,_=self.groups[g]; R=self.R; P=self.P; Z=P.Z; z=P.z
-        r=self.row(0)
-        def acc(zo,b):
-            d=R.at[r,zo,P.x,:,pl.ds(lo,n)]
-            d[...]=(d[...].astype(F32)+b[zo].astype(F32)).astype(BF)
+    def acc(self,g,zo,b):
+        lo,n,_=self.groups[g]
+        d=self.R.at[self.row(0),zo,self.P.x,:,pl.ds(lo,n)]
+        d[...]=d[...]+b[zo]
+    def zstep(self,g,h):
+        n=self.groups[g][1]; Z=self.P.Z; z=self.P.z
+        if h==0:
+            def first():
+                for zo in range(Z-1,0,-1): self.zc(g,0,zo,1).start()
+            def last():
+                for zo in range(Z-1): self.zc(g,1,zo,Z-2).start()
+            when(z==0,first); when(z==Z-1,last)
+            return
         def up():
-            zo=Z-1-t
-            @pl.when(z>0)
-            def _():
-                self.zc(g,0,zo,z).wait_recv()
-                acc(zo,self.buf(g,5,n))
+            zo=Z-1-h+z
+            self.zc(g,0,zo,z).wait_recv()
+            self.acc(g,zo,self.buf(g,5,n))
             self.zc(g,0,zo,z+1).start()
         def down():
-            zo=t
-            @pl.when(z<Z-1)
-            def _():
-                self.zc(g,1,zo,z).wait_recv()
-                acc(zo,self.buf(g,6,n))
+            zo=h-(Z-1)+z
+            self.zc(g,1,zo,z).wait_recv()
+            self.acc(g,zo,self.buf(g,6,n))
             self.zc(g,1,zo,z-1).start()
-        when(z<Z-1-t,up); when(z>t,down)
+        when(jnp.logical_and(z>=1,z<=h),up)
+        when(jnp.logical_and(z>=Z-1-h,z<=Z-2),down)
     def final(self,g,out):
         lo,n,_=self.groups[g]; P=self.P; Z=P.Z; z=P.z
         out[...]=self.R[self.row(0),z,P.x,:,pl.ds(lo,n)].astype(F32)
@@ -347,9 +351,9 @@
         for k in range(2):
             self.ccp(g,k).wait_send(); self.x1(g,k).wait_send()
         self.x2(g).wait_send(); self.y1(g).wait_send(); self.y2(g).wait_send()
-        for t in range(Z-1):
-            when(z<Z-1-t,lambda: self.zc(g,0,Z-1-t,z+1).wait_send())
-            when(z>t,lambda: self.zc(g,1,t,z-1).wait_send())
+        for zo in range(Z):
+            when(z<zo,lambda: self.zc(g,0,zo,z+1).wait_send())
+            when(z>zo,lambda: self.zc(g,1,zo,z-1).wait_send())
     def events(self,g,out):
         ev=[lambda: self.s_c(g),lambda: self.a_c(g),lambda: self.a_1(g),lambda: self.a_2(g)]
         for t in range(self.P.Z-1): ev.append(lambda t=t: self.zstep(g,t))
@@ -498,34 +502,54 @@
 
 RULES=((1,1,0),(2,3,1),(2,7,4))
 
+def places():
+    p=[("stat",i,0.6) for i in range(4)]
+    for i in range(3):
+        p.append(("third",i,0.6 if i else 2.0))
+        p+=[("qkv",4*i+k,0.42) for k in range(4)]
+        for pp in range(2): p+=[("af",4*i+2*pp+k,(1.2,2.4)[k]) for k in range(2)]
+    p.append(("out",0,0.6))
+    p+=[("ob",k,1.1) for k in range(4)]
+    for c in range(4):
+        p.append(("chunk",c,0.5))
+        p+=[("mr",4*c+k,1.75) for k in range(4)]
+        p+=[("mw",3*c+k,0.6+0.15*(k==2)) for k in range(3)]
+        p+=[("mu",3*c+k,0.6+0.2*(k==2)) for k in range(3)]
+        p.append(("mp",c,0.1))
+    p.append(("fin",0,1.0))
+    p+=[("bb",k,1.3) for k in range(4)]
+    p+=[("bw",k,0.6+0.2*(k==2)) for k in range(3)]
+    p.append(("bp",0,0.1))
+    p+=[("ag",k,0.5) for k in range(4)]
+    for i in range(3):
+        for pp in range(2): p+=[("ab",8*i+4*pp+k,1.0) for k in range(4)]
+        p+=[("dh",4*i+k,0.5) for k in range(4)]
+        if i==2: p+=[("ln",k,0.9) for k in range(4)]
+        p+=[("dq",3*i+k,0.6+0.2*(k==2)) for k in range(3)]
+        p.append(("dp",i,0.1))
+    return p
+
+def ready_places():
+    return [("mp",c) for c in range(4)]+[("mp",3)]*4+[("bp",0)]+[("dp",i) for i in range(3)]
+
+def due_places():
+    return [("third",0),("third",1),("out",0),("chunk",0),("chunk",1),("chunk",2)]
+
 class Clock:
-    def __init__(self, places):
-        self.times=places
+    def __init__(self, plan, ga, sc, own):
+        names=[p[:2] for p in places()]
+        index={p:i for i,p in enumerate(names)}
+        fns={}
+        for g in range(len(GATHER)):
+            for k,f in enumerate(ga.events(g)): fns[(0,g,k)]=f
+        for g,(lo,n,_) in enumerate(SCATTER):
+            for k,f in enumerate(sc.events(g,own.at[:,pl.ds(lo,n)])): fns[(1,g,k)]=f
+        check_plan(plan,set(fns),index)
         self.slots={}
         self.tail=[]
-    def fill(self, events, deadlines):
-        index={(n,s):i for i,(n,s,_) in enumerate(self.times)}
-        times=[t for _,_,t in self.times]
-        where={}
-        last=0
-        for time,key,fn in sorted(events,key=lambda e: e[0]):
-            i=next((i for i,t in enumerate(times) if t>=time),len(times))
-            where[key]=i
-        for key,place in deadlines.items():
-            where[key]=min(where[key],index[place])
-        keys=sorted(where,key=lambda k:(k[0],k[1],-k[2]))
-        prev=None
-        for k in keys:
-            if prev is not None and prev[:2]==k[:2]: where[k]=min(where[k],where[prev])
-            prev=k
-        fns={key:(time,fn) for time,key,fn in events}
-        self.where=where
-        self.order=[]
-        for key in sorted(where,key=lambda k:(where[k],fns[k][0],k)):
-            i=where[key]
-            self.order.append(key)
-            if i<len(times): self.slots.setdefault(self.times[i][:2],[]).append(fns[key][1])
-            else: self.tail.append(fns[key][1])
+        for i,*key in plan:
+            if i<len(names): self.slots.setdefault(names[i],[]).append(fns[tuple(key)])
+            else: self.tail.append(fns[tuple(key)])
     def at(self, name, step, count):
         for k in range(count):
             todo=self.slots.get((name,k))
@@ -536,40 +560,46 @@
                     if step==k: run()
                 else: pl.when(step==k)(run)
 
-def schedule(sched):
-    p=[]
-    t=[0.0]
-    def add(name,step,dt):
-        p.append((name,step,t[0])); t[0]+=dt
-    for i in range(4): add("stat",i,0.5)
-    t[0]=max(t[0],sched["first"])
-    for i in range(3):
-        add("third",i,0.6)
-        for k in range(4): add("qkv",4*i+k,0.4)
-        for pp in range(2):
-            for k in range(4): add("af",8*i+4*pp+k,(0.8,0.8,1.4,1.4)[k])
-    add("out",0,0.6)
-    for k in range(4): add("ob",k,1.0)
-    for c in range(4):
-        add("chunk",c,1.0)
-        for k in range(4): add("mr",4*c+k,1.35)
-        for k in range(3): add("mw",3*c+k,0.6)
-        for k in range(3): add("mu",3*c+k,0.6)
-        add("mp",c,0.3)
-    for k in range(4): add("bb",k,1.2)
-    for k in range(3): add("bw",k,0.6)
-    add("bp",0,0.3)
-    for i in range(3):
-        for pp in range(2):
-            for k in range(4): add("ab",8*i+4*pp+k,0.9)
-        for k in range(4): add("dh",4*i+k,0.5)
-        if i==2:
-            for k in range(4): add("ln",k,0.8)
-        for k in range(3): add("dq",3*i+k,0.6)
-        add("dp",i,0.3)
-    return p
-
-def mega_kernel(Z,sched,tok_h,cot_h,len_ref,wqkv_s,wout_s,wup_s,wdown_s,vec_s,
+PLAN = (
+    (0, 0, 0, 0), (2, 0, 0, 1), (3, 0, 1, 0), (3, 0, 0, 2), (4, 0, 0, 3), (4, 0, 0, 4), (4, 0, 1, 1), (4, 0, 0, 5),
+    (4, 0, 0, 6), (4, 0, 1, 2), (4, 0, 1, 3), (4, 0, 0, 7), (4, 0, 0, 8), (4, 0, 1, 4), (4, 0, 2, 0), (4, 0, 0, 9),
+    (4, 0, 1, 5), (5, 0, 1, 6), (10, 0, 2, 1), (10, 0, 1, 7), (11, 0, 1, 8), (12, 0, 2, 2), (12, 0, 2, 3),
+    (13, 0, 1, 9), (20, 0, 2, 4), (20, 0, 2, 5), (24, 0, 4, 0), (24, 0, 2, 6), (27, 0, 4, 1), (28, 0, 2, 7),
+    (28, 0, 3, 0), (29, 0, 3, 1), (30, 0, 3, 2), (30, 0, 3, 3), (30, 0, 2, 8), (30, 0, 4, 2), (30, 0, 3, 4),
+    (30, 0, 3, 5), (30, 0, 4, 3), (30, 0, 4, 4), (30, 0, 3, 6), (30, 0, 4, 5), (30, 0, 5, 0), (31, 0, 3, 7),
+    (31, 0, 2, 9), (31, 0, 5, 1), (32, 0, 3, 8), (33, 0, 4, 6), (34, 0, 5, 2), (35, 0, 4, 7), (36, 0, 3, 9),
+    (39, 0, 5, 3), (40, 0, 4, 8), (41, 0, 5, 4), (42, 0, 4, 9), (43, 0, 5, 5), (47, 1, 0, 0), (49, 0, 5, 6),
+    (49, 0, 5, 7), (50, 1, 0, 1), (53, 1, 0, 2), (54, 0, 5, 8), (58, 1, 0, 3), (59, 1, 1, 0), (60, 0, 5, 9),
+    (61, 1, 0, 4), (63, 1, 1, 1), (66, 1, 0, 5), (67, 1, 1, 2), (70, 1, 0, 6), (72, 1, 2, 0), (72, 1, 1, 3),
+    (72, 1, 1, 4), (74, 1, 2, 1), (75, 1, 1, 5), (76, 1, 0, 7), (78, 1, 2, 2), (81, 1, 2, 3), (81, 1, 2, 4),
+    (82, 1, 1, 6), (83, 1, 3, 0), (86, 1, 2, 5), (87, 1, 3, 1), (87, 1, 4, 0), (88, 1, 2, 6), (88, 1, 1, 7),
+    (89, 1, 4, 1), (90, 1, 5, 0), (90, 1, 2, 7), (94, 1, 3, 2), (97, 1, 4, 2), (99, 1, 3, 3), (100, 1, 3, 4),
+    (100, 1, 4, 3), (100, 1, 5, 1), (101, 1, 6, 0), (103, 1, 3, 5), (103, 1, 6, 1), (103, 1, 7, 0), (103, 1, 4, 4),
+    (105, 1, 5, 2), (107, 1, 3, 6), (108, 1, 4, 5), (109, 1, 6, 2), (110, 1, 5, 3), (110, 1, 7, 1), (110, 1, 8, 0),
+    (111, 1, 4, 6), (112, 1, 3, 7), (112, 1, 5, 4), (113, 1, 6, 3), (113, 1, 8, 1), (114, 1, 4, 7), (114, 1, 6, 4),
+    (115, 1, 5, 5), (115, 1, 9, 0), (116, 1, 7, 2), (116, 1, 6, 5), (117, 1, 5, 6), (119, 1, 6, 6), (120, 1, 8, 2),
+    (120, 1, 7, 3), (121, 1, 9, 1), (122, 1, 5, 7), (122, 1, 7, 4), (124, 1, 8, 3), (125, 1, 7, 5), (126, 1, 6, 7),
+    (126, 1, 8, 4), (128, 1, 10, 0), (128, 1, 9, 2), (128, 1, 8, 5), (130, 1, 7, 6), (131, 1, 8, 6),
+    (131, 1, 10, 1), (132, 1, 7, 7), (134, 1, 10, 2), (134, 1, 8, 7), (137, 1, 9, 3), (137, 1, 9, 4),
+    (139, 1, 9, 5), (141, 1, 10, 3), (143, 1, 9, 6), (148, 1, 11, 0), (148, 1, 10, 4), (148, 1, 10, 5),
+    (148, 1, 10, 6), (148, 1, 9, 7), (149, 1, 11, 1), (149, 1, 10, 7), (149, 1, 11, 2), (149, 1, 11, 3),
+    (149, 1, 11, 4), (149, 1, 11, 5), (149, 1, 11, 6), (149, 1, 11, 7),
+)
+
+def check_plan(plan, keys, index):
+    pos={tuple(e[1:]):(e[0],j) for j,e in enumerate(plan)}
+    assert set(pos)==keys and len(plan)==len(keys)
+    assert all(a[0]<=b[0] for a,b in zip(plan,plan[1:]))
+    last={0:9,1:7}
+    for kind,g,k in keys:
+        if k: assert pos[(kind,g,k-1)]<pos[(kind,g,k)]
+    for g,p in enumerate(due_places()): assert pos[(0,g,9)][0]<=index[p]
+    for g,p in enumerate(ready_places()):
+        assert pos[(1,g,0)][0]>=index[p]
+        for n,i,j in RULES:
+            if g>=n: assert pos[(1,g-n,i)]<pos[(1,g,j)]
+
+def mega_kernel(Z,plan,tok_h,cot_h,len_ref,wqkv_s,wout_s,wup_s,wdown_s,vec_s,
                mixed_o,dtok_o,own_o,nrm_o,
                G,tok,cot,F1,F2,F3,qkv,B1,B2,B3,hT,aT,oT,W0,W1,dW,lse,V,V1,dV1,dka,dva,own,nrm,dsem,*rest):
     gsems=rest[:8]; rbufs=rest[8:8+NB]; rsems=rest[8+NB:16+NB]; nb,got,ns,nr=rest[16+NB:]
@@ -583,43 +613,7 @@
     enter_all(place,Z)
     ga=Gather(place,G,GATHER,gsems)
     sc=Scatter(place,G,SCATTER,rbufs,rsems)
-    clock=Clock(schedule(sched))
-    events=[]; deadlines={}
-    w=0.0
-    for g,(lo,n,_) in enumerate(GATHER):
-        d=sched["link"]*n/COLS
-        ev=ga.events(g)
-        for k,f in enumerate(ev):
-            if k==0: time=max(0.0,w-sched["ahead"])
-            else: time=w+sched["lat"]+d*min(k,len(ev)-2)/(len(ev)-2)+(sched["sib"] if k==len(ev)-1 else 0.0)
-            events.append((time,("g",g,k),f))
-        w+=d
-    for g,place_ in enumerate((("third",0),("third",1),("out",0),("chunk",0),("chunk",1),("chunk",2))):
-        deadlines[("g",g,9)]=place_
-    tm={(n,s):t for n,s,t in clock.times}
-    ready=[tm[("mp",c)] for c in range(4)]+[tm[("mp",3)]+sched["dgap"]*(k+1) for k in range(4)]+[tm[("bp",0)]]+[tm[("dp",i)] for i in range(3)]
-    rt=sched["rs"]
-    at_=[]
-    for g,(lo,n,_) in enumerate(SCATTER):
-        ev=sc.events(g,own.at[:,pl.ds(lo,n)])
-        at_.append([])
-        t=ready[g]
-        for k,f in enumerate(ev):
-            t=t+rt[k]
-            if g: t=max(t,at_[g-1][k]+0.01)
-            for back_,slot,first in RULES:
-                if k==first and g>=back_: t=max(t,at_[g-back_][slot]+0.01)
-            at_[g].append(t)
-            events.append((t,("s",g,k),f))
-    clock.fill(events,deadlines)
-    index={(n,s):i for i,(n,s,_) in enumerate(clock.times)}
-    after=[("mp",c) for c in range(4)]+[("mp",3)]*4+[("bp",0)]+[("dp",i) for i in range(3)]
-    for g in range(len(SCATTER)): assert clock.where[("s",g,0)]>=index[after[g]]
-    pos={k:i for i,k in enumerate(clock.order)}
-    for g in range(len(SCATTER)):
-        for back_,slot,first in RULES:
-            if g>=back_: assert pos[("s",g-back_,slot)]<pos[("s",g,first)]
-        for k in range(1,8): assert pos[("s",g,k-1)]<pos[("s",g,k)]
+    clock=Clock(plan,ga,sc,own)
     def at(name,step,count): clock.at(name,step,count)
     def rows(i): return pl.ds(al(i*RB,RB),RB)
     length=len_ref[0]
@@ -650,7 +644,7 @@
             def col(j): return qkv.at[s,:,pl.ds(al(256*j+128*pp,128),128)]
             c=pl.ds(al(128*p,128),128)
             attn_fwd_pair(col(0),col(1),col(2),length,o.at[:,c],oT.at[c,:],lse.at[p],512,
-                          tick=lambda k: at("af",8*i+4*pp+k,24))
+                          tick=lambda k: at("af",4*i+2*pp+k,12))
             return 0
         lax.fori_loop(0,2,pair,0)
         return 0
@@ -710,6 +704,7 @@
         at("mp",c,4)
         return 0
     lax.fori_loop(0,FF//W3,chunk,0)
+    at("fin",0,1)
     mixed_b=B2
     def fin(i,_):
         mixed_b[rows(i),:]=mixed[rows(i),:].astype(BF)
@@ -744,6 +739,7 @@
     h1T=hT; dqkv=B3; dh1=F2
     outs[0].wait()
     def again(i,_):
+        at("ag",i,4)
         sl=rows(i)
         hb=(norm_parts(tok[sl,:].astype(F32))[0]*V1[:,0:D]+V1[:,D:2*D]).astype(BF)
         h1T[:,sl]=hb.T
@@ -797,23 +793,24 @@
     left=own[:,pl.ds(0,VEC_AT)]; right=own[:,pl.ds(OUT_AT,COLS-OUT_AT)]
     nb[0]=jnp.full((8,128),1.0,F32)*(jnp.sum(left*left)+jnp.sum(right*right)+jnp.sum(vec*vec))
     outs.append(dma(own,own_o,4))
-    nrm[...]=all_sum(place,nb,got,ns,nr)
+    nrm[8:24,:]=vec
+    nrm[0:8,:]=all_sum(place,nb,got,ns,nr)
     outs.append(dma(nrm,nrm_o,5))
     for g in range(len(SCATTER)): sc.drain(g)
     for cp in outs: cp.wait()
 
-SCHED=dict(first=14.0,link=57.0,ahead=4.0,lat=4.0,sib=2.0,dgap=1.5,rs=[0,1.8,4.5,3.0,1.5,2.0,2.0,2.0])
-def mega_call(Z,tok,cot,length,wqkv,wout,wup,wdown,vec,sched=SCHED):
+def mega_call(Z,tok,cot,length,wqkv,wout,wup,wdown,vec,plan=None):
+    plan=PLAN if plan is None else plan
     L=tok.shape[0]; pieces=8*Z
     S=jax.ShapeDtypeStruct; V=pltpu.VMEM
-    vm=pl.BlockSpec(memory_space=pltpu.VMEM); an=pl.BlockSpec(memory_space=pl.ANY); sm=pl.BlockSpec(memory_space=pltpu.SMEM)
-    outs=[S((L,D),BF),S((L,D),F32),S((16,COLS),F32),S((8,128),F32)]
+    vm=pl.BlockSpec(memory_space=pltpu.VMEM); an=pl.BlockSpec(memory_space=pltpu.HBM); sm=pl.BlockSpec(memory_space=pltpu.SMEM)
+    outs=[S((L,D),BF),S((L,D),F32),S((16,COLS),F32),S((24,128),F32)]
     f=lambda: V((L,D),F32)
     b=lambda: V((L,D),BF)
     scratch=[V((4,Z,2,16,COLS),BF),b(),b(),f(),f(),f(),V((3,L,D),BF),b(),b(),b(),V((D,L),BF),V((D,L),BF),V((D,L),F32),
              V((D,W3),BF),V((W3,D),BF),V((D,W3),F32),V((6,2,L),F32),V((80,128),F32),V((1,10*D),F32),V((1,10*D),F32),
-             V((L,128),F32),V((L,128),F32),V((16,COLS),F32),V((8,128),F32),pltpu.SemaphoreType.DMA((6,))]
-    return pl.pallas_call(functools.partial(mega_kernel,Z,sched),out_shape=outs,
+             V((L,128),F32),V((L,128),F32),V((16,COLS),F32),V((24,128),F32),pltpu.SemaphoreType.DMA((6,))]
+    return pl.pallas_call(functools.partial(mega_kernel,Z,plan),out_shape=outs,
         in_specs=[an,an,sm]+[vm]*5,out_specs=[an]*len(outs),
         scratch_shapes=scratch+gather_sems(len(GATHER),Z)+rs_bufs(Z)+rs_sems(len(SCATTER),Z)+norm_bufs(Z)+norm_sems(Z),
         compiler_params=pltpu.CompilerParams(collective_id=1,has_side_effects=True,vmem_limit_bytes=63*2**20),
@@ -831,8 +828,28 @@
     return (weight - step_rate * update, first_new, second_new)
 
 
-def adam_kernel(par_ref, own, nrm, *refs):
-    ins, outs = refs[:12], refs[12:]
+def adam_kernel(par_ref, own_h, nrm_h, mixed_h, dtok_h, *refs):
+    ins_h, outs_h = refs[:12], refs[12:24]
+    own, nrm, *rest = refs[26:]
+    ins, outs, mixed, dtok, sem = rest[:12], rest[12:24], rest[24], rest[25], rest[26]
+    pairs = list(zip((own_h, nrm_h) + tuple(ins_h), (own, nrm) + tuple(ins)))
+    loads = [pltpu.make_async_copy(a, b, sem.at[i]) for i, (a, b) in enumerate(pairs)]
+    moves = [
+        pltpu.make_async_copy(mixed_h, mixed, sem.at[14]),
+        pltpu.make_async_copy(dtok_h, dtok, sem.at[15]),
+    ]
+    for cp in loads + moves:
+        cp.start()
+    for cp in loads:
+        cp.wait()
+    for cp in moves:
+        cp.wait()
+    moves = [
+        pltpu.make_async_copy(mixed, refs[24], sem.at[14]),
+        pltpu.make_async_copy(dtok, refs[25], sem.at[15]),
+    ]
+    for cp in moves:
+        cp.start()
     factor = jnp.minimum(1.0, CLIP_NORM / (jnp.sqrt(nrm[0:1, 0:1]) + 1e-06))
     main_at = al(8 * par_ref[0], 8)
     rest_at = al(16 * (1 - par_ref[0]), 8)
@@ -864,21 +881,30 @@
     for r in range(6):
         grad = own[:, pl.ds(DOWN_AT + r * D, D)]
         step(3, pl.ds(16 * r, 16), slice(None), grad, FF ** (-0.5))
-
-
-def adam_call(parity, own, nrm, states):
-    vm = pl.BlockSpec(memory_space=pltpu.VMEM)
+    stores = [pltpu.make_async_copy(a, b, sem.at[i]) for i, (a, b) in enumerate(zip(outs, outs_h))]
+    for cp in stores:
+        cp.start()
+    for cp in stores + moves:
+        cp.wait()
+
+
+def adam_call(parity, own, nrm, mixed, d_tokens, states):
+    hb = pl.BlockSpec(memory_space=pltpu.HBM)
     sm = pl.BlockSpec(memory_space=pltpu.SMEM)
+    held = [pltpu.VMEM(a.shape, F32) for a in (own, nrm) + tuple(states) + tuple(states)]
     return pl.pallas_call(
         adam_kernel,
-        out_shape=[jax.ShapeDtypeStruct(a.shape, F32) for a in states],
-        in_specs=[sm, vm, vm] + [vm] * 12,
-        out_specs=[vm] * 12,
-        compiler_params=pltpu.CompilerParams(vmem_limit_bytes=40 * 2**20),
+        out_shape=[jax.ShapeDtypeStruct(a.shape, a.dtype) for a in states + (mixed, d_tokens)],
+        in_specs=[sm] + [hb] * 16,
+        out_specs=[hb] * 14,
+        scratch_shapes=held
+        + [pltpu.VMEM(mixed.shape, BF), pltpu.VMEM(d_tokens.shape, F32)]
+        + [pltpu.SemaphoreType.DMA((16,))],
+        compiler_params=pltpu.CompilerParams(vmem_limit_bytes=63 * 2**20),
         cost_estimate=pl.CostEstimate(
             flops=10**7, bytes_accessed=8 * 2**20, transcendentals=10**6
         ),
-    )(parity, own, nrm, *states)
+    )(parity, own, nrm, mixed, d_tokens, *states)
 
 
 def layer_norm(values, gain, shift):
@@ -975,14 +1001,14 @@
     vec = lax.dynamic_update_slice(
         jnp.zeros((16 * VEC_COLS,), BF), packed.astype(BF), (start,)
     ).reshape(16, VEC_COLS)
-    mixed, d_tokens, own, norm_tile = mega_call(
+    mixed, d_tokens, own, small = mega_call(
         Z, tokens[0], cotangent[0], lengths, state[0], state[3], state[6], state[9], vec
     )
-    grad_norm = jnp.sqrt(norm_tile[0, 0])
+    grad_norm = jnp.sqrt(small[0, 0])
     factor = jnp.minimum(1.0, CLIP_NORM / (grad_norm + 1e-06))
     parity = (fsdp % 2).astype(jnp.int32).reshape(1)
-    new = adam_call(parity, own, norm_tile, state[:12])
-    g_vec = lax.dynamic_slice(own[:, VEC_AT:OUT_AT].reshape(-1), (start,), (n,))
+    *new, mixed, d_tokens = adam_call(parity, own, small, mixed, d_tokens, state[:12])
+    g_vec = lax.dynamic_slice(small[8:].reshape(-1), (start,), (n,))
     new_vec = adam_step(packed, m_packed, v_packed, g_vec * factor, VECTOR_RATE)
     return (mixed[None], d_tokens[None], grad_norm) + tuple(new) + new_vec
 

time: 323 us -> 237 us (0.73)
  Pallas kernels: 302 us -> 231 us
  local copies, waits for them, and re-layouts: 16.1 us -> 0.73 us
    pallas_call x2, Pallas kernels: 302 us -> 231 us  [the longest x1 224 us: mega_call(): pl.pallas_call(functools.partial(mega_kernel, Z, plan), out_shape=outs, i...]
    unnamed x42 -> x10, local copies, waits for them, and re-layouts: 14 us -> 0.03 us
where the time goes in v1:
time: 237 us; the launch traced here: 236 us
  Pallas kernels  231 us (97%)
  between operations  3.3 us (1%)
    pallas_call x1, Pallas kernels, mega_call(): pl.pallas_call(functools.partial(mega_kernel, Z, plan), out_shape=outs, i...  224 us
    pallas_call x1, Pallas kernels, adam_call(): pl.pallas_call(adam_kernel, out_shape=[jax.ShapeDtypeStruct(a.shape, a.dt...  6.65 us

profile of v1, /device:TPU:0, one launch (start us, length us, event | category | flops | bytes accessed | tf_op | source)
XLA Modules:
  0.0 236.4 jit_solution(1901894177381298502)
XLA Ops:
  0.7 0.7 convert_element_type.3
  1.4 0.2 dynamic_update_slice.3
  1.5 0.0 copy-start.1
  2.2 0.0 copy-done.1
  2.2 224.4 %shard_map.313 = (bf16[1024,768]{1,0:T(8,128)(2,1)}, f32[1024,768]{1,0:T(8,128)}, f32[16,13952]{1,0:T(8,128)}, f32[24,128]{1,0:T(8,128)}) custom-call(bf16[1024,768]{1,0:T(8,128)(2,1)} %bitcast.11, bf16[1024,768]{1,0:T(8,128)(2,1)} %bitcast.12, s32[1]{0:T(128)S(6)} %copy.37.len_ref, f32[24,2304]{1,0:T(8,128)} %refs_0_.1, f32[24,768]{1,0:T(8,128)} %refs_3_.1, ...), custom_call_target="tpu_custom_call" | custom-call | flops 60000002048 | bytes 62914560 | tf_op jit(solution)/shard_map/pallas_call | solution.py:813
  226.6 0.0 copy-start
  226.6 0.0 copy-start.2
  226.6 0.0 copy-start.3
  226.6 0.0 copy-start.4
  226.7 6.6 %shard_map.314 = (f32[24,2304]{1,0:T(8,128)}, f32[24,2304]{1,0:T(8,128)}, f32[24,2304]{1,0:T(8,128)}, f32[24,768]{1,0:T(8,128)}, f32[24,768]{1,0:T(8,128)}, /*in...) custom-call(s32[1]{0:T(128)} %bitcast.par_ref, ...), custom_call_target="tpu_custom_call" | custom-call | flops 10000000 | bytes 8388608 | tf_op jit(solution)/shard_map/pallas_call | solution.py:895
  233.3 0.0 copy-done
  233.3 0.5 slice.6
  234.6 0.0 copy-done.2
  234.6 0.0 copy-done.3
  234.6 0.0 copy-done.4
  234.6 0.7 multiply_subtract_fusion
  (2 shorter events, 0.0 us)
Async XLA Ops:
  1.5 0.7 copy-start.1
  226.6 6.7 %copy-start = (f32[24,128]{1,0:T(8,128)S(1)}, f32[24,128]{1,0:T(8,128)}, u32[]{:S(2)}) copy-start(f32[24,128]{1,0:T(8,128)} %get-tuple-element.37.nrm_h) | copy-start | bytes 36868
  226.6 8.0 %copy-start.2 = (f32[240]{0:T(256)S(1)}, f32[240]{0:T(256)}, u32[]{:S(2)}) copy-start(f32[240]{0:T(256)} %param.33) | copy-start | bytes 2884
  226.6 8.0 %copy-start.3 = (f32[240]{0:T(256)S(1)}, f32[240]{0:T(256)}, u32[]{:S(2)}) copy-start(f32[240]{0:T(256)} %param.34) | copy-start | bytes 2884
  226.6 8.0 %copy-start.4 = (f32[240]{0:T(256)S(1)}, f32[240]{0:T(256)}, u32[]{:S(2)}) copy-start(f32[240]{0:T(256)} %param.35) | copy-start | bytes 2884

commit v2 on v1

--- a/solution.py
+++ b/solution.py
@@ -34,63 +34,74 @@
     m=head_mask(x.shape[0]); m = m if h==0 else jnp.logical_not(m)
     return jnp.where(m,x*jnp.asarray(scale,x.dtype),jnp.zeros_like(x))
 
-def attn_fwd_pair(q_ref,k_ref,v_ref,length,o_ref,oT_ref,lse_ref,QB,tick=None):
+def attn_fwd_pair(q_ref,k_ref,v_ref,length,o_ref,oT_ref,lse_ref,QB):
     L=q_ref.shape[0]
+    n=L//QB
     vT=v_ref[...].T
-    for i in range(L//QB):
+    lane=lax.broadcasted_iota(jnp.int32,(L,128),1)
+    dead=jnp.where(lax.broadcasted_iota(jnp.int32,(L,128),0)<length,0.0,-1e9).astype(BF)
+    keys=[jnp.where(lane==HD-HD*h,dead,k_ref[...]) for h in range(2)]
+    ql=lax.broadcasted_iota(jnp.int32,(QB,128),1)
+    tri=lax.broadcasted_iota(jnp.int32,(QB,QB),0)<=lax.broadcasted_iota(jnp.int32,(QB,QB),1)
+    def scores(i,h):
+        qh=jnp.where(ql==HD-HD*h,jnp.ones((),BF),half(q_ref[pl.ds(i*QB,QB),:],h,0.125))
+        return nt(keys[h][:(i+1)*QB],qh)
+    jobs=[(i,h) for i in range(n) for h in range(2)]
+    now=scores(*jobs[0])
+    outs=[]
+    for x,(i,h) in enumerate(jobs):
+        later=scores(*jobs[x+1]) if x+1<len(jobs) else None
         nk=(i+1)*QB
-        qs=q_ref[pl.ds(i*QB,QB),:]
-        if tick is not None: tick(i)
-        outs=[]
-        jidx=lax.broadcasted_iota(jnp.int32,(nk,QB),0)
-        lim=jnp.minimum(i*QB+1+lax.broadcasted_iota(jnp.int32,(1,QB),1),length)
-        for h in range(2):
-            s=nt(k_ref[pl.ds(0,nk),:],half(qs,h,0.125))
-            s=jnp.where(jidx<lim,s,-1e9)
-            m=jnp.max(s,0,keepdims=True)
-            e=jnp.exp(s-m)
-            l=jnp.sum(e,0,keepdims=True)
-            oT=nn(vT[HD*h:HD*h+HD,:nk],e.astype(BF))
-            outs.append(oT/l)
-            lse_ref[pl.ds(h,1),pl.ds(i*QB,QB)]=m+jnp.log(l)
-        oT=jnp.concatenate(outs,0)
-        oT_ref[:,pl.ds(i*QB,QB)]=oT
-        o_ref[pl.ds(i*QB,QB),:]=oT.T.astype(BF)
+        s=jnp.where(tri,now[nk-QB:],-1e9)
+        if i: s=jnp.concatenate([now[:nk-QB],s],0)
+        m=jnp.max(s,0,keepdims=True)
+        e=jnp.exp(s-m)
+        l=jnp.sum(e,0,keepdims=True)
+        outs.append(nn(vT[HD*h:HD*h+HD,:nk],e.astype(BF))/l)
+        lse_ref[pl.ds(h,1),pl.ds(i*QB,QB)]=m+jnp.log(l)
+        if h==1:
+            oT=jnp.concatenate(outs,0); outs=[]
+            oT_ref[:,pl.ds(i*QB,QB)]=oT
+            o_ref[pl.ds(i*QB,QB),:]=oT.T.astype(BF)
+        now=later
 
 def attn_bwd_pair(q_ref,k_ref,v_ref,do_ref,oT_ref,lse_ref,length,dq_ref,dk_ref,dv_ref,dk_acc,dv_acc,QB,tick=None):
     L=q_ref.shape[0]
+    n=L//QB
     kT=k_ref[...].T
-    for i in reversed(range(L//QB)):
-        if tick is not None: tick(L//QB-1-i)
-        nk=(i+1)*QB
-        sl=pl.ds(i*QB,QB)
-        qs=q_ref[sl,:]; do=do_ref[sl,:]
-        doT=do.astype(F32).T
-        prod=doT*oT_ref[:,sl]
+    jobs=list(reversed(range(n)))
+    tri=lax.broadcasted_iota(jnp.int32,(QB,2*QB),0)<=lax.rem(lax.broadcasted_iota(jnp.int32,(QB,2*QB),1),QB)
+    def products(i):
+        nk=(i+1)*QB; sl=pl.ds(i*QB,QB)
+        q=q_ref[sl,:]; do=do_ref[sl,:]
+        qm=jnp.concatenate([half(q,0,0.125),half(q,1,0.125)],0)
+        dom=jnp.concatenate([half(do,0),half(do,1)],0)
+        return nt(k_ref[pl.ds(0,nk),:],qm),nt(v_ref[pl.ds(0,nk),:],dom),qm,dom
+    now=products(jobs[0])
+    for x,i in enumerate(jobs):
+        split=tick is not None and x==1
+        later=products(jobs[x+1]) if x+1<n and not (tick is not None and x==0) else None
+        if split:
+            tick(1)
+            now=products(i)
+        nk=(i+1)*QB; sl=pl.ds(i*QB,QB)
+        s,dp,qm,dom=now
+        prod=do_ref[sl,:].astype(F32).T*oT_ref[:,sl]
+        delta=jnp.concatenate([jnp.sum(prod[:HD],0,keepdims=True),jnp.sum(prod[HD:],0,keepdims=True)],1)
         live=(i*QB+lax.broadcasted_iota(jnp.int32,(1,QB),1))<length
-        tri=lax.broadcasted_iota(jnp.int32,(QB,QB),0)<=lax.broadcasted_iota(jnp.int32,(QB,QB),1)
-        dqs=[]
-        k=k_ref[pl.ds(0,nk),:]; v=v_ref[pl.ds(0,nk),:]
-        dk=None; dv=None
-        for h in range(2):
-            delta=jnp.sum(prod[HD*h:HD*h+HD],0,keepdims=True)
-            lse=jnp.where(live,lse_ref[pl.ds(h,1),sl],1e30)
-            qm=half(qs,h,0.125); dom=half(do,h)
-            s=nt(k,qm)
-            p=jnp.exp(s-lse)
-            pd=jnp.where(tri,p[nk-QB:],0.0)
-            p=pd if i==0 else jnp.concatenate([p[:nk-QB],pd],0)
-            dp=nt(v,dom)
-            ds=(p*(dp-delta)).astype(BF)
-            a=nn(p.astype(BF),dom); b=nn(ds,qm)
-            dv=a if dv is None else dv+a
-            dk=b if dk is None else dk+b
-            dqs.append(nn(kT[HD*h:HD*h+HD,:nk],ds))
-        dq_ref[sl,:]=(jnp.concatenate(dqs,0)*0.125).T.astype(BF)
-        if i==L//QB-1:
+        lse=jnp.concatenate([jnp.where(live,lse_ref[pl.ds(h,1),sl],1e30) for h in range(2)],1)
+        p=jnp.exp(s-lse)
+        pd=jnp.where(tri,p[nk-QB:],0.0)
+        p=pd if i==0 else jnp.concatenate([p[:nk-QB],pd],0)
+        ds=(p*(dp-delta)).astype(BF)
+        dv=nn(p.astype(BF),dom); dk=nn(ds,qm)
+        dq=[nn(kT[HD*h:HD*h+HD,:nk],ds[:,QB*h:QB*h+QB]) for h in range(2)]
+        dq_ref[sl,:]=(jnp.concatenate(dq,0)*0.125).T.astype(BF)
+        if i==n-1:
             dk_acc[...]=dk; dv_acc[...]=dv
         else:
             dk_acc[pl.ds(0,nk),:]+=dk; dv_acc[pl.ds(0,nk),:]+=dv
+        now=later
     dk_ref[...]=dk_acc[...].astype(BF); dv_ref[...]=dv_acc[...].astype(BF)
 
 def fwd_call(qkv,length,QB=256):
@@ -195,7 +206,7 @@
             if t+1<Z-1:
                 when(z>0,lambda: self.zcp(g,1,t+1,zo,z-1).start())
             self.xfull(g,zo).start(); self.yfull(g,zo).start()
-        when(z-1-t>=0,below); when(z+1+t<Z,above)
+        when(z>t,below); when(z<Z-1-t,above)
     def _diag(self,g,zo):
         self.xfull(g,zo,1).wait_recv(); self.ydiag(g,zo).start()
         self.yfull(g,zo,1).wait_recv(); self.xdiag(g,zo).start()
@@ -203,8 +214,8 @@
         z=self.P.z; Z=self.P.Z
         if t==0: self._diag(g,z)
         else:
-            when(z-t>=0,lambda: self._diag(g,z-t))
-            when(z+t<Z,lambda: self._diag(g,z+t))
+            when(z>=t,lambda: self._diag(g,z-t))
+            when(z<Z-t,lambda: self._diag(g,z+t))
     def corner(self,g):
         self.ccp(g,0).start()
         for zo in range(self.P.Z):
@@ -219,8 +230,8 @@
             self.xdiag(g,zo).wait_send(); self.ydiag(g,zo).wait_send()
         for k in range(2): self.ccp(g,k).wait_send()
         for t in range(Z-1):
-            when(jnp.logical_and(z<Z-1,z-t>=0),lambda: self.zcp(g,0,t,z-t,z+1).wait_send())
-            when(jnp.logical_and(z>0,z+t<=Z-1),lambda: self.zcp(g,1,t,z+t,z-1).wait_send())
+            when(jnp.logical_and(z<Z-1,z>=t),lambda: self.zcp(g,0,t,z-t,z+1).wait_send())
+            when(jnp.logical_and(z>0,z<=Z-1-t),lambda: self.zcp(g,1,t,z+t,z-1).wait_send())
     def events(self,g):
         Z=self.P.Z
         ev=[lambda: self.own(g)]
@@ -233,24 +244,26 @@
         return ev
 
 
-SLOT = 1280
-NB=7
+SLOT = 1152
+NB=12
 def rs_sems(NG,Z):
     D=pltpu.SemaphoreType.DMA
     return [D((NG*2,)),D((NG*2,)),
             D((NG*3,)),D((NG*3,)),
             D((NG*2,)),D((NG*2,)),
-            D((NG*2*Z,)),D((NG*2*Z,))]
+            D((NG*Z,)),D((NG*Z,))]
 def rs_bufs(Z):
     V=lambda *s: pltpu.VMEM(s,BF)
     h=640
-    return [V(2,2,Z,2,16,SLOT),V(2,Z,2,16,h),V(2,Z,16,h),V(2,2,Z,16,h),V(2,Z,16,h),V(4,Z,16,SLOT),V(4,Z,16,SLOT)]
+    v=128
+    return [V(2,2,Z,2,16,SLOT),V(2,Z,2,16,h),V(2,Z,16,h),V(2,2,Z,16,h),V(2,Z,16,h),V(4,Z,16,SLOT),
+            V(1,2,Z,2,16,v),V(1,Z,2,16,v),V(1,Z,16,v),V(1,2,Z,16,v),V(1,Z,16,v),V(1,Z,16,v)]
 class Scatter:
     def __init__(self,P,R,groups,bufs,sems):
         self.P=P; self.R=R; self.groups=groups; self.bufs=bufs
         self.cs,self.cr,self.xs,self.xr,self.ys,self.yr,self.zs,self.zr=sems
     def buf(self,g,i,w):
-        b=self.bufs[i]
+        b=self.bufs[i+(NB//2 if g==len(self.groups)-1 else 0)]
         b=b.at[g%b.shape[0]]
         nd=len(b.shape)
         return b.at[(slice(None),)*(nd-1)+(pl.ds(0,w),)]
@@ -279,9 +292,10 @@
     def y2(self,g):
         lo,n,a=self.groups[g]
         return rcopy(self.R.at[self.row(1),:,self.P.x,:,pl.ds(lo+a,n-a)],self.buf(g,4,n-a),self.ys.at[g*2+1],self.yr.at[g*2+1],self.P.ny)
-    def zc(self,g,d,zo,to):
-        lo,n,_=self.groups[g]; i=(g*2+d)*self.P.Z+zo
-        return rcopy(self.R.at[self.row(0),zo,self.P.x,:,pl.ds(lo,n)],self.buf(g,5+d,n).at[zo],self.zs.at[i],self.zr.at[i],self.P.nz(to))
+    def zc(self,g,src,to):
+        lo,n,_=self.groups[g]; Z=self.P.Z
+        return rcopy(self.R.at[self.row(0),to,self.P.x,:,pl.ds(lo,n)],self.buf(g,5,n).at[src],self.zs.at[g*Z+to],self.zr.at[g*Z+src],self.P.nz(to))
+    def both(self,g): return self.groups[g][1]>self.groups[g][2]
     def s_c(self,g):
         self.ccp(g,1).start(); self.ccp(g,0).start()
     def a_c(self,g):
@@ -290,105 +304,93 @@
             self.ccp(g,k).wait_recv()
             r=self.row(k)
             self.add(lambda z: R.at[r,z,:,:,pl.ds(lo,n)],lambda z: b.at[k,z])
-            self.x1(g,k).start()
+            if self.both(g): self.x1(g,k).start()
             if k==1: self.y1(g).start()
     def a_1(self,g):
-        lo,n,a=self.groups[g]; R=self.R; P=self.P; B1=self.buf(g,1,a); B3=self.buf(g,3,n-a)
+        lo,n,a=self.groups[g]; R=self.R; P=self.P; B1=self.buf(g,1,a)
         self.y1(g).wait_recv()
         r=self.row(0)
         self.add(lambda z: R.at[r,z,:,:,pl.ds(lo,a)],lambda z: B1.at[z])
-        for k in (1,0):
-            self.x1(g,k).wait_recv()
-            q=self.row(k)
-            self.add(lambda z: R.at[q,z,P.x,:,pl.ds(lo+a,n-a)],lambda z: B3.at[k,z])
+        if self.both(g):
+            B3=self.buf(g,3,n-a)
+            for k in (1,0):
+                self.x1(g,k).wait_recv()
+                q=self.row(k)
+                self.add(lambda z: R.at[q,z,P.x,:,pl.ds(lo+a,n-a)],lambda z: B3.at[k,z])
+            self.y2(g).start()
         self.x2(g).start()
-        self.y2(g).start()
     def a_2(self,g):
-        lo,n,a=self.groups[g]; R=self.R; P=self.P; B2=self.buf(g,2,a); B4=self.buf(g,4,n-a)
+        lo,n,a=self.groups[g]; R=self.R; P=self.P; Z=P.Z; B2=self.buf(g,2,a)
         r=self.row(0)
         self.x2(g).wait_recv()
         self.add(lambda z: R.at[r,z,P.x,:,pl.ds(lo,a)],lambda z: B2.at[z])
-        self.y2(g).wait_recv()
-        self.add(lambda z: R.at[r,z,P.x,:,pl.ds(lo+a,n-a)],lambda z: B4.at[z])
-    def acc(self,g,zo,b):
-        lo,n,_=self.groups[g]
-        d=self.R.at[self.row(0),zo,self.P.x,:,pl.ds(lo,n)]
-        d[...]=d[...]+b[zo]
-    def zstep(self,g,h):
-        n=self.groups[g][1]; Z=self.P.Z; z=self.P.z
-        if h==0:
-            def first():
-                for zo in range(Z-1,0,-1): self.zc(g,0,zo,1).start()
-            def last():
-                for zo in range(Z-1): self.zc(g,1,zo,Z-2).start()
-            when(z==0,first); when(z==Z-1,last)
-            return
-        def up():
-            zo=Z-1-h+z
-            self.zc(g,0,zo,z).wait_recv()
-            self.acc(g,zo,self.buf(g,5,n))
-            self.zc(g,0,zo,z+1).start()
-        def down():
-            zo=h-(Z-1)+z
-            self.zc(g,1,zo,z).wait_recv()
-            self.acc(g,zo,self.buf(g,6,n))
-            self.zc(g,1,zo,z-1).start()
-        when(jnp.logical_and(z>=1,z<=h),up)
-        when(jnp.logical_and(z>=Z-1-h,z<=Z-2),down)
+        if self.both(g):
+            B4=self.buf(g,4,n-a)
+            self.y2(g).wait_recv()
+            self.add(lambda z: R.at[r,z,P.x,:,pl.ds(lo+a,n-a)],lambda z: B4.at[z])
+        for d in range(Z-1,0,-1):
+            when(P.z>=d,lambda: self.zc(g,P.z,P.z-d).start())
+            when(P.z<Z-d,lambda: self.zc(g,P.z,P.z+d).start())
     def final(self,g,out):
         lo,n,_=self.groups[g]; P=self.P; Z=P.Z; z=P.z
         out[...]=self.R[self.row(0),z,P.x,:,pl.ds(lo,n)].astype(F32)
-        @pl.when(z>0)
-        def _():
-            self.zc(g,0,z,z).wait_recv()
-            out[...]+=self.buf(g,5,n)[z].astype(F32)
-        @pl.when(z<Z-1)
-        def _():
-            self.zc(g,1,z,z).wait_recv()
-            out[...]+=self.buf(g,6,n)[z].astype(F32)
+        for zo in range(Z):
+            def take():
+                self.zc(g,zo,z).wait_recv()
+                out[...]+=self.buf(g,5,n)[zo].astype(F32)
+            when(z!=zo,take)
     def drain(self,g):
         Z=self.P.Z; z=self.P.z
         for k in range(2):
-            self.ccp(g,k).wait_send(); self.x1(g,k).wait_send()
-        self.x2(g).wait_send(); self.y1(g).wait_send(); self.y2(g).wait_send()
+            self.ccp(g,k).wait_send()
+            if self.both(g): self.x1(g,k).wait_send()
+        self.x2(g).wait_send(); self.y1(g).wait_send()
+        if self.both(g): self.y2(g).wait_send()
         for zo in range(Z):
-            when(z<zo,lambda: self.zc(g,0,zo,z+1).wait_send())
-            when(z>zo,lambda: self.zc(g,1,zo,z-1).wait_send())
+            when(z!=zo,lambda: self.zc(g,z,zo).wait_send())
     def events(self,g,out):
-        ev=[lambda: self.s_c(g),lambda: self.a_c(g),lambda: self.a_1(g),lambda: self.a_2(g)]
-        for t in range(self.P.Z-1): ev.append(lambda t=t: self.zstep(g,t))
-        ev.append(lambda: self.final(g,out))
-        return ev
+        return [lambda: self.s_c(g),lambda: self.a_c(g),lambda: self.a_1(g),lambda: self.a_2(g),lambda: self.final(g,out)]
 
 def norm_sems(Z):
     D=pltpu.SemaphoreType.DMA
-    return [D((3+Z,)),D((3+Z,))]
-def norm_bufs(Z): return [pltpu.VMEM((4+Z,8,128),F32),pltpu.VMEM((3,8,128),F32)]
+    return [D((8+Z,)),D((8+Z,))]
+def norm_bufs(Z): return [pltpu.VMEM((8+Z,8,128),F32),pltpu.VMEM((2,8,128),F32)]
+def cube(P):
+    out=[]
+    for d in range(1,8):
+        dy,dc,dx=d//4,d//2%2,d%2
+        y=1-P.y if dy else P.y
+        c=1-P.c if dc else P.c
+        x=1-P.x if dx else P.x
+        out.append((y*4+c*2+x,(y*2+c,P.z*2+x)))
+    return out
 def all_sum(P,buf,got,ss,rs):
     Z=P.Z
-    for i,dev in enumerate((P.nc,P.nx,P.ny)):
-        cp=rcopy(buf.at[i],got.at[i],ss.at[i],rs.at[i],dev)
-        cp.start(); cp.wait()
-        buf[i+1]=buf[i]+got[i]
-    buf[4+P.z]=buf[3]
-    for t in range(Z):
-        def send(): rcopy(buf.at[3],buf.at[4+P.z],ss.at[3+t],rs.at[3+P.z],P.nz(t)).start()
-        when(P.z!=t,send)
-    for t in range(Z):
-        def wait():
-            cp=rcopy(buf.at[3],buf.at[4+t],ss.at[3+t],rs.at[3+t],P.nz(t))
-            cp.wait_send(); cp.wait_recv()
-        when(P.z!=t,wait)
-    tot=buf[4]
-    for t in range(1,Z): tot=tot+buf[4+t]
+    me=P.y*4+P.c*2+P.x
+    buf[me]=got[0]
+    def term(i,dev): return rcopy(got.at[0],buf.at[me],ss.at[i],rs.at[me],dev)
+    def come(i): return rcopy(got.at[0],buf.at[i],ss.at[i],rs.at[i],P.nc)
+    for i,dev in cube(P): term(i,dev).start()
+    for i,dev in cube(P): come(i).wait_recv()
+    tot=buf[0]
+    for i in range(1,8): tot=tot+buf[i]
+    got[1]=tot
+    buf[8+P.z]=tot
+    def line(src,to): return rcopy(got.at[1],buf.at[8+src],ss.at[8+to],rs.at[8+src],P.nz(to))
+    for t in range(Z): when(P.z!=t,lambda: line(P.z,t).start())
+    for t in range(Z): when(P.z!=t,lambda: line(t,P.z).wait_recv())
+    tot=buf[8]
+    for t in range(1,Z): tot=tot+buf[8+t]
+    for i,dev in cube(P): term(i,dev).wait_send()
+    for t in range(Z): when(P.z!=t,lambda: line(P.z,t).wait_send())
     return tot
 def enter_all(P,Z):
     bar=pltpu.get_barrier_semaphore()
     def sig(d): pl.semaphore_signal(bar,inc=1,device_id=d,device_id_type=MESH)
-    sig(P.nx); sig(P.ny); sig(P.nc)
+    for _,d in cube(P): sig(d)
     for t in range(Z):
         when(P.z!=t,lambda: sig(P.nz(t)))
-    pl.semaphore_wait(bar,3+Z-1)
+    pl.semaphore_wait(bar,7+Z-1)
 
 
 W3 = 768
@@ -403,7 +405,7 @@
 GATHER = [(2304, 1280, 640), (0, 2304, 1152), (3584, 5760, 2944), (9344, 1152, 640), (10496, 1152, 512), (11648, 2304, 1152)]
 SCATTER = ([(UP_AT + CW * c, CW, 640 if c % 2 else 512) for c in range(4)]
            + [(DOWN_AT + CW * c, CW, 640 if c % 2 else 512) for c in range(4)]
-           + [(OUT_AT, CW, 512), (0, CW, 640), (CW, CW, 512), (2 * CW, 1280, 640)])
+           + [(OUT_AT, CW, 512), (0, CW, 640), (CW, CW, 512), (2 * CW, CW, 640), (VEC_AT, VEC_COLS, VEC_COLS)])
 
 def al(v, m): return pl.multiple_of(v, m)
 
@@ -500,14 +502,14 @@
 
 RB=256
 
-RULES=((1,1,0),(2,3,1),(2,7,4))
+RULES=((1,1,0),(2,3,1),(2,4,3))
 
 def places():
     p=[("stat",i,0.6) for i in range(4)]
     for i in range(3):
         p.append(("third",i,0.6 if i else 2.0))
         p+=[("qkv",4*i+k,0.42) for k in range(4)]
-        for pp in range(2): p+=[("af",4*i+2*pp+k,(1.2,2.4)[k]) for k in range(2)]
+        p+=[("af",2*i+pp,2.3) for pp in range(2)]
     p.append(("out",0,0.6))
     p+=[("ob",k,1.1) for k in range(4)]
     for c in range(4):
@@ -522,15 +524,16 @@
     p.append(("bp",0,0.1))
     p+=[("ag",k,0.5) for k in range(4)]
     for i in range(3):
-        for pp in range(2): p+=[("ab",8*i+4*pp+k,1.0) for k in range(4)]
-        p+=[("dh",4*i+k,0.5) for k in range(4)]
-        if i==2: p+=[("ln",k,0.9) for k in range(4)]
+        for pp in range(2): p+=[("ab",4*i+2*pp+k,(1.6,2.1)[k]) for k in range(2)]
         p+=[("dq",3*i+k,0.6+0.2*(k==2)) for k in range(3)]
         p.append(("dp",i,0.1))
+        p+=[("dh",4*i+k,0.5) for k in range(4)]
+    p+=[("ln",k,0.9) for k in range(4)]
+    p.append(("lp",0,0.3))
     return p
 
 def ready_places():
-    return [("mp",c) for c in range(4)]+[("mp",3)]*4+[("bp",0)]+[("dp",i) for i in range(3)]
+    return [("mp",c) for c in range(4)]+[("mp",3)]*4+[("bp",0)]+[("dp",i) for i in range(3)]+[("lp",0)]
 
 def due_places():
     return [("third",0),("third",1),("out",0),("chunk",0),("chunk",1),("chunk",2)]
@@ -561,36 +564,31 @@
                 else: pl.when(step==k)(run)
 
 PLAN = (
-    (0, 0, 0, 0), (2, 0, 0, 1), (3, 0, 1, 0), (3, 0, 0, 2), (4, 0, 0, 3), (4, 0, 0, 4), (4, 0, 1, 1), (4, 0, 0, 5),
-    (4, 0, 0, 6), (4, 0, 1, 2), (4, 0, 1, 3), (4, 0, 0, 7), (4, 0, 0, 8), (4, 0, 1, 4), (4, 0, 2, 0), (4, 0, 0, 9),
-    (4, 0, 1, 5), (5, 0, 1, 6), (10, 0, 2, 1), (10, 0, 1, 7), (11, 0, 1, 8), (12, 0, 2, 2), (12, 0, 2, 3),
-    (13, 0, 1, 9), (20, 0, 2, 4), (20, 0, 2, 5), (24, 0, 4, 0), (24, 0, 2, 6), (27, 0, 4, 1), (28, 0, 2, 7),
-    (28, 0, 3, 0), (29, 0, 3, 1), (30, 0, 3, 2), (30, 0, 3, 3), (30, 0, 2, 8), (30, 0, 4, 2), (30, 0, 3, 4),
-    (30, 0, 3, 5), (30, 0, 4, 3), (30, 0, 4, 4), (30, 0, 3, 6), (30, 0, 4, 5), (30, 0, 5, 0), (31, 0, 3, 7),
-    (31, 0, 2, 9), (31, 0, 5, 1), (32, 0, 3, 8), (33, 0, 4, 6), (34, 0, 5, 2), (35, 0, 4, 7), (36, 0, 3, 9),
-    (39, 0, 5, 3), (40, 0, 4, 8), (41, 0, 5, 4), (42, 0, 4, 9), (43, 0, 5, 5), (47, 1, 0, 0), (49, 0, 5, 6),
-    (49, 0, 5, 7), (50, 1, 0, 1), (53, 1, 0, 2), (54, 0, 5, 8), (58, 1, 0, 3), (59, 1, 1, 0), (60, 0, 5, 9),
-    (61, 1, 0, 4), (63, 1, 1, 1), (66, 1, 0, 5), (67, 1, 1, 2), (70, 1, 0, 6), (72, 1, 2, 0), (72, 1, 1, 3),
-    (72, 1, 1, 4), (74, 1, 2, 1), (75, 1, 1, 5), (76, 1, 0, 7), (78, 1, 2, 2), (81, 1, 2, 3), (81, 1, 2, 4),
-    (82, 1, 1, 6), (83, 1, 3, 0), (86, 1, 2, 5), (87, 1, 3, 1), (87, 1, 4, 0), (88, 1, 2, 6), (88, 1, 1, 7),
-    (89, 1, 4, 1), (90, 1, 5, 0), (90, 1, 2, 7), (94, 1, 3, 2), (97, 1, 4, 2), (99, 1, 3, 3), (100, 1, 3, 4),
-    (100, 1, 4, 3), (100, 1, 5, 1), (101, 1, 6, 0), (103, 1, 3, 5), (103, 1, 6, 1), (103, 1, 7, 0), (103, 1, 4, 4),
-    (105, 1, 5, 2), (107, 1, 3, 6), (108, 1, 4, 5), (109, 1, 6, 2), (110, 1, 5, 3), (110, 1, 7, 1), (110, 1, 8, 0),
-    (111, 1, 4, 6), (112, 1, 3, 7), (112, 1, 5, 4), (113, 1, 6, 3), (113, 1, 8, 1), (114, 1, 4, 7), (114, 1, 6, 4),
-    (115, 1, 5, 5), (115, 1, 9, 0), (116, 1, 7, 2), (116, 1, 6, 5), (117, 1, 5, 6), (119, 1, 6, 6), (120, 1, 8, 2),
-    (120, 1, 7, 3), (121, 1, 9, 1), (122, 1, 5, 7), (122, 1, 7, 4), (124, 1, 8, 3), (125, 1, 7, 5), (126, 1, 6, 7),
-    (126, 1, 8, 4), (128, 1, 10, 0), (128, 1, 9, 2), (128, 1, 8, 5), (130, 1, 7, 6), (131, 1, 8, 6),
-    (131, 1, 10, 1), (132, 1, 7, 7), (134, 1, 10, 2), (134, 1, 8, 7), (137, 1, 9, 3), (137, 1, 9, 4),
-    (139, 1, 9, 5), (141, 1, 10, 3), (143, 1, 9, 6), (148, 1, 11, 0), (148, 1, 10, 4), (148, 1, 10, 5),
-    (148, 1, 10, 6), (148, 1, 9, 7), (149, 1, 11, 1), (149, 1, 10, 7), (149, 1, 11, 2), (149, 1, 11, 3),
-    (149, 1, 11, 4), (149, 1, 11, 5), (149, 1, 11, 6), (149, 1, 11, 7),
+    (0, 0, 0, 0), (1, 0, 0, 1), (1, 0, 0, 2), (3, 0, 0, 3), (3, 0, 1, 0), (3, 0, 0, 4), (3, 0, 0, 5), (4, 0, 1, 1),
+    (4, 0, 0, 6), (4, 0, 0, 7), (4, 0, 0, 8), (4, 0, 1, 2), (4, 0, 1, 3), (4, 0, 1, 4), (4, 0, 0, 9), (5, 0, 1, 5),
+    (6, 0, 2, 0), (7, 0, 1, 6), (10, 0, 1, 7), (11, 0, 2, 1), (11, 0, 1, 8), (11, 0, 1, 9), (11, 0, 2, 2),
+    (17, 0, 2, 3), (18, 0, 2, 4), (18, 0, 2, 5), (22, 0, 3, 0), (23, 0, 3, 1), (24, 0, 2, 6), (25, 0, 3, 2),
+    (25, 0, 2, 7), (25, 0, 2, 8), (25, 0, 3, 3), (25, 0, 3, 4), (25, 0, 4, 0), (25, 0, 3, 5), (25, 0, 2, 9),
+    (26, 0, 4, 1), (26, 0, 4, 2), (27, 0, 3, 6), (27, 0, 3, 7), (28, 0, 4, 3), (29, 0, 3, 8), (30, 0, 4, 4),
+    (30, 0, 4, 5), (30, 0, 3, 9), (31, 0, 5, 0), (33, 0, 4, 6), (34, 0, 5, 1), (34, 0, 4, 7), (37, 0, 5, 2),
+    (37, 0, 5, 3), (38, 0, 4, 8), (40, 0, 5, 4), (41, 0, 5, 5), (41, 1, 0, 0), (41, 0, 4, 9), (44, 0, 5, 6),
+    (45, 1, 0, 1), (45, 0, 5, 7), (48, 0, 5, 8), (50, 1, 0, 2), (51, 0, 5, 9), (53, 1, 1, 0), (58, 1, 1, 1),
+    (62, 1, 0, 3), (65, 1, 2, 0), (65, 1, 1, 2), (69, 1, 2, 1), (73, 1, 2, 2), (73, 1, 1, 3), (73, 1, 0, 4),
+    (77, 1, 3, 0), (79, 1, 2, 3), (79, 1, 3, 1), (80, 1, 4, 0), (82, 1, 4, 1), (84, 1, 2, 4), (87, 1, 3, 2),
+    (88, 1, 5, 0), (90, 1, 4, 2), (91, 1, 1, 4), (92, 1, 3, 3), (92, 1, 5, 1), (92, 1, 6, 0), (93, 1, 4, 3),
+    (93, 1, 6, 1), (95, 1, 5, 2), (97, 1, 3, 4), (98, 1, 7, 0), (100, 1, 6, 2), (102, 1, 5, 3), (103, 1, 7, 1),
+    (103, 1, 8, 0), (104, 1, 4, 4), (104, 1, 6, 3), (105, 1, 8, 1), (107, 1, 7, 2), (107, 1, 9, 0), (108, 1, 6, 4),
+    (108, 1, 8, 2), (112, 1, 5, 4), (115, 1, 7, 3), (116, 1, 8, 3), (116, 1, 9, 1), (116, 1, 10, 0),
+    (117, 1, 10, 1), (118, 1, 9, 2), (119, 1, 8, 4), (120, 1, 10, 2), (121, 1, 7, 4), (122, 1, 11, 0),
+    (124, 1, 9, 3), (125, 1, 11, 1), (125, 1, 10, 3), (131, 1, 11, 2), (131, 1, 12, 0), (131, 1, 10, 4),
+    (132, 1, 9, 4), (132, 1, 12, 1), (132, 1, 11, 3), (132, 1, 12, 2), (132, 1, 12, 3), (132, 1, 12, 4),
+    (132, 1, 11, 4),
 )
 
 def check_plan(plan, keys, index):
     pos={tuple(e[1:]):(e[0],j) for j,e in enumerate(plan)}
     assert set(pos)==keys and len(plan)==len(keys)
     assert all(a[0]<=b[0] for a,b in zip(plan,plan[1:]))
-    last={0:9,1:7}
     for kind,g,k in keys:
         if k: assert pos[(kind,g,k-1)]<pos[(kind,g,k)]
     for g,p in enumerate(due_places()): assert pos[(0,g,9)][0]<=index[p]
@@ -643,8 +641,8 @@
             p=2*s+pp
             def col(j): return qkv.at[s,:,pl.ds(al(256*j+128*pp,128),128)]
             c=pl.ds(al(128*p,128),128)
-            attn_fwd_pair(col(0),col(1),col(2),length,o.at[:,c],oT.at[c,:],lse.at[p],512,
-                          tick=lambda k: at("af",4*i+2*pp+k,12))
+            at("af",2*i+pp,6)
+            attn_fwd_pair(col(0),col(1),col(2),length,o.at[:,c],oT.at[c,:],lse.at[p],512)
             return 0
         lax.fori_loop(0,2,pair,0)
         return 0
@@ -750,31 +748,14 @@
         unpack24(G,QKV_AT+CW*s,W0)
         def pair(pp,_):
             p=2*s+pp
+            at("ab",4*s+2*pp,12)
             def col(j): return qkv.at[s,:,pl.ds(al(256*j+128*pp,128),128)]
             def dcol(j): return dqkv.at[:,pl.ds(al(256*j+128*pp,128),128)]
             c=pl.ds(al(128*p,128),128)
             attn_bwd_pair(col(0),col(1),col(2),do.at[:,c],oT.at[c,:],lse.at[p],length,
-                          dcol(0),dcol(1),dcol(2),dka,dva,256,tick=lambda k: at("ab",8*s+4*pp+k,24))
+                          dcol(0),dcol(1),dcol(2),dka,dva,256,tick=lambda k: at("ab",4*s+2*pp+k,12))
             return 0
         lax.fori_loop(0,2,pair,0)
-        def drow(i,_):
-            at("dh",4*s+i,12)
-            dh1[rows(i),:]+=nt(dqkv[rows(i),:],W0[...])
-            return 0
-        lax.fori_loop(0,NBK,drow,0)
-        @pl.when(s==2)
-        def _():
-            def lrow(i,acc):
-                at("ln",i,4)
-                sl=rows(i)
-                dh=dh1[sl,:]
-                xh,r=norm_parts(tok[sl,:].astype(F32))
-                F1[sl,:]=dr1[sl,:]+norm_back(dh*V1[:,0:D],xh,r)
-                return tuple(a+jnp.sum(b,0,keepdims=True) for a,b in zip(acc,(dh*xh,dh)))
-            a,b=lax.fori_loop(0,NBK,lrow,(z1,z1))
-            dV1[:,0:D]=a
-            dV1[:,D:2*D]=b
-            pack_vec(G,V,dV1)
         def qrow(i,_):
             at("dq",3*s+i,9)
             dW[rows(i),:]=nn(h1T[rows(i),:],dqkv[...])
@@ -782,8 +763,24 @@
         lax.fori_loop(0,D//RB,qrow,0)
         pack24(G,QKV_AT+CW*s,dW)
         at("dp",s,3)
+        def drow(i,_):
+            at("dh",4*s+i,12)
+            dh1[rows(i),:]+=nt(dqkv[rows(i),:],W0[...])
+            return 0
+        lax.fori_loop(0,NBK,drow,0)
         return 0
     lax.fori_loop(0,3,third_back,0)
+    def lrow(i,acc):
+        at("ln",i,4)
+        sl=rows(i)
+        dh=dh1[sl,:]
+        xh,r=norm_parts(tok[sl,:].astype(F32))
+        F1[sl,:]=dr1[sl,:]+norm_back(dh*V1[:,0:D],xh,r)
+        return tuple(a+jnp.sum(b,0,keepdims=True) for a,b in zip(acc,(dh*xh,dh)))
+    sums=lax.fori_loop(0,NBK,lrow,(z1,z1))
+    for j,v in enumerate(sums): dV1[:,pl.ds(j*D,D)]=v
+    pack_vec(G,V,dV1)
+    at("lp",0,1)
     outs=[dma(F1,dtok_o,3)]
     for f in clock.tail: f()
     flat=lax.broadcasted_iota(jnp.int32,(16,VEC_COLS),0)*VEC_COLS+lax.broadcasted_iota(jnp.int32,(16,VEC_COLS),1)
@@ -791,7 +788,7 @@
     vec=own[:,pl.ds(VEC_AT,VEC_COLS)]
     vec=jnp.where(jnp.logical_and(flat>=start,flat<start+240),vec,0.0)
     left=own[:,pl.ds(0,VEC_AT)]; right=own[:,pl.ds(OUT_AT,COLS-OUT_AT)]
-    nb[0]=jnp.full((8,128),1.0,F32)*(jnp.sum(left*left)+jnp.sum(right*right)+jnp.sum(vec*vec))
+    got[0]=jnp.full((8,128),1.0,F32)*(jnp.sum(left*left)+jnp.sum(right*right)+jnp.sum(vec*vec))
     outs.append(dma(own,own_o,4))
     nrm[8:24,:]=vec
     nrm[0:8,:]=all_sum(place,nb,got,ns,nr)

time: 237 us -> 211 us (0.89)
  Pallas kernels: 231 us -> 206 us
    pallas_call x1, Pallas kernels: 224 us -> 199 us  [mega_call(): pl.pallas_call(functools.partial(mega_kernel, Z, plan), out_shape=outs, i...]
where the time goes in v2:
time: 211 us
  Pallas kernels  206 us (98%)
  between operations  3.3 us (2%)
    pallas_call x1, Pallas kernels, mega_call(): pl.pallas_call(functools.partial(mega_kernel, Z, plan), out_shape=outs, i...  199 us
    pallas_call x1, Pallas kernels, adam_call(): pl.pallas_call(adam_kernel, out_shape=[jax.ShapeDtypeStruct(a.shape, a.dt...  6.65 us

profile of v2, /device:TPU:0, one launch (start us, length us, event | category | flops | bytes accessed | tf_op | source)
XLA Modules:
  0.0 211.1 jit_solution(7139724986312731264)
XLA Ops:
  0.7 0.7 convert_element_type.3
  1.4 0.2 dynamic_update_slice.3
  1.5 0.0 copy-start.1
  2.2 0.0 copy-done.1
  2.2 199.1 %shard_map.313 = (bf16[1024,768]{1,0:T(8,128)(2,1)}, f32[1024,768]{1,0:T(8,128)}, f32[16,13952]{1,0:T(8,128)}, f32[24,128]{1,0:T(8,128)}) custom-call(bf16[1024,768]{1,0:T(8,128)(2,1)} %bitcast.11, bf16[1024,768]{1,0:T(8,128)(2,1)} %bitcast.12, s32[1]{0:T(128)S(6)} %copy.37.len_ref, f32[24,2304]{1,0:T(8,128)} %refs_0_.1, f32[24,768]{1,0:T(8,128)} %refs_3_.1, ...), custom_call_target="tpu_custom_call" | custom-call | flops 60000002048 | bytes 62914560 | tf_op jit(solution)/shard_map/pallas_call | solution.py:810
  201.3 0.0 copy-start
  201.3 0.0 copy-start.2
  201.3 0.0 copy-start.3
  201.4 0.0 copy-start.4
  201.4 6.6 %shard_map.314 = (f32[24,2304]{1,0:T(8,128)}, f32[24,2304]{1,0:T(8,128)}, f32[24,2304]{1,0:T(8,128)}, f32[24,768]{1,0:T(8,128)}, f32[24,768]{1,0:T(8,128)}, /*in...) custom-call(s32[1]{0:T(128)} %bitcast.par_ref, ...), custom_call_target="tpu_custom_call" | custom-call | flops 10000000 | bytes 8388608 | tf_op jit(solution)/shard_map/pallas_call | solution.py:892
  208.0 0.0 copy-done
  208.0 0.5 slice.6
  209.3 0.0 copy-done.2
  209.3 0.0 copy-done.3
  209.3 0.0 copy-done.4
  209.3 0.7 multiply_subtract_fusion
  (2 shorter events, 0.0 us)
Async XLA Ops:
  1.5 0.7 copy-start.1
  201.3 6.7 %copy-start = (f32[24,128]{1,0:T(8,128)S(1)}, f32[24,128]{1,0:T(8,128)}, u32[]{:S(2)}) copy-start(f32[24,128]{1,0:T(8,128)} %get-tuple-element.37.nrm_h) | copy-start | bytes 36868
  201.3 8.0 %copy-start.2 = (f32[240]{0:T(256)S(1)}, f32[240]{0:T(256)}, u32[]{:S(2)}) copy-start(f32[240]{0:T(256)} %param.33) | copy-start | bytes 2884
  201.3 8.0 %copy-start.3 = (f32[240]{0:T(256)S(1)}, f32[240]{0:T(256)}, u32[]{:S(2)}) copy-start(f32[240]{0:T(256)} %param.34) | copy-start | bytes 2884
  201.4 8.0 %copy-start.4 = (f32[240]{0:T(256)S(1)}, f32[240]{0:T(256)}, u32[]{:S(2)}) copy-start(f32[240]{0:T(256)} %param.35) | copy-start | bytes 2884

commit v3 on v2

--- a/solution.py
+++ b/solution.py
@@ -159,86 +159,122 @@
     return [D((NG*2*(Z-1),)),D((NG*2*(Z-1),)),
             D((NG*2*Z,)),D((NG*2*Z,)),
             D((NG*2*Z,)),D((NG*2*Z,)),
-            D((NG*2,)),D((NG*2,))]
+            D((NG*2,)),D((NG*2,)),
+            D((NG*2*(Z-1),)),D((NG*2*(Z-1),))]
 
 class Gather:
     def __init__(self,P,G,groups,sems):
-        self.P=P; self.G=G; self.groups=groups; self.zs,self.zr,self.xs,self.xr,self.ys,self.yr,self.cs,self.cr=sems
+        self.P=P; self.G=G; self.groups=groups
+        self.zs,self.zr,self.xs,self.xr,self.ys,self.yr,self.cs,self.cr,self.fs,self.fr=sems
+    def direct(self,g):
+        lo,n,a,p,q=self.groups[g]
+        return p+q==n
     def _cp(self,idx,lo,n,ss,rs,dev):
         r=self.G.at[(*idx,slice(None),pl.ds(lo,n))]
         return rcopy(r,r,ss,rs,dev)
     def zcp(self,g,d,t,zo,to):
-        lo,n,_=self.groups[g]; i=(g*2+d)*(self.P.Z-1)+t
+        lo,n=self.groups[g][:2]; i=(g*2+d)*(self.P.Z-1)+t
         return self._cp(self.P.piece(zo),lo,n,self.zs.at[i],self.zr.at[i],self.P.nz(to))
+    def zdiag(self,g,d,t,zo,to):
+        lo,n,a,p,q=self.groups[g]; i=(g*2+d)*(self.P.Z-1)+t
+        return self._cp(self.P.piece(zo,dx=1,dy=1),lo+p,n-p-q,self.fs.at[i],self.fr.at[i],self.P.nz(to))
     def xfull(self,g,zo,arrive=0):
-        lo,n,_=self.groups[g]; i=g*2*self.P.Z+zo
+        lo,n=self.groups[g][:2]; i=g*2*self.P.Z+zo
         return self._cp(self.P.piece(zo,dx=arrive),lo,n,self.xs.at[i],self.xr.at[i],self.P.nx)
     def yfull(self,g,zo,arrive=0):
-        lo,n,_=self.groups[g]; i=g*2*self.P.Z+zo
+        lo,n=self.groups[g][:2]; i=g*2*self.P.Z+zo
         return self._cp(self.P.piece(zo,dy=arrive),lo,n,self.ys.at[i],self.yr.at[i],self.P.ny)
-    def ydiag(self,g,zo,arrive=0):
-        lo,n,a=self.groups[g]; i=g*2*self.P.Z+self.P.Z+zo
-        return self._cp(self.P.piece(zo,dx=1,dy=arrive),lo,a,self.ys.at[i],self.yr.at[i],self.P.ny)
-    def xdiag(self,g,zo,arrive=0):
-        lo,n,a=self.groups[g]; i=g*2*self.P.Z+self.P.Z+zo
-        return self._cp(self.P.piece(zo,dy=1,dx=arrive),lo+a,n-a,self.xs.at[i],self.xr.at[i],self.P.nx)
+    def ydiag(self,g,zo,near,arrive=0):
+        lo,n,a,p,q=self.groups[g]; i=g*2*self.P.Z+self.P.Z+zo
+        return self._cp(self.P.piece(zo,dx=1,dy=arrive),lo,a if near else p,self.ys.at[i],self.yr.at[i],self.P.ny)
+    def xdiag(self,g,zo,near,arrive=0):
+        lo,n,a,p,q=self.groups[g]; i=g*2*self.P.Z+self.P.Z+zo
+        w=n-a if near else q
+        return self._cp(self.P.piece(zo,dy=1,dx=arrive),lo+n-w,w,self.xs.at[i],self.xr.at[i],self.P.nx)
     def ccp(self,g,k,arrive=0):
-        lo,n,_=self.groups[g]
+        lo,n=self.groups[g][:2]
         y=self.P.y if k==0 else 1-self.P.y
         r=self.G.at[self.P.slab(y,dc=arrive),:,:,:,pl.ds(lo,n)]
         return rcopy(r,r,self.cs.at[g*2+k],self.cr.at[g*2+k],self.P.nc)
+    def others(self,t,f):
+        when(self.P.z>=t,lambda: f(self.P.z-t)); when(self.P.z<self.P.Z-t,lambda: f(self.P.z+t))
     def own(self,g):
         z=self.P.z; Z=self.P.Z
-        when(z<Z-1,lambda: self.zcp(g,0,0,z,z+1).start())
-        when(z>0,lambda: self.zcp(g,1,0,z,z-1).start())
         self.xfull(g,z).start(); self.yfull(g,z).start()
+        for t in range(Z-1 if self.direct(g) else 1):
+            when(z<Z-1-t,lambda: self.zcp(g,0,t,z,z+1+t).start())
+            when(z>t,lambda: self.zcp(g,1,t,z,z-1-t).start())
     def zarrive(self,g,t):
         z=self.P.z; Z=self.P.Z
+        on=t+1<Z-1 and not self.direct(g)
         def below():
             zo=z-1-t
             self.zcp(g,0,t,zo,z).wait_recv()
-            if t+1<Z-1:
-                when(z<Z-1,lambda: self.zcp(g,0,t+1,zo,z+1).start())
+            if on: when(z<Z-1,lambda: self.zcp(g,0,t+1,zo,z+1).start())
             self.xfull(g,zo).start(); self.yfull(g,zo).start()
         def above():
             zo=z+1+t
             self.zcp(g,1,t,zo,z).wait_recv()
-            if t+1<Z-1:
-                when(z>0,lambda: self.zcp(g,1,t+1,zo,z-1).start())
+            if on: when(z>0,lambda: self.zcp(g,1,t+1,zo,z-1).start())
             self.xfull(g,zo).start(); self.yfull(g,zo).start()
         when(z>t,below); when(z<Z-1-t,above)
-    def _diag(self,g,zo):
-        self.xfull(g,zo,1).wait_recv(); self.ydiag(g,zo).start()
-        self.yfull(g,zo,1).wait_recv(); self.xdiag(g,zo).start()
     def diag(self,g,t):
+        def pass_on(zo):
+            self.xfull(g,zo,1).wait_recv(); self.ydiag(g,zo,t==0).start()
+            self.yfull(g,zo,1).wait_recv(); self.xdiag(g,zo,t==0).start()
+        if t==0: pass_on(self.P.z)
+        else: self.others(t,pass_on)
+    def line(self,g,t):
         z=self.P.z; Z=self.P.Z
-        if t==0: self._diag(g,z)
-        else:
-            when(z>=t,lambda: self._diag(g,z-t))
-            when(z<Z-t,lambda: self._diag(g,z+t))
+        if t==0:
+            self.ydiag(g,z,True,1).wait_recv(); self.xdiag(g,z,True,1).wait_recv()
+            when(z<Z-1,lambda: self.zdiag(g,0,0,z,z+1).start())
+            when(z>0,lambda: self.zdiag(g,1,0,z,z-1).start())
+            return
+        def below():
+            self.zdiag(g,0,t-1,z-t,z).wait_recv()
+            if t<Z-1: when(z<Z-1,lambda: self.zdiag(g,0,t,z-t,z+1).start())
+        def above():
+            self.zdiag(g,1,t-1,z+t,z).wait_recv()
+            if t<Z-1: when(z>0,lambda: self.zdiag(g,1,t,z+t,z-1).start())
+        when(z>=t,below); when(z<Z-t,above)
     def corner(self,g):
         self.ccp(g,0).start()
-        for zo in range(self.P.Z):
-            self.ydiag(g,zo,1).wait_recv(); self.xdiag(g,zo,1).wait_recv()
+        if self.direct(g):
+            self.ydiag(g,self.P.z,True,1).wait_recv(); self.xdiag(g,self.P.z,True,1).wait_recv()
+        else: self.line(g,self.P.Z-1)
+        def come(zo):
+            self.ydiag(g,zo,False,1).wait_recv(); self.xdiag(g,zo,False,1).wait_recv()
+        for t in range(1,self.P.Z): self.others(t,come)
         self.ccp(g,1).start()
     def sibling(self,g):
         self.ccp(g,0,1).wait_recv(); self.ccp(g,1,1).wait_recv()
     def drain(self,g):
         z=self.P.z; Z=self.P.Z
-        for zo in range(Z):
+        def sent(zo,near):
             self.xfull(g,zo).wait_send(); self.yfull(g,zo).wait_send()
-            self.xdiag(g,zo).wait_send(); self.ydiag(g,zo).wait_send()
+            self.xdiag(g,zo,near).wait_send(); self.ydiag(g,zo,near).wait_send()
+        sent(z,True)
+        for t in range(1,Z): self.others(t,lambda zo: sent(zo,False))
         for k in range(2): self.ccp(g,k).wait_send()
         for t in range(Z-1):
-            when(jnp.logical_and(z<Z-1,z>=t),lambda: self.zcp(g,0,t,z-t,z+1).wait_send())
-            when(jnp.logical_and(z>0,z<=Z-1-t),lambda: self.zcp(g,1,t,z+t,z-1).wait_send())
+            if self.direct(g):
+                when(z<Z-1-t,lambda: self.zcp(g,0,t,z,z+1+t).wait_send())
+                when(z>t,lambda: self.zcp(g,1,t,z,z-1-t).wait_send())
+                continue
+            def up():
+                self.zcp(g,0,t,z-t,z+1).wait_send(); self.zdiag(g,0,t,z-t,z+1).wait_send()
+            def down():
+                self.zcp(g,1,t,z+t,z-1).wait_send(); self.zdiag(g,1,t,z+t,z-1).wait_send()
+            when(jnp.logical_and(z<Z-1,z>=t),up)
+            when(jnp.logical_and(z>0,z<=Z-1-t),down)
     def events(self,g):
         Z=self.P.Z
         ev=[lambda: self.own(g)]
-        for t in range(Z-1):
-            ev.append(lambda t=t: self.zarrive(g,t))
+        for t in range(Z):
+            if t<Z-1: ev.append(lambda t=t: self.zarrive(g,t))
+            if t and not self.direct(g): ev.append(lambda t=t: self.line(g,t-1))
             ev.append(lambda t=t: self.diag(g,t))
-        ev.append(lambda: self.diag(g,Z-1))
         ev.append(lambda: self.corner(g))
         ev.append(lambda: self.sibling(g))
         return ev
@@ -353,44 +389,30 @@
 
 def norm_sems(Z):
     D=pltpu.SemaphoreType.DMA
-    return [D((8+Z,)),D((8+Z,))]
-def norm_bufs(Z): return [pltpu.VMEM((8+Z,8,128),F32),pltpu.VMEM((2,8,128),F32)]
-def cube(P):
-    out=[]
-    for d in range(1,8):
-        dy,dc,dx=d//4,d//2%2,d%2
-        y=1-P.y if dy else P.y
-        c=1-P.c if dc else P.c
-        x=1-P.x if dx else P.x
-        out.append((y*4+c*2+x,(y*2+c,P.z*2+x)))
-    return out
+    return [D((8*Z,)),D((8*Z,))]
+def norm_bufs(Z): return [pltpu.VMEM((8*Z,8,128),F32),pltpu.VMEM((1,8,128),F32)]
+def everyone(P):
+    n=8*P.Z
+    for k in range(1,n):
+        i=lax.rem(P.dp*2*P.Z+P.fs+k,n)
+        yield k,i,(i//(2*P.Z),lax.rem(i,2*P.Z))
 def all_sum(P,buf,got,ss,rs):
-    Z=P.Z
-    me=P.y*4+P.c*2+P.x
+    n=8*P.Z
+    me=P.dp*2*P.Z+P.fs
     buf[me]=got[0]
-    def term(i,dev): return rcopy(got.at[0],buf.at[me],ss.at[i],rs.at[me],dev)
-    def come(i): return rcopy(got.at[0],buf.at[i],ss.at[i],rs.at[i],P.nc)
-    for i,dev in cube(P): term(i,dev).start()
-    for i,dev in cube(P): come(i).wait_recv()
+    for k,i,dev in everyone(P):
+        rcopy(got.at[0],buf.at[me],ss.at[k],rs.at[me],dev).start()
+    for k,i,dev in everyone(P):
+        rcopy(got.at[0],buf.at[i],ss.at[k],rs.at[i],dev).wait_recv()
     tot=buf[0]
-    for i in range(1,8): tot=tot+buf[i]
-    got[1]=tot
-    buf[8+P.z]=tot
-    def line(src,to): return rcopy(got.at[1],buf.at[8+src],ss.at[8+to],rs.at[8+src],P.nz(to))
-    for t in range(Z): when(P.z!=t,lambda: line(P.z,t).start())
-    for t in range(Z): when(P.z!=t,lambda: line(t,P.z).wait_recv())
-    tot=buf[8]
-    for t in range(1,Z): tot=tot+buf[8+t]
-    for i,dev in cube(P): term(i,dev).wait_send()
-    for t in range(Z): when(P.z!=t,lambda: line(P.z,t).wait_send())
+    for i in range(1,n): tot=tot+buf[i]
+    for k,i,dev in everyone(P):
+        rcopy(got.at[0],buf.at[me],ss.at[k],rs.at[me],dev).wait_send()
     return tot
-def enter_all(P,Z):
+def announce(P,Z):
     bar=pltpu.get_barrier_semaphore()
-    def sig(d): pl.semaphore_signal(bar,inc=1,device_id=d,device_id_type=MESH)
-    for _,d in cube(P): sig(d)
-    for t in range(Z):
-        when(P.z!=t,lambda: sig(P.nz(t)))
-    pl.semaphore_wait(bar,7+Z-1)
+    for _,_,d in everyone(P): pl.semaphore_signal(bar,inc=1,device_id=d,device_id_type=MESH)
+    return bar
 
 
 W3 = 768
@@ -402,10 +424,11 @@
 DOWN_AT = 4736
 UP_AT = 9344
 COLS = 13952
-GATHER = [(2304, 1280, 640), (0, 2304, 1152), (3584, 5760, 2944), (9344, 1152, 640), (10496, 1152, 512), (11648, 2304, 1152)]
+GATHER = [(2304, 1280, 640, 640, 640), (0, 2304, 1152, 384, 384), (3584, 5760, 2944, 1024, 896),
+          (9344, 1152, 640, 256, 128), (10496, 1152, 512, 128, 256), (11648, 2304, 1152, 384, 384)]
 SCATTER = ([(UP_AT + CW * c, CW, 640 if c % 2 else 512) for c in range(4)]
            + [(DOWN_AT + CW * c, CW, 640 if c % 2 else 512) for c in range(4)]
-           + [(OUT_AT, CW, 512), (0, CW, 640), (CW, CW, 512), (2 * CW, CW, 640), (VEC_AT, VEC_COLS, VEC_COLS)])
+           + [(OUT_AT, CW, 512), (0, CW, 640), (CW, CW, 512), (2 * CW, 640, 256), (2 * CW + 640, 512, 256), (VEC_AT, VEC_COLS, VEC_COLS)])
 
 def al(v, m): return pl.multiple_of(v, m)
 
@@ -416,17 +439,19 @@
     parts=[jnp.concatenate([rest[:,256*s:256*s+128],rest[:,256*s+128:256*s+256]],0) for s in range(3)]
     G[(*me,slice(None),pl.ds(al(at+W3,128),W3//2))]=jnp.concatenate(parts,1).astype(BF)
 
-def pack_own(place, G, wqkv, wout, wup, wdown, vec):
+def pack_own(place, G, wqkv, wout, wup, wdown, vec, first):
     me=place.me
     lo=al(8*place.x,8); ro=al(16*(1-place.x),8)
     def cols(w,cs):
         return [jnp.concatenate([w[pl.ds(a,n),pl.ds(c,k)] for c,k in cs],1) for a,n in ((lo,16),(ro,8))]
-    for s in range(3): pack_rows(G,me,QKV_AT+CW*s,*cols(wqkv,third_cols(s)))
+    for s in ((2,) if first else (0,1)): pack_rows(G,me,QKV_AT+CW*s,*cols(wqkv,third_cols(s)))
+    if first:
+        G[(*me,slice(None),pl.ds(VEC_AT,VEC_COLS))]=vec[...]
+        return
     pack_rows(G,me,OUT_AT,*cols(wout,[(0,W3)]))
     for c in range(4): pack_rows(G,me,UP_AT+CW*c,*cols(wup,[(W3*c,W3)]))
     for r in range(6):
         G[(*me,slice(None),pl.ds(DOWN_AT+r*D,D))]=wdown[pl.ds(16*r,16),:].astype(BF)
-    G[(*me,slice(None),pl.ds(VEC_AT,VEC_COLS))]=vec[...]
 
 def unpack24(G, at, dst):
     Z=G.shape[1]
@@ -505,7 +530,7 @@
 RULES=((1,1,0),(2,3,1),(2,4,3))
 
 def places():
-    p=[("stat",i,0.6) for i in range(4)]
+    p=[("in",0,0.7),("in",1,0.8)]+[("stat",i,0.6) for i in range(4)]
     for i in range(3):
         p.append(("third",i,0.6 if i else 2.0))
         p+=[("qkv",4*i+k,0.42) for k in range(4)]
@@ -514,26 +539,26 @@
     p+=[("ob",k,1.1) for k in range(4)]
     for c in range(4):
         p.append(("chunk",c,0.5))
-        p+=[("mr",4*c+k,1.75) for k in range(4)]
+        p+=[("mr",4*c+k,1.7) for k in range(4)]
         p+=[("mw",3*c+k,0.6+0.15*(k==2)) for k in range(3)]
         p+=[("mu",3*c+k,0.6+0.2*(k==2)) for k in range(3)]
         p.append(("mp",c,0.1))
     p.append(("fin",0,1.0))
     p+=[("bb",k,1.3) for k in range(4)]
     p+=[("bw",k,0.6+0.2*(k==2)) for k in range(3)]
-    p.append(("bp",0,0.1))
-    p+=[("ag",k,0.5) for k in range(4)]
+    p.append(("bp",0,0.4))
     for i in range(3):
         for pp in range(2): p+=[("ab",4*i+2*pp+k,(1.6,2.1)[k]) for k in range(2)]
         p+=[("dq",3*i+k,0.6+0.2*(k==2)) for k in range(3)]
         p.append(("dp",i,0.1))
         p+=[("dh",4*i+k,0.5) for k in range(4)]
-    p+=[("ln",k,0.9) for k in range(4)]
-    p.append(("lp",0,0.3))
+    p+=[("ln",k,0.5+0.4*(k==3)) for k in range(4)]
+    p.append(("lp",0,0.1))
+    p+=[("lx",k,0.65) for k in range(4)]
     return p
 
 def ready_places():
-    return [("mp",c) for c in range(4)]+[("mp",3)]*4+[("bp",0)]+[("dp",i) for i in range(3)]+[("lp",0)]
+    return [("mp",c) for c in range(4)]+[("mp",3)]*4+[("bp",0)]+[("dp",i) for i in (0,1,2,2)]+[("lp",0)]
 
 def due_places():
     return [("third",0),("third",1),("out",0),("chunk",0),("chunk",1),("chunk",2)]
@@ -564,25 +589,27 @@
                 else: pl.when(step==k)(run)
 
 PLAN = (
-    (0, 0, 0, 0), (1, 0, 0, 1), (1, 0, 0, 2), (3, 0, 0, 3), (3, 0, 1, 0), (3, 0, 0, 4), (3, 0, 0, 5), (4, 0, 1, 1),
-    (4, 0, 0, 6), (4, 0, 0, 7), (4, 0, 0, 8), (4, 0, 1, 2), (4, 0, 1, 3), (4, 0, 1, 4), (4, 0, 0, 9), (5, 0, 1, 5),
-    (6, 0, 2, 0), (7, 0, 1, 6), (10, 0, 1, 7), (11, 0, 2, 1), (11, 0, 1, 8), (11, 0, 1, 9), (11, 0, 2, 2),
-    (17, 0, 2, 3), (18, 0, 2, 4), (18, 0, 2, 5), (22, 0, 3, 0), (23, 0, 3, 1), (24, 0, 2, 6), (25, 0, 3, 2),
-    (25, 0, 2, 7), (25, 0, 2, 8), (25, 0, 3, 3), (25, 0, 3, 4), (25, 0, 4, 0), (25, 0, 3, 5), (25, 0, 2, 9),
-    (26, 0, 4, 1), (26, 0, 4, 2), (27, 0, 3, 6), (27, 0, 3, 7), (28, 0, 4, 3), (29, 0, 3, 8), (30, 0, 4, 4),
-    (30, 0, 4, 5), (30, 0, 3, 9), (31, 0, 5, 0), (33, 0, 4, 6), (34, 0, 5, 1), (34, 0, 4, 7), (37, 0, 5, 2),
-    (37, 0, 5, 3), (38, 0, 4, 8), (40, 0, 5, 4), (41, 0, 5, 5), (41, 1, 0, 0), (41, 0, 4, 9), (44, 0, 5, 6),
-    (45, 1, 0, 1), (45, 0, 5, 7), (48, 0, 5, 8), (50, 1, 0, 2), (51, 0, 5, 9), (53, 1, 1, 0), (58, 1, 1, 1),
-    (62, 1, 0, 3), (65, 1, 2, 0), (65, 1, 1, 2), (69, 1, 2, 1), (73, 1, 2, 2), (73, 1, 1, 3), (73, 1, 0, 4),
-    (77, 1, 3, 0), (79, 1, 2, 3), (79, 1, 3, 1), (80, 1, 4, 0), (82, 1, 4, 1), (84, 1, 2, 4), (87, 1, 3, 2),
-    (88, 1, 5, 0), (90, 1, 4, 2), (91, 1, 1, 4), (92, 1, 3, 3), (92, 1, 5, 1), (92, 1, 6, 0), (93, 1, 4, 3),
-    (93, 1, 6, 1), (95, 1, 5, 2), (97, 1, 3, 4), (98, 1, 7, 0), (100, 1, 6, 2), (102, 1, 5, 3), (103, 1, 7, 1),
-    (103, 1, 8, 0), (104, 1, 4, 4), (104, 1, 6, 3), (105, 1, 8, 1), (107, 1, 7, 2), (107, 1, 9, 0), (108, 1, 6, 4),
-    (108, 1, 8, 2), (112, 1, 5, 4), (115, 1, 7, 3), (116, 1, 8, 3), (116, 1, 9, 1), (116, 1, 10, 0),
-    (117, 1, 10, 1), (118, 1, 9, 2), (119, 1, 8, 4), (120, 1, 10, 2), (121, 1, 7, 4), (122, 1, 11, 0),
-    (124, 1, 9, 3), (125, 1, 11, 1), (125, 1, 10, 3), (131, 1, 11, 2), (131, 1, 12, 0), (131, 1, 10, 4),
-    (132, 1, 9, 4), (132, 1, 12, 1), (132, 1, 11, 3), (132, 1, 12, 2), (132, 1, 12, 3), (132, 1, 12, 4),
-    (132, 1, 11, 4),
+    (0, 0, 0, 0), (1, 0, 1, 0), (1, 0, 2, 0), (1, 0, 0, 1), (1, 0, 0, 2), (1, 0, 0, 3), (1, 0, 1, 1), (1, 0, 1, 2),
+    (1, 0, 0, 4), (1, 0, 0, 5), (1, 0, 1, 3), (2, 0, 1, 4), (3, 0, 0, 6), (3, 0, 0, 7), (3, 0, 2, 1), (3, 0, 3, 0),
+    (3, 0, 1, 5), (3, 0, 1, 6), (4, 0, 2, 2), (5, 0, 1, 7), (6, 0, 0, 8), (6, 0, 0, 9), (8, 0, 1, 8), (8, 0, 1, 9),
+    (8, 0, 1, 10), (9, 0, 2, 3), (12, 0, 2, 4), (12, 0, 1, 11), (13, 0, 1, 12), (14, 0, 3, 1), (15, 0, 2, 5),
+    (15, 0, 2, 6), (16, 0, 3, 2), (17, 0, 2, 7), (19, 0, 5, 0), (20, 0, 3, 3), (20, 0, 2, 8), (21, 0, 3, 4),
+    (22, 0, 4, 0), (22, 0, 2, 9), (24, 0, 2, 10), (25, 0, 3, 5), (25, 0, 3, 6), (26, 0, 5, 1), (26, 0, 3, 7),
+    (26, 0, 3, 8), (26, 0, 2, 11), (26, 0, 4, 1), (27, 0, 4, 2), (27, 0, 4, 3), (27, 0, 3, 9), (27, 0, 3, 10),
+    (27, 0, 2, 12), (28, 0, 5, 2), (29, 0, 4, 4), (29, 0, 4, 5), (30, 0, 3, 11), (31, 0, 5, 3), (31, 0, 4, 6),
+    (31, 0, 5, 4), (31, 0, 5, 5), (32, 0, 3, 12), (32, 0, 4, 7), (35, 0, 5, 6), (35, 0, 5, 7), (35, 0, 4, 8),
+    (35, 0, 4, 9), (35, 0, 4, 10), (37, 0, 5, 8), (37, 0, 5, 9), (37, 0, 4, 11), (40, 0, 4, 12), (43, 1, 0, 0),
+    (45, 0, 5, 10), (47, 1, 0, 1), (51, 0, 5, 11), (54, 1, 0, 2), (55, 1, 1, 0), (56, 0, 5, 12), (58, 1, 1, 1),
+    (59, 1, 0, 3), (67, 1, 2, 0), (68, 1, 1, 2), (70, 1, 0, 4), (70, 1, 2, 1), (75, 1, 2, 2), (79, 1, 3, 0),
+    (80, 1, 1, 3), (81, 1, 3, 1), (81, 1, 4, 0), (82, 1, 2, 3), (83, 1, 4, 1), (86, 1, 3, 2), (88, 1, 5, 0),
+    (89, 1, 2, 4), (89, 1, 4, 2), (90, 1, 1, 4), (90, 1, 3, 3), (90, 1, 5, 1), (90, 1, 6, 0), (91, 1, 4, 3),
+    (91, 1, 6, 1), (92, 1, 7, 0), (95, 1, 5, 2), (96, 1, 6, 2), (97, 1, 3, 4), (102, 1, 5, 3), (102, 1, 7, 1),
+    (102, 1, 8, 0), (103, 1, 4, 4), (103, 1, 6, 3), (103, 1, 8, 1), (105, 1, 7, 2), (105, 1, 5, 4), (108, 1, 8, 2),
+    (109, 1, 6, 4), (109, 1, 9, 0), (113, 1, 7, 3), (113, 1, 9, 1), (114, 1, 10, 0), (114, 1, 8, 3),
+    (115, 1, 10, 1), (117, 1, 9, 2), (120, 1, 10, 2), (120, 1, 11, 0), (121, 1, 8, 4), (123, 1, 7, 4),
+    (124, 1, 9, 3), (124, 1, 11, 1), (124, 1, 12, 0), (127, 1, 10, 3), (127, 1, 12, 1), (129, 1, 11, 2),
+    (130, 1, 13, 0), (131, 1, 12, 2), (133, 1, 9, 4), (134, 1, 11, 3), (134, 1, 13, 1), (134, 1, 13, 2),
+    (134, 1, 11, 4), (134, 1, 10, 4), (134, 1, 12, 3), (134, 1, 13, 3), (134, 1, 13, 4), (134, 1, 12, 4),
 )
 
 def check_plan(plan, keys, index):
@@ -591,7 +618,8 @@
     assert all(a[0]<=b[0] for a,b in zip(plan,plan[1:]))
     for kind,g,k in keys:
         if k: assert pos[(kind,g,k-1)]<pos[(kind,g,k)]
-    for g,p in enumerate(due_places()): assert pos[(0,g,9)][0]<=index[p]
+    assert pos[(0,0,0)][0]==0 and all(pos[(0,g,0)][0]>=1 for g in range(1,len(GATHER)))
+    for g,p in enumerate(due_places()): assert max(v[0] for e,v in pos.items() if e[:2]==(0,g))<=index[p]
     for g,p in enumerate(ready_places()):
         assert pos[(1,g,0)][0]>=index[p]
         for n,i,j in RULES:
@@ -599,22 +627,31 @@
 
 def mega_kernel(Z,plan,tok_h,cot_h,len_ref,wqkv_s,wout_s,wup_s,wdown_s,vec_s,
                mixed_o,dtok_o,own_o,nrm_o,
-               G,tok,cot,F1,F2,F3,qkv,B1,B2,B3,hT,aT,oT,W0,W1,dW,lse,V,V1,dV1,dka,dva,own,nrm,dsem,*rest):
-    gsems=rest[:8]; rbufs=rest[8:8+NB]; rsems=rest[8+NB:16+NB]; nb,got,ns,nr=rest[16+NB:]
+               G,tok,cot,F1,F2,F3,qkv,B1,B2,B3,h1T,h2T,aT,oT,W0,W1,dW,lse,V,V1,dV1,dka,dva,own,nrm,dsem,*rest):
+    gsems=rest[:10]; rbufs=rest[10:10+NB]; rsems=rest[10+NB:18+NB]; nb,got,ns,nr=rest[18+NB:]
     L=tok.shape[0]
     NBK=L//RB
     place=Place(Z)
     def dma(a,b,i):
         cp=pltpu.make_async_copy(a,b,dsem.at[i]); cp.start(); return cp
     ldt=dma(tok_h,tok,0); ldc=dma(cot_h,cot,1)
-    pack_own(place,G,wqkv_s,wout_s,wup_s,wdown_s,vec_s)
-    enter_all(place,Z)
+    bar=announce(place,Z)
+    shards=(wqkv_s,wout_s,wup_s,wdown_s,vec_s)
+    pack_own(place,G,*shards,True)
+    pl.semaphore_wait(bar,8*Z-1)
     ga=Gather(place,G,GATHER,gsems)
     sc=Scatter(place,G,SCATTER,rbufs,rsems)
     clock=Clock(plan,ga,sc,own)
     def at(name,step,count): clock.at(name,step,count)
     def rows(i): return pl.ds(al(i*RB,RB),RB)
     length=len_ref[0]
+    at("in",0,2)
+    pack_own(place,G,*shards,False)
+    at("in",1,2)
+    F3[...]=jnp.zeros_like(F3)
+    ldc.wait()
+    dead=lax.broadcasted_iota(jnp.int32,(L,D),0)>=length
+    cot[...]=jnp.where(dead,jnp.zeros((),BF),cot[...])
     ldt.wait()
     xhat=F1; h1=B1; o=B3
     for i in range(4):
@@ -628,7 +665,9 @@
         def _():
             unpack_vec(G,V,V1)
             def first(j,_):
-                h1[rows(j),:]=(xhat[rows(j),:]*V1[:,0:D]+V1[:,D:2*D]).astype(BF)
+                hb=(xhat[rows(j),:]*V1[:,0:D]+V1[:,D:2*D]).astype(BF)
+                h1[rows(j),:]=hb
+                h1T[:,rows(j)]=hb.T
                 return 0
             lax.fori_loop(0,NBK,first,0)
         unpack24(G,QKV_AT+CW*s,W0)
@@ -649,8 +688,7 @@
     lax.fori_loop(0,3,third,0)
     at("out",0,1)
     unpack24(G,OUT_AT,W0)
-    ldc.wait()
-    r1=F1; mixed=F2; dh2=F3; h2=B1; h2T=hT
+    r1=F1; mixed=F2; dh2=F3; h2=B1
     def out_block(i,_):
         at("ob",i,4)
         sl=rows(i)
@@ -660,9 +698,6 @@
         hb=(norm_parts(r)[0]*V1[:,2*D:3*D]+V1[:,3*D:4*D]).astype(BF)
         h2[sl,:]=hb
         h2T[:,sl]=hb.T
-        pos_=i*RB+lax.broadcasted_iota(jnp.int32,(RB,D),0)
-        cot[sl,:]=jnp.where(pos_<length,cot[sl,:],jnp.zeros((),BF))
-        dh2[sl,:]=jnp.zeros((RB,D),F32)
         return 0
     lax.fori_loop(0,NBK,out_block,0)
     du_s=B2
@@ -734,16 +769,9 @@
     lax.fori_loop(0,D//RB,orow,0)
     pack24(G,OUT_AT,dW)
     at("bp",0,1)
-    h1T=hT; dqkv=B3; dh1=F2
+    dqkv=B3; dh1=F2
     outs[0].wait()
-    def again(i,_):
-        at("ag",i,4)
-        sl=rows(i)
-        hb=(norm_parts(tok[sl,:].astype(F32))[0]*V1[:,0:D]+V1[:,D:2*D]).astype(BF)
-        h1T[:,sl]=hb.T
-        dh1[sl,:]=jnp.zeros((RB,D),F32)
-        return 0
-    lax.fori_loop(0,NBK,again,0)
+    dh1[...]=jnp.zeros_like(dh1)
     def third_back(s,_):
         unpack24(G,QKV_AT+CW*s,W0)
         def pair(pp,_):
@@ -770,17 +798,23 @@
         lax.fori_loop(0,NBK,drow,0)
         return 0
     lax.fori_loop(0,3,third_back,0)
-    def lrow(i,acc):
+    def srow(i,acc):
         at("ln",i,4)
         sl=rows(i)
         dh=dh1[sl,:]
-        xh,r=norm_parts(tok[sl,:].astype(F32))
-        F1[sl,:]=dr1[sl,:]+norm_back(dh*V1[:,0:D],xh,r)
+        xh,_=norm_parts(tok[sl,:].astype(F32))
         return tuple(a+jnp.sum(b,0,keepdims=True) for a,b in zip(acc,(dh*xh,dh)))
-    sums=lax.fori_loop(0,NBK,lrow,(z1,z1))
+    sums=lax.fori_loop(0,NBK,srow,(z1,z1))
     for j,v in enumerate(sums): dV1[:,pl.ds(j*D,D)]=v
     pack_vec(G,V,dV1)
     at("lp",0,1)
+    def lrow(i,_):
+        at("lx",i,4)
+        sl=rows(i)
+        xh,r=norm_parts(tok[sl,:].astype(F32))
+        F1[sl,:]=dr1[sl,:]+norm_back(dh1[sl,:]*V1[:,0:D],xh,r)
+        return 0
+    lax.fori_loop(0,NBK,lrow,0)
     outs=[dma(F1,dtok_o,3)]
     for f in clock.tail: f()
     flat=lax.broadcasted_iota(jnp.int32,(16,VEC_COLS),0)*VEC_COLS+lax.broadcasted_iota(jnp.int32,(16,VEC_COLS),1)
@@ -804,7 +838,7 @@
     outs=[S((L,D),BF),S((L,D),F32),S((16,COLS),F32),S((24,128),F32)]
     f=lambda: V((L,D),F32)
     b=lambda: V((L,D),BF)
-    scratch=[V((4,Z,2,16,COLS),BF),b(),b(),f(),f(),f(),V((3,L,D),BF),b(),b(),b(),V((D,L),BF),V((D,L),BF),V((D,L),F32),
+    scratch=[V((4,Z,2,16,COLS),BF),b(),b(),f(),f(),f(),V((3,L,D),BF),b(),b(),b(),V((D,L),BF),V((D,L),BF),V((D,L),BF),V((D,L),F32),
              V((D,W3),BF),V((W3,D),BF),V((D,W3),F32),V((6,2,L),F32),V((80,128),F32),V((1,10*D),F32),V((1,10*D),F32),
              V((L,128),F32),V((L,128),F32),V((16,COLS),F32),V((24,128),F32),pltpu.SemaphoreType.DMA((6,))]
     return pl.pallas_call(functools.partial(mega_kernel,Z,plan),out_shape=outs,

time: 211 us -> 200 us (0.948)
  Pallas kernels: 206 us -> 195 us
    pallas_call x1, Pallas kernels: 199 us -> 188 us  [mega_call(): pl.pallas_call(functools.partial(mega_kernel, Z, plan), out_shape=outs, i...]
where the time goes in v3:
time: 200 us
  Pallas kernels  195 us (98%)
  between operations  3.3 us (2%)
    pallas_call x1, Pallas kernels, mega_call(): pl.pallas_call(functools.partial(mega_kernel, Z, plan), out_shape=outs, i...  188 us
    pallas_call x1, Pallas kernels, adam_call(): pl.pallas_call(adam_kernel, out_shape=[jax.ShapeDtypeStruct(a.shape, a.dt...  6.65 us

profile of v3, /device:TPU:0, one launch (start us, length us, event | category | flops | bytes accessed | tf_op | source)
XLA Modules:
  0.0 200.1 jit_solution(8734467004063028245)
XLA Ops:
  0.7 0.7 convert_element_type.3
  1.4 0.2 dynamic_update_slice.3
  1.5 0.0 copy-start.1
  2.2 0.0 copy-done.1
  2.2 188.0 %shard_map.313 = (bf16[1024,768]{1,0:T(8,128)(2,1)}, f32[1024,768]{1,0:T(8,128)}, f32[16,13952]{1,0:T(8,128)}, f32[24,128]{1,0:T(8,128)}) custom-call(bf16[1024,768]{1,0:T(8,128)(2,1)} %bitcast.11, bf16[1024,768]{1,0:T(8,128)(2,1)} %bitcast.12, s32[1]{0:T(128)S(6)} %copy.37.len_ref, f32[24,2304]{1,0:T(8,128)} %refs_0_.1, f32[24,768]{1,0:T(8,128)} %refs_3_.1, ...), custom_call_target="tpu_custom_call" | custom-call | flops 60000002048 | bytes 62914560 | tf_op jit(solution)/shard_map/pallas_call | solution.py:844
  190.3 0.0 copy-start
  190.3 0.0 copy-start.2
  190.3 0.0 copy-start.3
  190.3 0.0 copy-start.4
  190.3 6.6 %shard_map.314 = (f32[24,2304]{1,0:T(8,128)}, f32[24,2304]{1,0:T(8,128)}, f32[24,2304]{1,0:T(8,128)}, f32[24,768]{1,0:T(8,128)}, f32[24,768]{1,0:T(8,128)}, /*in...) custom-call(s32[1]{0:T(128)} %bitcast.par_ref, ...), custom_call_target="tpu_custom_call" | custom-call | flops 10000000 | bytes 8388608 | tf_op jit(solution)/shard_map/pallas_call | solution.py:926
  197.0 0.0 copy-done
  197.0 0.5 slice.6
  198.2 0.0 copy-done.2
  198.3 0.0 copy-done.3
  198.3 0.0 copy-done.4
  198.3 0.7 multiply_subtract_fusion
  (2 shorter events, 0.0 us)
Async XLA Ops:
  1.5 0.7 copy-start.1
  190.3 6.7 %copy-start = (f32[24,128]{1,0:T(8,128)S(1)}, f32[24,128]{1,0:T(8,128)}, u32[]{:S(2)}) copy-start(f32[24,128]{1,0:T(8,128)} %get-tuple-element.37.nrm_h) | copy-start | bytes 36868
  190.3 8.0 %copy-start.2 = (f32[240]{0:T(256)S(1)}, f32[240]{0:T(256)}, u32[]{:S(2)}) copy-start(f32[240]{0:T(256)} %param.33) | copy-start | bytes 2884
  190.3 8.0 %copy-start.3 = (f32[240]{0:T(256)S(1)}, f32[240]{0:T(256)}, u32[]{:S(2)}) copy-start(f32[240]{0:T(256)} %param.34) | copy-start | bytes 2884
  190.3 8.0 %copy-start.4 = (f32[240]{0:T(256)S(1)}, f32[240]{0:T(256)}, u32[]{:S(2)}) copy-start(f32[240]{0:T(256)} %param.35) | copy-start | bytes 2884

commit v4 on v3

--- a/solution.py
+++ b/solution.py
@@ -439,14 +439,23 @@
     parts=[jnp.concatenate([rest[:,256*s:256*s+128],rest[:,256*s+128:256*s+256]],0) for s in range(3)]
     G[(*me,slice(None),pl.ds(al(at+W3,128),W3//2))]=jnp.concatenate(parts,1).astype(BF)
 
-def pack_own(place, G, wqkv, wout, wup, wdown, vec, first):
+def pack_own_vec(G, me, vec, wide, start):
+    wide[...]=jnp.zeros_like(wide)
+    wide[0:1,0:vec.shape[1]]=vec[...]
+    n=3*VEC_COLS
+    i=lax.broadcasted_iota(jnp.int32,(n,n),0); j=lax.broadcasted_iota(jnp.int32,(n,n),1)
+    row=nn(wide[...].astype(BF),jnp.where(j==i+start,1.0,0.0).astype(BF))[0:1]
+    parts=[row[:,VEC_COLS*k:VEC_COLS*k+VEC_COLS] for k in range(3)]+[jnp.zeros((13,VEC_COLS),F32)]
+    G[(*me,slice(None),pl.ds(VEC_AT,VEC_COLS))]=jnp.concatenate(parts,0).astype(BF)
+
+def pack_own(place, G, wqkv, wout, wup, wdown, vec, wide, start, first):
     me=place.me
     lo=al(8*place.x,8); ro=al(16*(1-place.x),8)
     def cols(w,cs):
         return [jnp.concatenate([w[pl.ds(a,n),pl.ds(c,k)] for c,k in cs],1) for a,n in ((lo,16),(ro,8))]
     for s in ((2,) if first else (0,1)): pack_rows(G,me,QKV_AT+CW*s,*cols(wqkv,third_cols(s)))
     if first:
-        G[(*me,slice(None),pl.ds(VEC_AT,VEC_COLS))]=vec[...]
+        pack_own_vec(G,me,vec,wide,start)
         return
     pack_rows(G,me,OUT_AT,*cols(wout,[(0,W3)]))
     for c in range(4): pack_rows(G,me,UP_AT+CW*c,*cols(wup,[(W3*c,W3)]))
@@ -534,7 +543,7 @@
     for i in range(3):
         p.append(("third",i,0.6 if i else 2.0))
         p+=[("qkv",4*i+k,0.42) for k in range(4)]
-        p+=[("af",2*i+pp,2.3) for pp in range(2)]
+        p+=[("af",2*i+pp,2.1) for pp in range(2)]
     p.append(("out",0,0.6))
     p+=[("ob",k,1.1) for k in range(4)]
     for c in range(4):
@@ -552,9 +561,9 @@
         p+=[("dq",3*i+k,0.6+0.2*(k==2)) for k in range(3)]
         p.append(("dp",i,0.1))
         p+=[("dh",4*i+k,0.5) for k in range(4)]
-    p+=[("ln",k,0.5+0.4*(k==3)) for k in range(4)]
+    p+=[("ln",k,0.35+0.4*(k==3)) for k in range(4)]
     p.append(("lp",0,0.1))
-    p+=[("lx",k,0.65) for k in range(4)]
+    p+=[("lx",k,0.45) for k in range(4)]
     return p
 
 def ready_places():
@@ -590,23 +599,23 @@
 
 PLAN = (
     (0, 0, 0, 0), (1, 0, 1, 0), (1, 0, 2, 0), (1, 0, 0, 1), (1, 0, 0, 2), (1, 0, 0, 3), (1, 0, 1, 1), (1, 0, 1, 2),
-    (1, 0, 0, 4), (1, 0, 0, 5), (1, 0, 1, 3), (2, 0, 1, 4), (3, 0, 0, 6), (3, 0, 0, 7), (3, 0, 2, 1), (3, 0, 3, 0),
+    (1, 0, 0, 4), (1, 0, 0, 5), (1, 0, 1, 3), (1, 0, 1, 4), (2, 0, 0, 6), (2, 0, 0, 7), (3, 0, 2, 1), (3, 0, 3, 0),
     (3, 0, 1, 5), (3, 0, 1, 6), (4, 0, 2, 2), (5, 0, 1, 7), (6, 0, 0, 8), (6, 0, 0, 9), (8, 0, 1, 8), (8, 0, 1, 9),
     (8, 0, 1, 10), (9, 0, 2, 3), (12, 0, 2, 4), (12, 0, 1, 11), (13, 0, 1, 12), (14, 0, 3, 1), (15, 0, 2, 5),
     (15, 0, 2, 6), (16, 0, 3, 2), (17, 0, 2, 7), (19, 0, 5, 0), (20, 0, 3, 3), (20, 0, 2, 8), (21, 0, 3, 4),
     (22, 0, 4, 0), (22, 0, 2, 9), (24, 0, 2, 10), (25, 0, 3, 5), (25, 0, 3, 6), (26, 0, 5, 1), (26, 0, 3, 7),
-    (26, 0, 3, 8), (26, 0, 2, 11), (26, 0, 4, 1), (27, 0, 4, 2), (27, 0, 4, 3), (27, 0, 3, 9), (27, 0, 3, 10),
-    (27, 0, 2, 12), (28, 0, 5, 2), (29, 0, 4, 4), (29, 0, 4, 5), (30, 0, 3, 11), (31, 0, 5, 3), (31, 0, 4, 6),
-    (31, 0, 5, 4), (31, 0, 5, 5), (32, 0, 3, 12), (32, 0, 4, 7), (35, 0, 5, 6), (35, 0, 5, 7), (35, 0, 4, 8),
+    (26, 0, 3, 8), (26, 0, 2, 11), (26, 0, 4, 1), (27, 0, 4, 2), (27, 0, 4, 3), (27, 0, 3, 9), (27, 0, 2, 12),
+    (27, 0, 3, 10), (28, 0, 5, 2), (29, 0, 4, 4), (29, 0, 4, 5), (30, 0, 3, 11), (31, 0, 5, 3), (31, 0, 5, 4),
+    (31, 0, 5, 5), (31, 0, 4, 6), (32, 0, 3, 12), (32, 0, 4, 7), (35, 0, 5, 6), (35, 0, 5, 7), (35, 0, 4, 8),
     (35, 0, 4, 9), (35, 0, 4, 10), (37, 0, 5, 8), (37, 0, 5, 9), (37, 0, 4, 11), (40, 0, 4, 12), (43, 1, 0, 0),
-    (45, 0, 5, 10), (47, 1, 0, 1), (51, 0, 5, 11), (54, 1, 0, 2), (55, 1, 1, 0), (56, 0, 5, 12), (58, 1, 1, 1),
-    (59, 1, 0, 3), (67, 1, 2, 0), (68, 1, 1, 2), (70, 1, 0, 4), (70, 1, 2, 1), (75, 1, 2, 2), (79, 1, 3, 0),
+    (45, 0, 5, 10), (47, 1, 0, 1), (51, 0, 5, 11), (54, 1, 0, 2), (56, 0, 5, 12), (57, 1, 1, 0), (59, 1, 0, 3),
+    (59, 1, 1, 1), (67, 1, 2, 0), (69, 1, 1, 2), (70, 1, 0, 4), (70, 1, 2, 1), (75, 1, 2, 2), (79, 1, 3, 0),
     (80, 1, 1, 3), (81, 1, 3, 1), (81, 1, 4, 0), (82, 1, 2, 3), (83, 1, 4, 1), (86, 1, 3, 2), (88, 1, 5, 0),
     (89, 1, 2, 4), (89, 1, 4, 2), (90, 1, 1, 4), (90, 1, 3, 3), (90, 1, 5, 1), (90, 1, 6, 0), (91, 1, 4, 3),
-    (91, 1, 6, 1), (92, 1, 7, 0), (95, 1, 5, 2), (96, 1, 6, 2), (97, 1, 3, 4), (102, 1, 5, 3), (102, 1, 7, 1),
-    (102, 1, 8, 0), (103, 1, 4, 4), (103, 1, 6, 3), (103, 1, 8, 1), (105, 1, 7, 2), (105, 1, 5, 4), (108, 1, 8, 2),
-    (109, 1, 6, 4), (109, 1, 9, 0), (113, 1, 7, 3), (113, 1, 9, 1), (114, 1, 10, 0), (114, 1, 8, 3),
-    (115, 1, 10, 1), (117, 1, 9, 2), (120, 1, 10, 2), (120, 1, 11, 0), (121, 1, 8, 4), (123, 1, 7, 4),
+    (91, 1, 6, 1), (92, 1, 7, 0), (95, 1, 5, 2), (97, 1, 3, 4), (98, 1, 6, 2), (102, 1, 5, 3), (102, 1, 7, 1),
+    (102, 1, 8, 0), (103, 1, 4, 4), (103, 1, 6, 3), (103, 1, 8, 1), (105, 1, 5, 4), (105, 1, 7, 2), (108, 1, 8, 2),
+    (109, 1, 6, 4), (109, 1, 9, 0), (113, 1, 7, 3), (113, 1, 9, 1), (114, 1, 8, 3), (114, 1, 10, 0),
+    (115, 1, 10, 1), (117, 1, 9, 2), (120, 1, 11, 0), (120, 1, 10, 2), (121, 1, 8, 4), (124, 1, 7, 4),
     (124, 1, 9, 3), (124, 1, 11, 1), (124, 1, 12, 0), (127, 1, 10, 3), (127, 1, 12, 1), (129, 1, 11, 2),
     (130, 1, 13, 0), (131, 1, 12, 2), (133, 1, 9, 4), (134, 1, 11, 3), (134, 1, 13, 1), (134, 1, 13, 2),
     (134, 1, 11, 4), (134, 1, 10, 4), (134, 1, 12, 3), (134, 1, 13, 3), (134, 1, 13, 4), (134, 1, 12, 4),
@@ -626,8 +635,8 @@
             if g>=n: assert pos[(1,g-n,i)]<pos[(1,g,j)]
 
 def mega_kernel(Z,plan,tok_h,cot_h,len_ref,wqkv_s,wout_s,wup_s,wdown_s,vec_s,
-               mixed_o,dtok_o,own_o,nrm_o,
-               G,tok,cot,F1,F2,F3,qkv,B1,B2,B3,h1T,h2T,aT,oT,W0,W1,dW,lse,V,V1,dV1,dka,dva,own,nrm,dsem,*rest):
+               mixed_o,dtok_o,own_o,nrm_o,place_o,
+               G,tok,cot,F1,F2,F3,qkv,B1,B2,B3,h1T,h2T,aT,oT,W0,W1,dW,lse,V,V1,dV1,dka,dva,own,nrm,wide,dsem,*rest):
     gsems=rest[:10]; rbufs=rest[10:10+NB]; rsems=rest[10+NB:18+NB]; nb,got,ns,nr=rest[18+NB:]
     L=tok.shape[0]
     NBK=L//RB
@@ -636,7 +645,10 @@
         cp=pltpu.make_async_copy(a,b,dsem.at[i]); cp.start(); return cp
     ldt=dma(tok_h,tok,0); ldc=dma(cot_h,cot,1)
     bar=announce(place,Z)
-    shards=(wqkv_s,wout_s,wup_s,wdown_s,vec_s)
+    start=lax.rem(240*((place.dp*Z+place.z)*2+place.x),128)
+    place_o[0]=place.x
+    place_o[1]=start
+    shards=(wqkv_s,wout_s,wup_s,wdown_s,vec_s,wide,start)
     pack_own(place,G,*shards,True)
     pl.semaphore_wait(bar,8*Z-1)
     ga=Gather(place,G,GATHER,gsems)
@@ -818,7 +830,6 @@
     outs=[dma(F1,dtok_o,3)]
     for f in clock.tail: f()
     flat=lax.broadcasted_iota(jnp.int32,(16,VEC_COLS),0)*VEC_COLS+lax.broadcasted_iota(jnp.int32,(16,VEC_COLS),1)
-    start=lax.rem(240*((place.dp*Z+place.z)*2+place.x),128)
     vec=own[:,pl.ds(VEC_AT,VEC_COLS)]
     vec=jnp.where(jnp.logical_and(flat>=start,flat<start+240),vec,0.0)
     left=own[:,pl.ds(0,VEC_AT)]; right=own[:,pl.ds(OUT_AT,COLS-OUT_AT)]
@@ -835,14 +846,14 @@
     L=tok.shape[0]; pieces=8*Z
     S=jax.ShapeDtypeStruct; V=pltpu.VMEM
     vm=pl.BlockSpec(memory_space=pltpu.VMEM); an=pl.BlockSpec(memory_space=pltpu.HBM); sm=pl.BlockSpec(memory_space=pltpu.SMEM)
-    outs=[S((L,D),BF),S((L,D),F32),S((16,COLS),F32),S((24,128),F32)]
+    outs=[S((L,D),BF),S((L,D),F32),S((16,COLS),F32),S((24,128),F32),S((2,),jnp.int32)]
     f=lambda: V((L,D),F32)
     b=lambda: V((L,D),BF)
     scratch=[V((4,Z,2,16,COLS),BF),b(),b(),f(),f(),f(),V((3,L,D),BF),b(),b(),b(),V((D,L),BF),V((D,L),BF),V((D,L),BF),V((D,L),F32),
              V((D,W3),BF),V((W3,D),BF),V((D,W3),F32),V((6,2,L),F32),V((80,128),F32),V((1,10*D),F32),V((1,10*D),F32),
-             V((L,128),F32),V((L,128),F32),V((16,COLS),F32),V((24,128),F32),pltpu.SemaphoreType.DMA((6,))]
+             V((L,128),F32),V((L,128),F32),V((16,COLS),F32),V((24,128),F32),V((8,3*VEC_COLS),F32),pltpu.SemaphoreType.DMA((6,))]
     return pl.pallas_call(functools.partial(mega_kernel,Z,plan),out_shape=outs,
-        in_specs=[an,an,sm]+[vm]*5,out_specs=[an]*len(outs),
+        in_specs=[an,an,sm]+[vm]*5,out_specs=[an]*4+[sm],
         scratch_shapes=scratch+gather_sems(len(GATHER),Z)+rs_bufs(Z)+rs_sems(len(SCATTER),Z)+norm_bufs(Z)+norm_sems(Z),
         compiler_params=pltpu.CompilerParams(collective_id=1,has_side_effects=True,vmem_limit_bytes=63*2**20),
         cost_estimate=pl.CostEstimate(flops=60*10**9,bytes_accessed=60*2**20,transcendentals=10**7))(tok,cot,length,wqkv,wout,wup,wdown,vec)
@@ -860,28 +871,32 @@
 
 
 def adam_kernel(par_ref, own_h, nrm_h, mixed_h, dtok_h, *refs):
-    ins_h, outs_h = refs[:12], refs[12:24]
-    own, nrm, *rest = refs[26:]
-    ins, outs, mixed, dtok, sem = rest[:12], rest[12:24], rest[24], rest[25], rest[26]
+    ins_h, outs_h, moved, norm_ref = refs[:15], refs[15:30], refs[30:32], refs[32]
+    own, nrm, *rest = refs[33:]
+    ins, outs, (mixed, dtok, wide, sem) = rest[:15], rest[15:30], rest[30:]
     pairs = list(zip((own_h, nrm_h) + tuple(ins_h), (own, nrm) + tuple(ins)))
     loads = [pltpu.make_async_copy(a, b, sem.at[i]) for i, (a, b) in enumerate(pairs)]
     moves = [
-        pltpu.make_async_copy(mixed_h, mixed, sem.at[14]),
-        pltpu.make_async_copy(dtok_h, dtok, sem.at[15]),
+        pltpu.make_async_copy(mixed_h, mixed, sem.at[32]),
+        pltpu.make_async_copy(dtok_h, dtok, sem.at[33]),
     ]
     for cp in loads + moves:
         cp.start()
-    for cp in loads:
-        cp.wait()
-    for cp in moves:
-        cp.wait()
-    moves = [
-        pltpu.make_async_copy(mixed, refs[24], sem.at[14]),
-        pltpu.make_async_copy(dtok, refs[25], sem.at[15]),
-    ]
-    for cp in moves:
-        cp.start()
-    factor = jnp.minimum(1.0, CLIP_NORM / (jnp.sqrt(nrm[0:1, 0:1]) + 1e-06))
+    loads[0].wait()
+    loads[1].wait()
+    stores = [pltpu.make_async_copy(a, b, sem.at[i]) for i, (a, b) in enumerate(zip(outs, outs_h), 17)]
+
+    def take(i):
+        for cp in loads[2 + 3 * i : 5 + 3 * i]:
+            cp.wait()
+
+    def give(i):
+        for cp in stores[3 * i : 3 * i + 3]:
+            cp.start()
+
+    norm = jnp.sqrt(nrm[0:1, 0:1])
+    norm_ref[0] = norm[0, 0]
+    factor = jnp.minimum(1.0, CLIP_NORM / (norm + 1e-06))
     main_at = al(8 * par_ref[0], 8)
     rest_at = al(16 * (1 - par_ref[0]), 8)
 
@@ -904,18 +919,41 @@
             step(i, pl.ds(rest_at, 8), pl.ds(c, n), rest[:, done : done + n], rate)
             done += n
 
+    take(0)
     for s in range(3):
         chunk(0, QKV_AT + CW * s, third_cols(s), D ** (-0.5))
+    for cp in moves:
+        cp.wait()
+    out_moves = [
+        pltpu.make_async_copy(mixed, moved[0], sem.at[32]),
+        pltpu.make_async_copy(dtok, moved[1], sem.at[33]),
+    ]
+    for cp in out_moves:
+        cp.start()
+    give(0)
+    take(1)
     chunk(1, OUT_AT, [(0, W3)], D ** (-0.5))
+    give(1)
+    take(2)
     for c in range(4):
         chunk(2, UP_AT + CW * c, [(W3 * c, W3)], D ** (-0.5))
+    give(2)
+    take(3)
     for r in range(6):
         grad = own[:, pl.ds(DOWN_AT + r * D, D)]
         step(3, pl.ds(16 * r, 16), slice(None), grad, FF ** (-0.5))
-    stores = [pltpu.make_async_copy(a, b, sem.at[i]) for i, (a, b) in enumerate(zip(outs, outs_h))]
-    for cp in stores:
-        cp.start()
-    for cp in stores + moves:
+    give(3)
+    take(4)
+    n = ins[12].shape[1]
+    for k in range(3):
+        wide[0:8, VEC_COLS * k : VEC_COLS * k + VEC_COLS] = jnp.broadcast_to(
+            nrm[8 + k : 9 + k, :], (8, VEC_COLS)
+        )
+    width = 3 * VEC_COLS
+    turned = pltpu.roll(wide[...], lax.rem(width - par_ref[1], width), 1)
+    step(4, slice(None), slice(None), turned[0:1, :n], VECTOR_RATE)
+    give(4)
+    for cp in stores + out_moves:
         cp.wait()
 
 
@@ -925,12 +963,14 @@
     held = [pltpu.VMEM(a.shape, F32) for a in (own, nrm) + tuple(states) + tuple(states)]
     return pl.pallas_call(
         adam_kernel,
-        out_shape=[jax.ShapeDtypeStruct(a.shape, a.dtype) for a in states + (mixed, d_tokens)],
-        in_specs=[sm] + [hb] * 16,
-        out_specs=[hb] * 14,
+        out_shape=[jax.ShapeDtypeStruct(a.shape, a.dtype) for a in states + (mixed, d_tokens)]
+        + [jax.ShapeDtypeStruct((1,), F32)],
+        in_specs=[sm] + [hb] * 19,
+        out_specs=[hb] * 17 + [sm],
         scratch_shapes=held
         + [pltpu.VMEM(mixed.shape, BF), pltpu.VMEM(d_tokens.shape, F32)]
-        + [pltpu.SemaphoreType.DMA((16,))],
+        + [pltpu.VMEM((8, 3 * VEC_COLS), F32)]
+        + [pltpu.SemaphoreType.DMA((34,))],
         compiler_params=pltpu.CompilerParams(vmem_limit_bytes=63 * 2**20),
         cost_estimate=pl.CostEstimate(
             flops=10**7, bytes_accessed=8 * 2**20, transcendentals=10**6
@@ -1024,24 +1064,16 @@
 
 
 def direct_shards(Z, tokens, lengths, cotangent, *state):
-    packed, m_packed, v_packed = state[12:]
-    dp = lax.axis_index("dp")
-    fsdp = lax.axis_index("fsdp")
-    n = packed.shape[0]
-    start = ((dp * 2 * Z + fsdp) * n) % VEC_COLS
-    vec = lax.dynamic_update_slice(
-        jnp.zeros((16 * VEC_COLS,), BF), packed.astype(BF), (start,)
-    ).reshape(16, VEC_COLS)
-    mixed, d_tokens, own, small = mega_call(
-        Z, tokens[0], cotangent[0], lengths, state[0], state[3], state[6], state[9], vec
+    n = state[12].shape[0]
+    vecs = tuple(v.reshape(1, n) for v in state[12:])
+    mixed, d_tokens, own, small, place = mega_call(
+        Z, tokens[0], cotangent[0], lengths, state[0], state[3], state[6], state[9], vecs[0]
     )
-    grad_norm = jnp.sqrt(small[0, 0])
-    factor = jnp.minimum(1.0, CLIP_NORM / (grad_norm + 1e-06))
-    parity = (fsdp % 2).astype(jnp.int32).reshape(1)
-    *new, mixed, d_tokens = adam_call(parity, own, small, mixed, d_tokens, state[:12])
-    g_vec = lax.dynamic_slice(small[8:].reshape(-1), (start,), (n,))
-    new_vec = adam_step(packed, m_packed, v_packed, g_vec * factor, VECTOR_RATE)
-    return (mixed[None], d_tokens[None], grad_norm) + tuple(new) + new_vec
+    *new, mixed, d_tokens, grad_norm = adam_call(
+        place, own, small, mixed, d_tokens, state[:12] + vecs
+    )
+    new[12:] = [v.reshape(n) for v in new[12:]]
+    return (mixed[None], d_tokens[None], grad_norm[0]) + tuple(new)
 
 
 def solution(mesh):

time: 200 us -> 198 us (0.990)
  Pallas kernels: 195 us -> 197 us
where the time goes in v4:
time: 198 us
  Pallas kernels  197 us (99%)
    pallas_call x1, Pallas kernels, mega_call(): pl.pallas_call(functools.partial(mega_kernel, Z, plan), out_shape=outs, i...  189 us
    pallas_call x1, Pallas kernels, adam_call(): pl.pallas_call(adam_kernel, out_shape=[jax.ShapeDtypeStruct(a.shape, a.dt...  8.04 us

profile of v4, /device:TPU:0, one launch (start us, length us, event | category | flops | bytes accessed | tf_op | source)
XLA Modules:
  0.0 198.2 jit_solution(8555713897319886428)
XLA Ops:
  1.3 188.7 %shard_map.313 = (bf16[1024,768]{1,0:T(8,128)(2,1)}, f32[1024,768]{1,0:T(8,128)}, f32[16,13952]{1,0:T(8,128)}, f32[24,128]{1,0:T(8,128)}, s32[2]{0:T(128)}) custom-call(bf16[1024,768]{1,0:T(8,128)(2,1)} %bitcast.16, bf16[1024,768]{1,0:T(8,128)(2,1)} %bitcast.17, s32[1]{0:T(128)S(6)} %copy.36.len_ref, f32[24,2304]{1,0:T(8,128)} %refs_0_.1, ...), custom_call_target="tpu_custom_call" | custom-call | flops 60000002048 | bytes 62914560 | tf_op jit(solution)/shard_map/pallas_call | solution.py:855
  190.0 8.0 %shard_map.314 = (f32[24,2304]{1,0:T(8,128)}, f32[24,2304]{1,0:T(8,128)}, f32[24,2304]{1,0:T(8,128)}, f32[24,768]{1,0:T(8,128)}, f32[24,768]{1,0:T(8,128)}, /*in...) custom-call(s32[2]{0:T(128)} %get-tuple-element.41.par_ref, ...), custom_call_target="tpu_custom_call" | custom-call | flops 10000000 | bytes 8388608 | tf_op jit(solution)/shard_map/pallas_call | solution.py:964

commit v5 on v4

--- a/solution.py
+++ b/solution.py
@@ -880,8 +880,15 @@
         pltpu.make_async_copy(mixed_h, mixed, sem.at[32]),
         pltpu.make_async_copy(dtok_h, dtok, sem.at[33]),
     ]
-    for cp in loads + moves:
+    for cp in moves + loads:
         cp.start()
+    out_moves = [
+        pltpu.make_async_copy(mixed, moved[0], sem.at[32]),
+        pltpu.make_async_copy(dtok, moved[1], sem.at[33]),
+    ]
+    for cp, out in zip(moves, out_moves):
+        cp.wait()
+        out.start()
     loads[0].wait()
     loads[1].wait()
     stores = [pltpu.make_async_copy(a, b, sem.at[i]) for i, (a, b) in enumerate(zip(outs, outs_h), 17)]
@@ -922,14 +929,6 @@
     take(0)
     for s in range(3):
         chunk(0, QKV_AT + CW * s, third_cols(s), D ** (-0.5))
-    for cp in moves:
-        cp.wait()
-    out_moves = [
-        pltpu.make_async_copy(mixed, moved[0], sem.at[32]),
-        pltpu.make_async_copy(dtok, moved[1], sem.at[33]),
-    ]
-    for cp in out_moves:
-        cp.start()
     give(0)
     take(1)
     chunk(1, OUT_AT, [(0, W3)], D ** (-0.5))

time: 198 us -> 198 us (level)
  no operation moved by 1% of the time
where the time goes in v5:
time: 198 us
  Pallas kernels  197 us (99%)
    pallas_call x1, Pallas kernels, mega_call(): pl.pallas_call(functools.partial(mega_kernel, Z, plan), out_shape=outs, i...  189 us
    pallas_call x1, Pallas kernels, adam_call(): pl.pallas_call(adam_kernel, out_shape=[jax.ShapeDtypeStruct(a.shape, a.dt...  8.07 us

profile of v5, /device:TPU:0, one launch (start us, length us, event | category | flops | bytes accessed | tf_op | source)
XLA Modules:
  0.0 198.3 jit_solution(12433163784993820443)
XLA Ops:
  1.3 188.7 %shard_map.313 = (bf16[1024,768]{1,0:T(8,128)(2,1)}, f32[1024,768]{1,0:T(8,128)}, f32[16,13952]{1,0:T(8,128)}, f32[24,128]{1,0:T(8,128)}, s32[2]{0:T(128)}) custom-call(bf16[1024,768]{1,0:T(8,128)(2,1)} %bitcast.16, bf16[1024,768]{1,0:T(8,128)(2,1)} %bitcast.17, s32[1]{0:T(128)S(6)} %copy.36.len_ref, f32[24,2304]{1,0:T(8,128)} %refs_0_.1, ...), custom_call_target="tpu_custom_call" | custom-call | flops 60000002048 | bytes 62914560 | tf_op jit(solution)/shard_map/pallas_call | solution.py:855
  190.0 8.1 %shard_map.314 = (f32[24,2304]{1,0:T(8,128)}, f32[24,2304]{1,0:T(8,128)}, f32[24,2304]{1,0:T(8,128)}, f32[24,768]{1,0:T(8,128)}, f32[24,768]{1,0:T(8,128)}, /*in...) custom-call(s32[2]{0:T(128)} %get-tuple-element.41.par_ref, ...), custom_call_target="tpu_custom_call" | custom-call | flops 10000000 | bytes 8388608 | tf_op jit(solution)/shard_map/pallas_call | solution.py:963
